TPU v7x, 256 devices: a whole 4x4x8 slice. The times are simulated.
256 devices in a mesh: segment: 2 (over x_lo), ha: 8 (over y, core), wa: 16 (over z, x_hi).
Axes of the slice: x: 4 (x_hi: 2, x_lo: 2; x = x_hi * 2 + x_lo), y: 4, z: 8, core: 2. Of those that a mesh axis runs over, the one named last changes fastest.
Arguments:
- latent: bfloat16 [4, 32, 320, 384], P(None, 'ha', 'wa'), may hold values from -6 to 6
- w_mid: bfloat16 [2, 3, 3, 3, 384, 384], P('segment'), may hold values from -0.0625 to 0.0625
- b_mid: float32 [2, 384], P('segment'), may hold values from -1 to 1
- g_mid: float32 [2, 384], P('segment'), may hold values from 0.25 to 1.75
- cache_mid: bfloat16 [2, 2, 32, 320, 384], P('segment', None, 'ha', 'wa'), may hold values from -4 to 4
- w_up: bfloat16 [3, 3, 384, 192], replicated, may hold values from -0.109375 to 0.109375
- b_up: float32 [192], replicated, may hold values from -1 to 1
- g_fine: float32 [192], replicated, may hold values from 0.25 to 1.75
- cache_fine: bfloat16 [2, 64, 640, 192], P(None, 'ha', 'wa'), may hold values from -4 to 4
- w_fine: bfloat16 [3, 3, 3, 192, 192], replicated, may hold values from -0.078125 to 0.078125
- b_fine: float32 [192], replicated, may hold values from -1 to 1
Outputs:
- decoded: bfloat16 [4, 64, 640, 192], P('segment', 'ha', 'wa')
All inputs are finite; a program needn't handle non-finite values.
Results may differ from a plain program's by a relative error of at most 0.019.
Values may be sent and summed in bfloat16 or wider, within the bound.
No kernel may reach another device: no remote copies, remote signals or barrier semaphores. Data moves between devices by JAX's collectives and lax.ppermute only.
A program may use at most 128 MiB of HBM per device.

v0:
```python
import jax
import jax.numpy as jnp
from jax import lax
from jax.sharding import PartitionSpec as P

GROUPS = 2


def with_halo(shard, sides, width):
    for axis, dim in sides:
        size, length = (lax.axis_size(axis), shard.shape[dim])
        up = [(i, (i + 1) % size) for i in range(size - 1)]
        down = [(j, i) for i, j in up]
        last = lax.slice_in_dim(shard, length - width, length, axis=dim)
        first = lax.slice_in_dim(shard, 0, width, axis=dim)
        before = lax.ppermute(last, axis, up)
        after = lax.ppermute(first, axis, down)
        shard = jnp.concatenate([before, shard, after], axis=dim)
    return shard


def passed_along(shard, axis, by):
    length = lax.axis_size(axis)
    pairs = [(i, i + by) for i in range(length) if 0 <= i + by < length]
    return lax.ppermute(shard, axis, pairs)


def normed(values, gain_vec):
    as_float = values.astype(jnp.float32)
    inv_rms = lax.rsqrt(jnp.mean(as_float * as_float, axis=-1, keepdims=True) + 1e-06)
    return jax.nn.silu(as_float * inv_rms * gain_vec).astype(jnp.bfloat16)


def conv_valid(extended, kernel):
    return lax.conv_general_dilated(
        extended[None],
        kernel,
        (1, 1, 1),
        "VALID",
        dimension_numbers=("NDHWC", "DHWIO", "NDHWC"),
        preferred_element_type=jnp.float32,
    )[0]


def shards(latent, w_mid, b_mid, g_mid, cache_mid, w_up, b_up, g_fine, cache_fine, w_fine, b_fine):
    segment_index = lax.axis_index("segment")
    frame_count = latent.shape[0]
    group_len = frame_count // GROUPS
    kernel = w_mid[0]
    bias_vec = b_mid[0]
    gain_vec = g_mid[0]
    cache_frames = cache_mid[0]

    def mid_block(current):
        sequence = jnp.concatenate([cache_frames, normed(current, gain_vec)], axis=0)
        extended = with_halo(sequence, (("ha", 1), ("wa", 2)), 1)
        return (current.astype(jnp.float32) + conv_valid(extended, kernel) + bias_vec).astype(
            jnp.bfloat16
        )

    section_one = mid_block(latent)
    received = passed_along(section_one, "segment", 1)
    section_two = mid_block(received)
    returned = passed_along(section_two[:group_len], "segment", -1)
    lead_frames = jnp.zeros((2,) + section_two.shape[1:], section_two.dtype)
    coarse = jnp.where(
        segment_index == 0,
        jnp.concatenate([lead_frames, returned], axis=0),
        section_two[section_two.shape[0] - group_len - 2 :],
    )
    coarse_ext = with_halo(coarse, (("ha", 1), ("wa", 2)), 1)
    doubled = jnp.repeat(jnp.repeat(coarse_ext, 2, axis=1), 2, axis=2)[:, 1:-1, 1:-1, :]
    upsampled = lax.conv_general_dilated(
        doubled,
        w_up,
        (1, 1),
        "VALID",
        dimension_numbers=("NHWC", "HWIO", "NHWC"),
        preferred_element_type=jnp.float32,
    )
    upsampled = (upsampled + b_up).astype(jnp.bfloat16)
    fine_input = normed(upsampled, g_fine)
    context_fine = jnp.where(segment_index == 0, cache_fine, fine_input[:2])
    fine_ext = with_halo(
        jnp.concatenate([context_fine, fine_input[2:]], axis=0), (("ha", 1), ("wa", 2)), 1
    )
    decoded = upsampled[2:].astype(jnp.float32) + conv_valid(fine_ext, w_fine) + b_fine
    return decoded.astype(jnp.bfloat16)


def solution(mesh):
    return jax.shard_map(
        shards,
        mesh=mesh,
        in_specs=(
            P(None, "ha", "wa", None),
            P("segment", None, None, None, None, None),
            P("segment", None),
            P("segment", None),
            P("segment", None, "ha", "wa", None),
            P(),
            P(),
            P(),
            P(None, "ha", "wa", None),
            P(),
            P(),
        ),
        out_specs=P("segment", "ha", "wa", None),
        check_vma=False,
    )
```

profile of v0, /device:TPU:65, one launch (start us, length us, event | category | flops | bytes accessed | tf_op | source)
XLA Modules:
  0.0 142.0 jit_solution(12169875723783852142)
XLA Ops:
  0.0 1.3 fusion.64
  1.3 0.7 reduce.1
  2.0 1.3 fusion.69
  3.3 1.3 fusion.81
  4.7 3.8 %collective-permute-start = (bf16[6,1,20,384]{3,1,2,0:T(2,128)(2,1)S(1)}, bf16[6,1,20,384]{3,1,2,0:T(2,128)(2,1)S(1)}, u32[]{:S(2)}, u32[]{:S(2)}) collective-permute-start(bf16[6,1,20,384]{3,1,2,0:T(2,128)(2,1)S(1)} %get-tuple-element.19), channel_id=1, source_target_pairs={{0,16},{16,32},{32,48},{48,64},{64,80},{80,96},{96,112},{1,17},{17... | collective-permute-start | bytes 276488 | tf_op jit(solution)/shard_map/ppermute | solution.py:16
  8.4 1.9 %collective-permute-start.1 = (bf16[6,1,20,384]{3,1,2,0:T(2,128)(2,1)S(1)}, bf16[6,1,20,384]{3,1,2,0:T(2,128)(2,1)S(1)}, u32[]{:S(2)}, u32[]{:S(2)}) collective-permute-start(bf16[6,1,20,384]{3,1,2,0:T(2,128)(2,1)S(1)} %get-tuple-element.20), channel_id=1, source_target_pairs={{16,0},{32,16},{48,32},{64,48},{80,64},{96,80},{112,96},{17,1},{33... | collective-permute-start | bytes 276488 | tf_op jit(solution)/shard_map/ppermute | solution.py:17
  10.4 0.5 collective-permute-done
  10.9 4.4 %collective-permute-done.1 = bf16[6,1,20,384]{3,1,2,0:T(2,128)(2,1)S(1)} collective-permute-done((bf16[6,1,20,384]{3,1,2,0:T(2,128)(2,1)S(1)}, bf16[6,1,20,384]{3,1,2,0:T(2,128)(2,1)S(1)}, u32[]{:S(2)}, u32[]{:S(2)}) %collective-permute-start.1) | collective-permute-done | bytes 92192 | tf_op jit(solution)/shard_map/ppermute | solution.py:17
  15.3 0.6 fusion.55
  15.9 4.7 %collective-permute-start.2 = (bf16[6,6,1,384]{3,1,2,0:T(8,128)(2,1)S(1)}, bf16[6,6,1,384]{3,1,2,0:T(8,128)(2,1)S(1)}, u32[]{:S(2)}, u32[]{:S(2)}) collective-permute-start(bf16[6,6,1,384]{3,1,2,0:T(8,128)(2,1)S(1)} %get-tuple-element.9), channel_id=1, source_target_pairs={{0,1},{1,2},{2,3},{3,4},{4,5},{5,6},{6,7},{7,8},{8,9},{9,10},{10,1... | collective-permute-start | bytes 82952 | tf_op jit(solution)/shard_map/ppermute | solution.py:16
  20.6 3.0 %collective-permute-start.3 = (bf16[6,6,1,384]{3,1,2,0:T(8,128)(2,1)S(1)}, bf16[6,6,1,384]{3,1,2,0:T(8,128)(2,1)S(1)}, u32[]{:S(2)}, u32[]{:S(2)}) collective-permute-start(bf16[6,6,1,384]{3,1,2,0:T(8,128)(2,1)S(1)} %get-tuple-element.10), channel_id=1, source_target_pairs={{1,0},{2,1},{3,2},{4,3},{5,4},{6,5},{7,6},{8,7},{9,8},{10,9},{11,1... | collective-permute-start | bytes 82952 | tf_op jit(solution)/shard_map/ppermute | solution.py:17
  23.7 3.1 %collective-permute-done.3 = bf16[6,6,1,384]{3,1,2,0:T(8,128)(2,1)S(1)} collective-permute-done((bf16[6,6,1,384]{3,1,2,0:T(8,128)(2,1)S(1)}, bf16[6,6,1,384]{3,1,2,0:T(8,128)(2,1)S(1)}, u32[]{:S(2)}, u32[]{:S(2)}) %collective-permute-start.3) | collective-permute-done | bytes 27680 | tf_op jit(solution)/shard_map/ppermute | solution.py:17
  26.8 0.6 fusion.48
  28.2 8.9 %fusion.26 = f32[4,4,8,3,384]{4,2,3,1,0:T(8,128)S(1)} fusion(bf16[1,3,3,3,384,384]{5,4,3,2,1,0:T(8,128)(2,1)} %param.12, bf16[6,6,1,7,2,384]{5,3,4,1,0,2:T(8,128)(2,1)S(1)} %slice.96, bf16[6,6,1,8,3,384]{5,3,4,1,0,2:T(8,128)(2,1)S(1)} %copy.54, pred[8,3]{0,1:T(4,128)(4,1)S(1)} %copy-done.11), kind=kOutput, calls=%fused_computation.30 | convolution fusion | flops 3061112832 | bytes 9603096 | tf_op jit(solution)/shard_map/conv_general_dilated | solution.py:35
  37.4 2.2 %collective-permute-start.4 = (bf16[4,4,20,384]{3,1,2,0:T(4,128)(2,1)S(1)}, bf16[4,4,20,384]{3,1,2,0:T(4,128)(2,1)S(1)}, u32[]{:S(2)}, u32[]{:S(2)}) collective-permute-start(bf16[4,4,20,384]{3,1,2,0:T(4,128)(2,1)S(1)} %fusion.71), channel_id=1, source_target_pairs={{0,128},{1,129},{2,130},{3,131},{4,132},{5,133},{6,134},{7,135},{8... | collective-permute-start | bytes 737288 | tf_op jit(solution)/shard_map/ppermute | solution.py:25
  39.7 4.4 %collective-permute-done.4 = bf16[4,4,20,384]{3,1,2,0:T(4,128)(2,1)S(1)} collective-permute-done((bf16[4,4,20,384]{3,1,2,0:T(4,128)(2,1)S(1)}, bf16[4,4,20,384]{3,1,2,0:T(4,128)(2,1)S(1)}, u32[]{:S(2)}, u32[]{:S(2)}) %collective-permute-start.4) | collective-permute-done | bytes 245792 | tf_op jit(solution)/shard_map/ppermute | solution.py:25
  45.0 4.8 %collective-permute-start.5 = (bf16[6,1,20,384]{3,1,2,0:T(2,128)(2,1)S(1)}, bf16[6,1,20,384]{3,1,2,0:T(2,128)(2,1)S(1)}, u32[]{:S(2)}, u32[]{:S(2)}) collective-permute-start(bf16[6,1,20,384]{3,1,2,0:T(2,128)(2,1)S(1)} %get-tuple-element.17), channel_id=1, source_target_pairs={{0,16},{16,32},{32,48},{48,64},{64,80},{80,96},{96,112},{1,17},{17... | collective-permute-start | bytes 276488 | tf_op jit(solution)/shard_map/ppermute | solution.py:16
  49.8 1.9 %collective-permute-start.6 = (bf16[6,1,20,384]{3,1,2,0:T(2,128)(2,1)S(1)}, bf16[6,1,20,384]{3,1,2,0:T(2,128)(2,1)S(1)}, u32[]{:S(2)}, u32[]{:S(2)}) collective-permute-start(bf16[6,1,20,384]{3,1,2,0:T(2,128)(2,1)S(1)} %get-tuple-element.18), channel_id=1, source_target_pairs={{16,0},{32,16},{48,32},{64,48},{80,64},{96,80},{112,96},{17,1},{33... | collective-permute-start | bytes 276488 | tf_op jit(solution)/shard_map/ppermute | solution.py:17
  52.3 4.4 %collective-permute-done.6 = bf16[6,1,20,384]{3,1,2,0:T(2,128)(2,1)S(1)} collective-permute-done((bf16[6,1,20,384]{3,1,2,0:T(2,128)(2,1)S(1)}, bf16[6,1,20,384]{3,1,2,0:T(2,128)(2,1)S(1)}, u32[]{:S(2)}, u32[]{:S(2)}) %collective-permute-start.6) | collective-permute-done | bytes 92192 | tf_op jit(solution)/shard_map/ppermute | solution.py:17
  56.7 0.6 fusion.57
  57.3 5.9 %collective-permute-start.7 = (bf16[6,6,1,384]{3,1,2,0:T(8,128)(2,1)S(1)}, bf16[6,6,1,384]{3,1,2,0:T(8,128)(2,1)S(1)}, u32[]{:S(2)}, u32[]{:S(2)}) collective-permute-start(bf16[6,6,1,384]{3,1,2,0:T(8,128)(2,1)S(1)} %get-tuple-element.7), channel_id=1, source_target_pairs={{0,1},{1,2},{2,3},{3,4},{4,5},{5,6},{6,7},{7,8},{8,9},{9,10},{10,1... | collective-permute-start | bytes 82952 | tf_op jit(solution)/shard_map/ppermute | solution.py:16
  63.2 2.1 %collective-permute-start.8 = (bf16[6,6,1,384]{3,1,2,0:T(8,128)(2,1)S(1)}, bf16[6,6,1,384]{3,1,2,0:T(8,128)(2,1)S(1)}, u32[]{:S(2)}, u32[]{:S(2)}) collective-permute-start(bf16[6,6,1,384]{3,1,2,0:T(8,128)(2,1)S(1)} %get-tuple-element.8), channel_id=1, source_target_pairs={{1,0},{2,1},{3,2},{4,3},{5,4},{6,5},{7,6},{8,7},{9,8},{10,9},{11,1... | collective-permute-start | bytes 82952 | tf_op jit(solution)/shard_map/ppermute | solution.py:17
  65.3 4.1 %collective-permute-done.8 = bf16[6,6,1,384]{3,1,2,0:T(8,128)(2,1)S(1)} collective-permute-done((bf16[6,6,1,384]{3,1,2,0:T(8,128)(2,1)S(1)}, bf16[6,6,1,384]{3,1,2,0:T(8,128)(2,1)S(1)}, u32[]{:S(2)}, u32[]{:S(2)}) %collective-permute-start.8) | collective-permute-done | bytes 27680 | tf_op jit(solution)/shard_map/ppermute | solution.py:17
  69.4 0.6 fusion.53
  70.5 4.3 %fusion.29 = f32[4,4,8,3,384]{4,2,3,1,0:T(8,128)S(1)} fusion(bf16[1,3,3,3,384,384]{5,4,3,2,1,0:T(8,128)(2,1)S(1)} %bitcast.96, bf16[6,6,1,7,2,384]{5,3,4,1,0,2:T(8,128)(2,1)S(1)} %slice.102, bf16[6,6,1,8,3,384]{5,3,4,1,0,2:T(8,128)(2,1)S(1)} %copy.58, pred[8,3]{0,1:T(4,128)(4,1)S(1)} %copy-done.11), kind=kOutput, calls=%fused_computation.31 | convolution fusion | flops 3061112832 | bytes 9603096 | tf_op jit(solution)/shard_map/conv_general_dilated | solution.py:35
  75.2 1.3 collective-permute-start.9
  76.5 4.3 %collective-permute-done.9 = bf16[2,4,20,384]{3,1,2,0:T(4,128)(2,1)S(1)} collective-permute-done((bf16[2,4,20,384]{3,1,2,0:T(4,128)(2,1)S(1)}, bf16[2,4,20,384]{3,1,2,0:T(4,128)(2,1)S(1)}, u32[]{:S(2)}, u32[]{:S(2)}) %collective-permute-start.9) | collective-permute-done | bytes 122912 | tf_op jit(solution)/shard_map/ppermute | solution.py:25
  81.1 4.9 %collective-permute-start.10 = (bf16[4,1,20,384]{3,1,2,0:T(2,128)(2,1)S(1)}, bf16[4,1,20,384]{3,1,2,0:T(2,128)(2,1)S(1)}, u32[]{:S(2)}, u32[]{:S(2)}) collective-permute-start(bf16[4,1,20,384]{3,1,2,0:T(2,128)(2,1)S(1)} %get-tuple-element.21), channel_id=1, source_target_pairs={{0,16},{16,32},{32,48},{48,64},{64,80},{80,96},{96,112},{1,17},{17... | collective-permute-start | bytes 184328 | tf_op jit(solution)/shard_map/ppermute | solution.py:16
  86.0 1.9 %collective-permute-start.11 = (bf16[4,1,20,384]{3,1,2,0:T(2,128)(2,1)S(1)}, bf16[4,1,20,384]{3,1,2,0:T(2,128)(2,1)S(1)}, u32[]{:S(2)}, u32[]{:S(2)}) collective-permute-start(bf16[4,1,20,384]{3,1,2,0:T(2,128)(2,1)S(1)} %get-tuple-element.22), channel_id=1, source_target_pairs={{16,0},{32,16},{48,32},{64,48},{80,64},{96,80},{112,96},{17,1},{33... | collective-permute-start | bytes 184328 | tf_op jit(solution)/shard_map/ppermute | solution.py:17
  88.0 4.3 %collective-permute-done.11 = bf16[4,1,20,384]{3,1,2,0:T(2,128)(2,1)S(1)} collective-permute-done((bf16[4,1,20,384]{3,1,2,0:T(2,128)(2,1)S(1)}, bf16[4,1,20,384]{3,1,2,0:T(2,128)(2,1)S(1)}, u32[]{:S(2)}, u32[]{:S(2)}) %collective-permute-start.11) | collective-permute-done | bytes 61472 | tf_op jit(solution)/shard_map/ppermute | solution.py:17
  92.3 5.8 %collective-permute-start.12 = (bf16[4,6,1,384]{3,1,2,0:T(8,128)(2,1)S(1)}, bf16[4,6,1,384]{3,1,2,0:T(8,128)(2,1)S(1)}, u32[]{:S(2)}, u32[]{:S(2)}) collective-permute-start(bf16[4,6,1,384]{3,1,2,0:T(8,128)(2,1)S(1)} %get-tuple-element.15), channel_id=1, source_target_pairs={{0,1},{1,2},{2,3},{3,4},{4,5},{5,6},{6,7},{7,8},{8,9},{9,10},{10,1... | collective-permute-start | bytes 55304 | tf_op jit(solution)/shard_map/ppermute | solution.py:16
  98.1 2.1 %collective-permute-start.13 = (bf16[4,6,1,384]{3,1,2,0:T(8,128)(2,1)S(1)}, bf16[4,6,1,384]{3,1,2,0:T(8,128)(2,1)S(1)}, u32[]{:S(2)}, u32[]{:S(2)}) collective-permute-start(bf16[4,6,1,384]{3,1,2,0:T(8,128)(2,1)S(1)} %get-tuple-element.16), channel_id=1, source_target_pairs={{1,0},{2,1},{3,2},{4,3},{5,4},{6,5},{7,6},{8,7},{9,8},{10,9},{11,1... | collective-permute-start | bytes 55304 | tf_op jit(solution)/shard_map/ppermute | solution.py:17
  100.2 3.9 %collective-permute-done.13 = bf16[4,6,1,384]{3,1,2,0:T(8,128)(2,1)S(1)} collective-permute-done((bf16[4,6,1,384]{3,1,2,0:T(8,128)(2,1)S(1)}, bf16[4,6,1,384]{3,1,2,0:T(8,128)(2,1)S(1)}, u32[]{:S(2)}, u32[]{:S(2)}) %collective-permute-start.13) | collective-permute-done | bytes 18464 | tf_op jit(solution)/shard_map/ppermute | solution.py:17
  105.4 0.9 pad_slice_fusion
  106.5 1.1 fusion.6
  107.8 3.5 %multiply_reduce_fusion = (f32[8,32,6]{1,2,0:T(8,128)S(1)}, bf16[8,32,6,192]{3,1,2,0:T(8,128)(2,1)S(1)}) fusion(f32[192]{0:T(256)S(1)} %copy-done.8, bf16[3,3,384,192]{2,3,1,0:T(8,128)(2,1)S(1)} %copy-done.7, bf16[12,4,8,8,384]{4,1,3,2,0:T(4,128)(2,1)S(1)} %fusion.6, pred[32,6]{0,1:T(8,128)(4,1)S(1)} %copy-done.10), kind=kOutput, calls=%fused_computation.16 | convolution fusion | flops 2040199680 | bytes 4283328 | tf_op jit(solution)/shard_map/conv_general_dilated | solution.py:73
  111.4 0.8 copy.65
  112.2 1.0 reshape.61
  114.6 3.2 %collective-permute-start.14 = (bf16[4,1,40,192]{3,1,2,0:T(2,128)(2,1)S(1)}, bf16[4,1,40,192]{3,1,2,0:T(2,128)(2,1)S(1)}, u32[]{:S(2)}, u32[]{:S(2)}) collective-permute-start(bf16[4,1,40,192]{3,1,2,0:T(2,128)(2,1)S(1)} %get-tuple-element.11), channel_id=1, source_target_pairs={{0,16},{16,32},{32,48},{48,64},{64,80},{80,96},{96,112},{1,17},{17... | collective-permute-start | bytes 184328 | tf_op jit(solution)/shard_map/ppermute | solution.py:16
  117.8 1.9 %collective-permute-start.15 = (bf16[4,1,40,192]{3,1,2,0:T(2,128)(2,1)S(1)}, bf16[4,1,40,192]{3,1,2,0:T(2,128)(2,1)S(1)}, u32[]{:S(2)}, u32[]{:S(2)}) collective-permute-start(bf16[4,1,40,192]{3,1,2,0:T(2,128)(2,1)S(1)} %get-tuple-element.12), channel_id=1, source_target_pairs={{16,0},{32,16},{48,32},{64,48},{80,64},{96,80},{112,96},{17,1},{33... | collective-permute-start | bytes 184328 | tf_op jit(solution)/shard_map/ppermute | solution.py:17
  120.2 4.3 %collective-permute-done.15 = bf16[4,1,40,192]{3,1,2,0:T(2,128)(2,1)S(1)} collective-permute-done((bf16[4,1,40,192]{3,1,2,0:T(2,128)(2,1)S(1)}, bf16[4,1,40,192]{3,1,2,0:T(2,128)(2,1)S(1)}, u32[]{:S(2)}, u32[]{:S(2)}) %collective-permute-start.15) | collective-permute-done | bytes 61472 | tf_op jit(solution)/shard_map/ppermute | solution.py:17
  124.5 5.7 %collective-permute-start.16 = (bf16[4,10,1,192]{3,1,2,0:T(8,128)(2,1)S(1)}, bf16[4,10,1,192]{3,1,2,0:T(8,128)(2,1)S(1)}, u32[]{:S(2)}, u32[]{:S(2)}) collective-permute-start(bf16[4,10,1,192]{3,1,2,0:T(8,128)(2,1)S(1)} %get-tuple-element.5), channel_id=1, source_target_pairs={{0,1},{1,2},{2,3},{3,4},{4,5},{5,6},{6,7},{7,8},{8,9},{9,10},{10,1... | collective-permute-start | bytes 46088 | tf_op jit(solution)/shard_map/ppermute | solution.py:16
  130.2 2.3 %collective-permute-start.17 = (bf16[4,10,1,192]{3,1,2,0:T(8,128)(2,1)S(1)}, bf16[4,10,1,192]{3,1,2,0:T(8,128)(2,1)S(1)}, u32[]{:S(2)}, u32[]{:S(2)}) collective-permute-start(bf16[4,10,1,192]{3,1,2,0:T(8,128)(2,1)S(1)} %get-tuple-element.6), channel_id=1, source_target_pairs={{1,0},{2,1},{3,2},{4,3},{5,4},{6,5},{7,6},{8,7},{9,8},{10,9},{11,1... | collective-permute-start | bytes 46088 | tf_op jit(solution)/shard_map/ppermute | solution.py:17
  132.5 3.8 %collective-permute-done.17 = bf16[4,10,1,192]{3,1,2,0:T(8,128)(2,1)S(1)} collective-permute-done((bf16[4,10,1,192]{3,1,2,0:T(8,128)(2,1)S(1)}, bf16[4,10,1,192]{3,1,2,0:T(8,128)(2,1)S(1)}, u32[]{:S(2)}, u32[]{:S(2)}) %collective-permute-start.17) | collective-permute-done | bytes 15392 | tf_op jit(solution)/shard_map/ppermute | solution.py:17
  136.4 0.9 maximum_bitcast_fusion
  137.6 0.6 copy.70
  138.3 2.4 %fusion.23 = f32[2,8,8,6,192]{4,2,3,1,0:T(8,128)S(1)} fusion(bf16[3,3,3,192,192]{4,3,2,1,0:T(8,128)(2,1)S(1)} %copy-done, bf16[4,10,1,7,2,192]{5,3,4,1,0,2:T(8,128)(2,1)S(1)} %slice.114, bf16[4,10,1,8,6,192]{5,3,4,1,0,2:T(8,128)(2,1)S(1)} %copy.70, pred[8,6]{0,1:T(8,128)(4,1)S(1)} %copy-done.9), kind=kOutput, calls=%fused_computation.29 | convolution fusion | flops 1531920384 | bytes 3532848 | tf_op jit(solution)/shard_map/conv_general_dilated | solution.py:35
  141.2 0.8 copy.72
  (77 shorter events, 8.2 us)
Async XLA Ops:
  0.0 138.2 %copy-start = (bf16[3,3,3,192,192]{4,3,2,1,0:T(8,128)(2,1)S(1)}, bf16[3,3,3,192,192]{4,3,2,1,0:T(8,128)(2,1)}, u32[]{:S(2)}) copy-start(bf16[3,3,3,192,192]{4,3,2,1,0:T(8,128)(2,1)} %param.20) | copy-start | bytes 5971972
  0.0 15.3 %copy-start.1 = (bf16[1,2,4,20,384]{4,2,3,1,0:T(4,128)(2,1)S(1)}, bf16[1,2,4,20,384]{4,2,3,1,0:T(4,128)(2,1)}, u32[]{:S(2)}) copy-start(bf16[1,2,4,20,384]{4,2,3,1,0:T(4,128)(2,1)} %param.15) | copy-start | bytes 368644
  0.0 23.6 %copy-start.4 = (f32[1,384]{1,0:T(1,128)S(1)}, f32[1,384]{1,0:T(1,128)}, u32[]{:S(2)}) copy-start(f32[1,384]{1,0:T(1,128)} %param.13) | copy-start | bytes 4612
  4.7 6.2 %collective-permute-start = (bf16[6,1,20,384]{3,1,2,0:T(2,128)(2,1)S(1)}, bf16[6,1,20,384]{3,1,2,0:T(2,128)(2,1)S(1)}, u32[]{:S(2)}, u32[]{:S(2)}) collective-permute-start(bf16[6,1,20,384]{3,1,2,0:T(2,128)(2,1)S(1)} %get-tuple-element.19), channel_id=1, source_target_pairs={{0,16},{16,32},{32,48},{48,64},{64,80},{80,96},{96,112},{1,17},{17... | collective-permute-start | bytes 276488 | tf_op jit(solution)/shard_map/ppermute | solution.py:16
  8.4 6.9 %collective-permute-start.1 = (bf16[6,1,20,384]{3,1,2,0:T(2,128)(2,1)S(1)}, bf16[6,1,20,384]{3,1,2,0:T(2,128)(2,1)S(1)}, u32[]{:S(2)}, u32[]{:S(2)}) collective-permute-start(bf16[6,1,20,384]{3,1,2,0:T(2,128)(2,1)S(1)} %get-tuple-element.20), channel_id=1, source_target_pairs={{16,0},{32,16},{48,32},{64,48},{80,64},{96,80},{112,96},{17,1},{33... | collective-permute-start | bytes 276488 | tf_op jit(solution)/shard_map/ppermute | solution.py:17
  15.9 7.7 %collective-permute-start.2 = (bf16[6,6,1,384]{3,1,2,0:T(8,128)(2,1)S(1)}, bf16[6,6,1,384]{3,1,2,0:T(8,128)(2,1)S(1)}, u32[]{:S(2)}, u32[]{:S(2)}) collective-permute-start(bf16[6,6,1,384]{3,1,2,0:T(8,128)(2,1)S(1)} %get-tuple-element.9), channel_id=1, source_target_pairs={{0,1},{1,2},{2,3},{3,4},{4,5},{5,6},{6,7},{7,8},{8,9},{9,10},{10,1... | collective-permute-start | bytes 82952 | tf_op jit(solution)/shard_map/ppermute | solution.py:16
  20.6 6.2 %collective-permute-start.3 = (bf16[6,6,1,384]{3,1,2,0:T(8,128)(2,1)S(1)}, bf16[6,6,1,384]{3,1,2,0:T(8,128)(2,1)S(1)}, u32[]{:S(2)}, u32[]{:S(2)}) collective-permute-start(bf16[6,6,1,384]{3,1,2,0:T(8,128)(2,1)S(1)} %get-tuple-element.10), channel_id=1, source_target_pairs={{1,0},{2,1},{3,2},{4,3},{5,4},{6,5},{7,6},{8,7},{9,8},{10,9},{11,1... | collective-permute-start | bytes 82952 | tf_op jit(solution)/shard_map/ppermute | solution.py:17
  27.6 0.7 copy-start.11
  27.7 42.7 %slice-start = ((s8[7962624]{0:T(1024)(128)(4,1)}), s8[4194304]{0:T(1024)(128)(4,1)S(1)}, s32[]{:S(2)}) async-start(s8[7962624]{0:T(1024)(128)(4,1)} %bitcast.95), calls=%async_computation | async-start | bytes 8388608
  28.2 9.0 %copy-start.2 = (bf16[4,4,20,384]{3,1,2,0:T(4,128)(2,1)S(1)}, bf16[4,4,20,384]{3,1,2,0:T(4,128)(2,1)}, u32[]{:S(2)}) copy-start(bf16[4,4,20,384]{3,1,2,0:T(4,128)(2,1)} %param.11) | copy-start | bytes 737284
  28.2 42.2 %slice-start.1 = ((s8[7962624]{0:T(1024)(128)(4,1)}), s8[3768320]{0:T(1024)(128)(4,1)S(1)}, s32[]{:S(2)}) async-start(s8[7962624]{0:T(1024)(128)(4,1)} %bitcast.95), calls=%async_computation.1 | async-start | bytes 7536640
  37.4 6.7 %collective-permute-start.4 = (bf16[4,4,20,384]{3,1,2,0:T(4,128)(2,1)S(1)}, bf16[4,4,20,384]{3,1,2,0:T(4,128)(2,1)S(1)}, u32[]{:S(2)}, u32[]{:S(2)}) collective-permute-start(bf16[4,4,20,384]{3,1,2,0:T(4,128)(2,1)S(1)} %fusion.71), channel_id=1, source_target_pairs={{0,128},{1,129},{2,130},{3,131},{4,132},{5,133},{6,134},{7,135},{8... | collective-permute-start | bytes 737288 | tf_op jit(solution)/shard_map/ppermute | solution.py:25
  45.0 7.3 %collective-permute-start.5 = (bf16[6,1,20,384]{3,1,2,0:T(2,128)(2,1)S(1)}, bf16[6,1,20,384]{3,1,2,0:T(2,128)(2,1)S(1)}, u32[]{:S(2)}, u32[]{:S(2)}) collective-permute-start(bf16[6,1,20,384]{3,1,2,0:T(2,128)(2,1)S(1)} %get-tuple-element.17), channel_id=1, source_target_pairs={{0,16},{16,32},{32,48},{48,64},{64,80},{80,96},{96,112},{1,17},{17... | collective-permute-start | bytes 276488 | tf_op jit(solution)/shard_map/ppermute | solution.py:16
  49.8 6.9 %collective-permute-start.6 = (bf16[6,1,20,384]{3,1,2,0:T(2,128)(2,1)S(1)}, bf16[6,1,20,384]{3,1,2,0:T(2,128)(2,1)S(1)}, u32[]{:S(2)}, u32[]{:S(2)}) collective-permute-start(bf16[6,1,20,384]{3,1,2,0:T(2,128)(2,1)S(1)} %get-tuple-element.18), channel_id=1, source_target_pairs={{16,0},{32,16},{48,32},{64,48},{80,64},{96,80},{112,96},{17,1},{33... | collective-permute-start | bytes 276488 | tf_op jit(solution)/shard_map/ppermute | solution.py:17
  57.3 8.0 %collective-permute-start.7 = (bf16[6,6,1,384]{3,1,2,0:T(8,128)(2,1)S(1)}, bf16[6,6,1,384]{3,1,2,0:T(8,128)(2,1)S(1)}, u32[]{:S(2)}, u32[]{:S(2)}) collective-permute-start(bf16[6,6,1,384]{3,1,2,0:T(8,128)(2,1)S(1)} %get-tuple-element.7), channel_id=1, source_target_pairs={{0,1},{1,2},{2,3},{3,4},{4,5},{5,6},{6,7},{7,8},{8,9},{9,10},{10,1... | collective-permute-start | bytes 82952 | tf_op jit(solution)/shard_map/ppermute | solution.py:16
  63.2 6.2 %collective-permute-start.8 = (bf16[6,6,1,384]{3,1,2,0:T(8,128)(2,1)S(1)}, bf16[6,6,1,384]{3,1,2,0:T(8,128)(2,1)S(1)}, u32[]{:S(2)}, u32[]{:S(2)}) collective-permute-start(bf16[6,6,1,384]{3,1,2,0:T(8,128)(2,1)S(1)} %get-tuple-element.8), channel_id=1, source_target_pairs={{1,0},{2,1},{3,2},{4,3},{5,4},{6,5},{7,6},{8,7},{9,8},{10,9},{11,1... | collective-permute-start | bytes 82952 | tf_op jit(solution)/shard_map/ppermute | solution.py:17
  75.2 5.6 %collective-permute-start.9 = (bf16[2,4,20,384]{3,1,2,0:T(4,128)(2,1)S(1)}, bf16[2,4,20,384]{3,1,2,0:T(4,128)(2,1)S(1)}, u32[]{:S(2)}, u32[]{:S(2)}) collective-permute-start(bf16[2,4,20,384]{3,1,2,0:T(4,128)(2,1)S(1)} %slice.104), channel_id=1, source_target_pairs={{128,0},{129,1},{130,2},{131,3},{132,4},{133,5},{134,6},{135,7},{1... | collective-permute-start | bytes 368648 | tf_op jit(solution)/shard_map/ppermute | solution.py:25
  81.1 6.8 %collective-permute-start.10 = (bf16[4,1,20,384]{3,1,2,0:T(2,128)(2,1)S(1)}, bf16[4,1,20,384]{3,1,2,0:T(2,128)(2,1)S(1)}, u32[]{:S(2)}, u32[]{:S(2)}) collective-permute-start(bf16[4,1,20,384]{3,1,2,0:T(2,128)(2,1)S(1)} %get-tuple-element.21), channel_id=1, source_target_pairs={{0,16},{16,32},{32,48},{48,64},{64,80},{80,96},{96,112},{1,17},{17... | collective-permute-start | bytes 184328 | tf_op jit(solution)/shard_map/ppermute | solution.py:16
  86.0 6.2 %collective-permute-start.11 = (bf16[4,1,20,384]{3,1,2,0:T(2,128)(2,1)S(1)}, bf16[4,1,20,384]{3,1,2,0:T(2,128)(2,1)S(1)}, u32[]{:S(2)}, u32[]{:S(2)}) collective-permute-start(bf16[4,1,20,384]{3,1,2,0:T(2,128)(2,1)S(1)} %get-tuple-element.22), channel_id=1, source_target_pairs={{16,0},{32,16},{48,32},{64,48},{80,64},{96,80},{112,96},{17,1},{33... | collective-permute-start | bytes 184328 | tf_op jit(solution)/shard_map/ppermute | solution.py:17
  92.3 8.0 %collective-permute-start.12 = (bf16[4,6,1,384]{3,1,2,0:T(8,128)(2,1)S(1)}, bf16[4,6,1,384]{3,1,2,0:T(8,128)(2,1)S(1)}, u32[]{:S(2)}, u32[]{:S(2)}) collective-permute-start(bf16[4,6,1,384]{3,1,2,0:T(8,128)(2,1)S(1)} %get-tuple-element.15), channel_id=1, source_target_pairs={{0,1},{1,2},{2,3},{3,4},{4,5},{5,6},{6,7},{7,8},{8,9},{9,10},{10,1... | collective-permute-start | bytes 55304 | tf_op jit(solution)/shard_map/ppermute | solution.py:16
  98.1 6.1 %collective-permute-start.13 = (bf16[4,6,1,384]{3,1,2,0:T(8,128)(2,1)S(1)}, bf16[4,6,1,384]{3,1,2,0:T(8,128)(2,1)S(1)}, u32[]{:S(2)}, u32[]{:S(2)}) collective-permute-start(bf16[4,6,1,384]{3,1,2,0:T(8,128)(2,1)S(1)} %get-tuple-element.16), channel_id=1, source_target_pairs={{1,0},{2,1},{3,2},{4,3},{5,4},{6,5},{7,6},{8,7},{9,8},{10,9},{11,1... | collective-permute-start | bytes 55304 | tf_op jit(solution)/shard_map/ppermute | solution.py:17
  106.5 1.3 copy-start.7
  106.5 1.3 copy-start.8
  106.5 1.3 copy-start.10
  111.3 2.4 %copy-start.5 = (f32[192]{0:T(256)S(1)}, f32[192]{0:T(256)}, u32[]{:S(2)}) copy-start(f32[192]{0:T(256)} %param.18) | copy-start | bytes 2308
  113.3 1.0 copy-start.3
  114.6 5.6 %collective-permute-start.14 = (bf16[4,1,40,192]{3,1,2,0:T(2,128)(2,1)S(1)}, bf16[4,1,40,192]{3,1,2,0:T(2,128)(2,1)S(1)}, u32[]{:S(2)}, u32[]{:S(2)}) collective-permute-start(bf16[4,1,40,192]{3,1,2,0:T(2,128)(2,1)S(1)} %get-tuple-element.11), channel_id=1, source_target_pairs={{0,16},{16,32},{32,48},{48,64},{64,80},{80,96},{96,112},{1,17},{17... | collective-permute-start | bytes 184328 | tf_op jit(solution)/shard_map/ppermute | solution.py:16
  117.8 6.6 %collective-permute-start.15 = (bf16[4,1,40,192]{3,1,2,0:T(2,128)(2,1)S(1)}, bf16[4,1,40,192]{3,1,2,0:T(2,128)(2,1)S(1)}, u32[]{:S(2)}, u32[]{:S(2)}) collective-permute-start(bf16[4,1,40,192]{3,1,2,0:T(2,128)(2,1)S(1)} %get-tuple-element.12), channel_id=1, source_target_pairs={{16,0},{32,16},{48,32},{64,48},{80,64},{96,80},{112,96},{17,1},{33... | collective-permute-start | bytes 184328 | tf_op jit(solution)/shard_map/ppermute | solution.py:17
  124.5 8.0 %collective-permute-start.16 = (bf16[4,10,1,192]{3,1,2,0:T(8,128)(2,1)S(1)}, bf16[4,10,1,192]{3,1,2,0:T(8,128)(2,1)S(1)}, u32[]{:S(2)}, u32[]{:S(2)}) collective-permute-start(bf16[4,10,1,192]{3,1,2,0:T(8,128)(2,1)S(1)} %get-tuple-element.5), channel_id=1, source_target_pairs={{0,1},{1,2},{2,3},{3,4},{4,5},{5,6},{6,7},{7,8},{8,9},{9,10},{10,1... | collective-permute-start | bytes 46088 | tf_op jit(solution)/shard_map/ppermute | solution.py:16
  130.2 6.2 %collective-permute-start.17 = (bf16[4,10,1,192]{3,1,2,0:T(8,128)(2,1)S(1)}, bf16[4,10,1,192]{3,1,2,0:T(8,128)(2,1)S(1)}, u32[]{:S(2)}, u32[]{:S(2)}) collective-permute-start(bf16[4,10,1,192]{3,1,2,0:T(8,128)(2,1)S(1)} %get-tuple-element.6), channel_id=1, source_target_pairs={{1,0},{2,1},{3,2},{4,3},{5,4},{6,5},{7,6},{8,7},{9,8},{10,9},{11,1... | collective-permute-start | bytes 46088 | tf_op jit(solution)/shard_map/ppermute | solution.py:17
  137.6 0.7 copy-start.9
  138.3 2.9 %copy-start.6 = (f32[192]{0:T(256)S(1)}, f32[192]{0:T(256)}, u32[]{:S(2)}) copy-start(f32[192]{0:T(256)} %param.21) | copy-start | bytes 2308
where the time goes:
time: 143 us; the launch traced here: 142 us
  starting transfers between devices  59.5 us (42%)
  waiting for transfers between devices  42.1 us (29%)
  matrix products  19.1 us (13%)
  other arithmetic  11.8 us (8%)
  local copies, waits for them, and re-layouts  8.86 us (6%)
    ppermute x8, starting transfers between devices, with_halo(): before = lax.ppermute(last, axis, up)  38.7 us
    ppermute x8, waiting for transfers between devices, with_halo(): after = lax.ppermute(first, axis, down)  32.3 us
    ppermute x8, starting transfers between devices, with_halo(): after = lax.ppermute(first, axis, down)  17.2 us
    conv_general_dilated x3, matrix products, conv_valid(): lax.conv_general_dilated(extended[None], kernel, (1, 1, 1), 'VALID', dime...  15.6 us
    ppermute x2, waiting for transfers between devices, passed_along(): return lax.ppermute(shard, axis, pairs)  8.75 us
    conv_general_dilated x1, matrix products, shards(): lax.conv_general_dilated(doubled, w_up, (1, 1), 'VALID', dimension_number...  3.55 us
    ppermute x2, starting transfers between devices, passed_along(): return lax.ppermute(shard, axis, pairs)  3.52 us
  transfers between devices with their start and end apart: 18, of which 12 were waited for; matrix products, arithmetic and copies ran while one was open for 0% of the time, Pallas kernels for 0%

commit v1 on v0

v1 whole, which is shorter than its diff:
```python
import jax
import jax.numpy as jnp
from jax import lax
from jax.experimental import pallas as pl
from jax.experimental.pallas import tpu as pltpu
from jax.sharding import PartitionSpec as P

F32 = jnp.float32
BF16 = jnp.bfloat16
CM = 384
CF = 192
AXES = ("segment", "ha", "wa")
N_HA = 8
N_WA = 16
GRID_ROWS = 32
GRID_COLS = 320
TILE_ROWS = 4
TILE_COLS = 20
WIDE = 26
NARROW = 24
HALF = 56


def normed(values, gain_vec, channels):
    inv_rms = lax.rsqrt(jnp.sum(values * values, axis=-1, keepdims=True) * (1.0 / channels) + 1e-06)
    scaled = values * inv_rms * gain_vec
    return scaled / (1.0 + jnp.exp(-scaled))


def conv_frames(patches, w_ref, length):
    total = None
    for a in range(3):
        for pq in range(9):
            lhs = patches[a : a + 2, pq].reshape(2 * length, patches.shape[-1])
            part = jnp.dot(lhs, w_ref[a * 9 + pq], preferred_element_type=F32)
            total = part if total is None else total + part
    return total


def first_kernel(group, info, latent, cache, below, left, right, w, b, g, out, raw, act, side, patches):
    @pl.when(info[0] == 0)
    def _():
        last = info[1] == N_HA - 1
        side[0] = left[...].astype(F32)
        side[1] = right[...].astype(F32)
        slots = [(1, False), (2, False), (3, False), (4, True), (3, True), (4, False), (5, False), (6, False)]
        for f in range(4):
            lead = group == 0 and f < 2
            frame = f if group == 1 else (4 + f if lead else f - 2)
            for slot, (row, hide) in enumerate(slots):
                if row >= TILE_ROWS:
                    mid = below[frame, row - TILE_ROWS]
                elif frame >= 4:
                    mid = cache[frame - 4, row]
                else:
                    mid = latent[frame, row]
                mid = mid.astype(F32)
                at = (frame * 7 + row) * 3
                lo = side[0, at : at + 3]
                hi = side[1, at : at + 3]
                if hide:
                    mid = jnp.where(last, 0.0, mid)
                    lo = jnp.where(last, 0.0, lo)
                    hi = jnp.where(last, 0.0, hi)
                base = slot * WIDE
                raw[f, base : base + 3] = lo
                raw[f, base + 3 : base + 3 + TILE_COLS] = mid
                raw[f, base + 3 + TILE_COLS : base + WIDE] = hi
            raw[f, 8 * WIDE : 216] = jnp.zeros((8, CM), F32)
            for h in range(3):
                part = raw[f, h * 72 : h * 72 + 72]
                act[f, h * 72 : h * 72 + 72] = part if lead else normed(part, g[...], CM)
            for p in range(3):
                for q in range(3):
                    top = p * WIDE + q
                    low = top + 4 * WIDE
                    both = jnp.concatenate([act[f, top : top + HALF], act[f, low : low + HALF]], axis=0)
                    patches[f, p * 3 + q] = both.astype(BF16)
        total = conv_frames(patches, w, 2 * HALF) + b[...]
        cols = lax.broadcasted_iota(jnp.int32, (NARROW, 1), 0) + (info[2] * TILE_COLS - 2)
        inside = (cols >= 0) & (cols < GRID_COLS)
        act[0, 0 : 2 * HALF] = total[: 2 * HALF]
        act[1, 0 : 2 * HALF] = total[2 * HALF :]
        for t in range(2):
            for r in range(4):
                src = (r // 2) * HALF + (r % 2) * WIDE
                res = ((r // 2) * 4 + r % 2 + 1) * WIDE + 1
                value = act[t, src : src + NARROW] + raw[2 + t, res : res + NARROW]
                out[t, r] = jnp.where(inside, value, 0.0).astype(BF16)


def second_kernel(group, info, cache, above, top_a, low_a, top_b, low_b, w, b, g, out, raw, act, patches):
    @pl.when(info[0] == 1)
    def _():
        first = info[1] == 0
        last = info[1] == N_HA - 1
        for f in range(4):
            lead = group == 0 and f < 2
            index = f % 2
            top, low = (top_a, low_a) if (group == 0 or f < 2) else (top_b, low_b)
            for u in range(8):
                if lead:
                    row = above[index, u] if u < 2 else cache[index, u - 2]
                else:
                    row = top[index, u] if u < 4 else low[index, u - 4]
                row = row.astype(F32)
                if u < 2:
                    row = jnp.where(first, 0.0, row)
                if u > 5:
                    row = jnp.where(last, 0.0, row)
                raw[f, u * NARROW : (u + 1) * NARROW] = row
            raw[f, 8 * NARROW : 200] = jnp.zeros((8, CM), F32)
            for h in range(2):
                lo, hi = (0, 96) if h == 0 else (96, 200)
                part = raw[f, lo:hi]
                act[f, lo:hi] = part if lead else normed(part, g[...], CM)
            for p in range(3):
                for q in range(3):
                    at = p * NARROW + q
                    patches[f, p * 3 + q] = act[f, at : at + 144].astype(BF16)
        total = conv_frames(patches, w, 144) + b[...]
        cell = lax.broadcasted_iota(jnp.int32, (NARROW, 1), 0)
        cols = cell + (info[2] * TILE_COLS - 1)
        inside = (cols >= 0) & (cols < GRID_COLS) & (cell < 22)
        for t in range(2):
            for i in range(6):
                row_at = info[1] * TILE_ROWS - 1 + i
                fits = inside & (row_at >= 0) & (row_at < GRID_ROWS)
                res = (i + 1) * NARROW + 1
                value = total[t * 144 + i * NARROW : t * 144 + (i + 1) * NARROW] + raw[2 + t, res : res + NARROW]
                out[t, i * NARROW : (i + 1) * NARROW] = jnp.where(fits, value, 0.0).astype(BF16)


def fine_kernel(info, lead, main, returned, cache, w_up, b_up, g, w, b, out, coarse, ups, act, rows, patches, wide):
    def upsample(src, slot, keep):
        for t in range(2):
            coarse[t, 0:144] = src[t].astype(F32)
            coarse[t, 144:160] = jnp.zeros((16, CM), F32)
        lhs = [
            jnp.concatenate([coarse[t, du * NARROW + dv : du * NARROW + dv + 128].astype(BF16) for t in range(2)], axis=0)
            for du in range(2)
            for dv in range(2)
        ]
        cell = lax.broadcasted_iota(jnp.int32, (128, 1), 0)
        col = lax.rem(cell, NARROW)
        for phase in range(4):
            br, bc = phase // 2, phase % 2
            total = None
            for k in range(4):
                part = jnp.dot(lhs[k], w_up[k, :, phase * 256 : phase * 256 + 256], preferred_element_type=F32)
                total = part if total is None else total + part
            value = (total + b_up[...]).astype(BF16).astype(F32)
            if br == 0:
                outside = (cell < NARROW) & (info[1] == 0)
            else:
                outside = (cell >= 4 * NARROW) & (info[1] == N_HA - 1)
            if bc == 0:
                outside |= (col == 0) & (info[2] == 0)
            else:
                outside |= (col == TILE_COLS) & (info[2] == N_WA - 1)
            unit = normed(value, g[...], CF)
            for t in range(2):
                if keep:
                    ups[t, phase] = value[t * 128 : t * 128 + 128]
                act[slot + t, phase] = jnp.where(outside, 0.0, unit[t * 128 : t * 128 + 128])

    @pl.when(info[0] == 0)
    def _():
        for t in range(2):
            for e in range(10):
                line = cache[t, e].astype(F32)
                rows[0, 0:42] = line[:, :128]
                rows[1, 0:42, 0:64] = line[:, 128:]
                br, u = e % 2, e // 2
                for bc in range(2):
                    for c in range(2):
                        act[t, br * 2 + bc, u * NARROW : (u + 1) * NARROW, c * 128 : c * 128 + 128] = rows[
                            c, pl.ds(bc, NARROW, 2), :
                        ]
        upsample(returned, 2, True)

    @pl.when(info[0] == 1)
    def _():
        upsample(lead, 0, False)
        upsample(main, 2, True)

    for f in range(4):
        for plane in range(4):
            for s in range(4):
                at = (s // 2) * NARROW + s % 2
                patches[f, plane * 4 + s] = act[f, plane, at : at + 96].astype(BF16)
    for yb in range(2):
        for xb in range(2):
            total = None
            for a in range(3):
                for p in range(3):
                    for q in range(3):
                        plane = ((yb + p) % 2) * 2 + (xb + q) % 2
                        block = plane * 4 + ((yb + p) // 2) * 2 + (xb + q) // 2
                        lhs = patches[a : a + 2, block].reshape(192, 256)[:, :CF]
                        part = jnp.dot(lhs, w[a * 9 + p * 3 + q], preferred_element_type=F32)
                        total = part if total is None else total + part
            total = total + b[...]
            plane = ((yb + 1) % 2) * 2 + (xb + 1) % 2
            at = ((yb + 1) // 2) * NARROW + (xb + 1) // 2
            for t in range(2):
                value = total[t * 96 : t * 96 + 96] + ups[t, plane, at : at + 96][:, :CF]
                for y in range(4):
                    line = value[y * NARROW : y * NARROW + TILE_COLS]
                    wide[0, t, 2 * y + yb, pl.ds(xb, TILE_COLS, 2), :] = line[:, :128]
                    wide[1, t, 2 * y + yb, pl.ds(xb, TILE_COLS, 2), :] = jnp.concatenate(
                        [line[:, 128:], line[:, 128:]], axis=1
                    )
    for t in range(2):
        for y in range(8):
            out[t, y, :, :128] = wide[0, t, y].astype(BF16)
            out[t, y, :, 128:] = wide[1, t, y][:, :64].astype(BF16)


def call(body, out_shape, scratch, *operands):
    specs = [pl.BlockSpec(memory_space=pltpu.SMEM)] + [pl.BlockSpec(memory_space=pltpu.VMEM)] * (len(operands) - 1)
    return pl.pallas_call(
        body,
        out_shape=jax.ShapeDtypeStruct(out_shape, BF16),
        in_specs=specs,
        out_specs=pl.BlockSpec(memory_space=pltpu.VMEM),
        scratch_shapes=scratch,
        compiler_params=pltpu.CompilerParams(vmem_limit_bytes=40 * 2**20),
    )(*operands)


def device_at(s, h, w):
    return (s * N_HA + h) * N_WA + w


def from_first(by):
    return [
        (device_at(0, (h + by) % N_HA, w), device_at(1, h, w)) for h in range(N_HA) for w in range(N_WA)
    ]


def shards(latent, w_mid, b_mid, g_mid, cache_mid, w_up, b_up, g_fine, cache_fine, w_fine, b_fine):
    segment, ha, wa = (lax.axis_index(axis) for axis in AXES)
    info = jnp.stack([segment, ha, wa]).astype(jnp.int32)
    cache = cache_mid[0]
    kernel = w_mid.reshape(27, CM, CM)

    below = lax.ppermute(
        jnp.concatenate([latent[:, :3], cache[:, :3]], axis=0), "ha", [(i, (i - 1) % N_HA) for i in range(N_HA)]
    )
    tall = jnp.concatenate([jnp.concatenate([latent, cache], axis=0), below], axis=1)
    pad = ((0, 2), (0, 0))
    edge = lambda lo, hi: jnp.pad(tall[:, :, lo:hi].reshape(6 * 7 * 3, CM), pad)
    left = lax.ppermute(edge(TILE_COLS - 3, TILE_COLS), "wa", [(i, i + 1) for i in range(N_WA - 1)])
    right = lax.ppermute(edge(0, 3), "wa", [(i + 1, i) for i in range(N_WA - 1)])

    first_scratch = [
        pltpu.VMEM((4, 216, CM), F32),
        pltpu.VMEM((4, 216, CM), F32),
        pltpu.VMEM((2, 128, CM), F32),
        pltpu.VMEM((4, 9, 2 * HALF, CM), BF16),
    ]
    first = lambda group: call(
        lambda *refs: first_kernel(group, *refs),
        (2, TILE_ROWS, NARROW, CM),
        first_scratch,
        info, latent, cache, below, left, right, kernel, b_mid, g_mid,
    )
    early = first(0)
    low_a, top_a = (lax.ppermute(early, AXES, from_first(by)) for by in (0, -1))
    late = first(1)
    low_b, top_b = (lax.ppermute(late, AXES, from_first(by)) for by in (0, -1))

    sides = [v[:126].reshape(6, 7, 3, CM)[4:, :6] for v in (left, right)]
    cache_ext = jnp.concatenate([sides[0][:, :, 1:], tall[4:, :6], sides[1][:, :, :2]], axis=2)
    above = lax.ppermute(
        cache_ext[:, 2:4],
        AXES,
        [(device_at(1, h, w), device_at(1, h + 1, w)) for h in range(N_HA - 1) for w in range(N_WA)],
    )
    second_scratch = [
        pltpu.VMEM((4, 200, CM), F32),
        pltpu.VMEM((4, 200, CM), F32),
        pltpu.VMEM((4, 9, 144, CM), BF16),
    ]
    second = lambda group: call(
        lambda *refs: second_kernel(group, *refs),
        (2, 6 * NARROW, CM),
        second_scratch,
        info, cache_ext, above, top_a, low_a, top_b, low_b, kernel, b_mid, g_mid,
    )
    second_a = call(
        lambda i, c, ab, ta, la, *refs: second_kernel(0, i, c, ab, ta, la, ta, la, *refs),
        (2, 6 * NARROW, CM),
        second_scratch,
        info, cache_ext, above, top_a, low_a, kernel, b_mid, g_mid,
    )
    returned = lax.ppermute(second_a, "segment", [(1, 0)])
    second_b = call(
        lambda i, ta, la, tb, lb, *refs: second_kernel(1, i, None, None, ta, la, tb, lb, *refs),
        (2, 6 * NARROW, CM),
        second_scratch,
        info, top_a, low_a, top_b, low_b, kernel, b_mid, g_mid,
    )

    fine = cache_fine
    for axis, dim, size in (("ha", 1, N_HA), ("wa", 2, N_WA)):
        up = [(i, i + 1) for i in range(size - 1)]
        down = [(i + 1, i) for i in range(size - 1)]
        length = fine.shape[dim]
        before = lax.ppermute(lax.slice_in_dim(fine, length - 1, length, axis=dim), axis, up)
        after = lax.ppermute(lax.slice_in_dim(fine, 0, 1, axis=dim), axis, down)
        fine = jnp.concatenate([before, fine, after], axis=dim)

    taps = w_up.astype(F32)
    fold = lambda t: jnp.stack([jnp.stack([t[0], t[1] + t[2]]), jnp.stack([t[0] + t[1], t[2]])])
    by_row = [[taps[0], taps[1] + taps[2]], [taps[0] + taps[1], taps[2]]]
    blocks = []
    for du in range(2):
        for dv in range(2):
            places = []
            for br in range(2):
                for bc in range(2):
                    t = by_row[1 - br][du]
                    pair = [[t[0], t[1] + t[2]], [t[0] + t[1], t[2]]][1 - bc][dv]
                    places.append(jnp.pad(pair, ((0, 0), (0, 64))))
            blocks.append(jnp.concatenate(places, axis=1))
    up_kernel = jnp.stack(blocks).astype(BF16)
    lanes = lambda v: jnp.pad(v[None], ((0, 0), (0, 64)))
    return call(
        fine_kernel,
        (2, 8, 40, CF),
        [
            pltpu.VMEM((2, 160, CM), F32),
            pltpu.VMEM((2, 4, 128, 256), F32),
            pltpu.VMEM((4, 4, 128, 256), F32),
            pltpu.VMEM((2, 56, 128), F32),
            pltpu.VMEM((4, 16, 96, 256), BF16),
            pltpu.VMEM((2, 2, 8, 40, 128), F32),
        ],
        info, second_a, second_b, returned, fine, up_kernel, lanes(b_up), lanes(g_fine),
        w_fine.reshape(27, CF, CF), b_fine[None],
    )


def solution(mesh):
    return jax.shard_map(
        shards,
        mesh=mesh,
        in_specs=(
            P(None, "ha", "wa", None),
            P("segment", None, None, None, None, None),
            P("segment", None),
            P("segment", None),
            P("segment", None, "ha", "wa", None),
            P(),
            P(),
            P(),
            P(None, "ha", "wa", None),
            P(),
            P(),
        ),
        out_specs=P("segment", "ha", "wa", None),
        check_vma=False,
    )
```

time: 143 us -> 87.3 us (0.61)
  the two profiles are of different devices: /device:TPU:65 before, /device:TPU:102 now
where the time goes in v1:
time: 87.3 us; the launch traced here: 86.5 us
  starting transfers between devices  31.2 us (36%)
  local copies, waits for them, and re-layouts  20.1 us (23%)
  Pallas kernels  18 us (21%)
  waiting for transfers between devices  8.36 us (10%)
  other arithmetic  8.26 us (9%)
    pallas_call x5, Pallas kernels, call(): pl.pallas_call(body, out_shape=jax.ShapeDtypeStruct(out_shape, BF16), in_...  18 us
    unnamed x39, local copies, waits for them, and re-layouts  15.9 us
    ppermute x1, waiting for transfers between devices, shards(): lax.ppermute(edge(0, 3), 'wa', [(i + 1, i) for i in range(N_WA - 1)])  8.14 us
    ppermute x2, starting transfers between devices, shards(): after = lax.ppermute(lax.slice_in_dim(fine, 0, 1, axis=dim), axis, down)  6.4 us
    ppermute x1, starting transfers between devices, shards(): lax.ppermute(edge(TILE_COLS - 3, TILE_COLS), 'wa', [(i, i + 1) for i in r...  5.88 us
    ppermute x2, starting transfers between devices, shards(): lax.ppermute(lax.slice_in_dim(fine, length - 1, length, axis=dim), axis, up)  4.12 us
    another operation x5, other arithmetic, shards(): up_kernel = jnp.stack(blocks).astype(BF16)  3.7 us
    ppermute x1, starting transfers between devices, shards(): returned = lax.ppermute(second_a, 'segment', [(1, 0)])  3.4 us
  transfers between devices with their start and end apart: 13, of which 2 were waited for; matrix products, arithmetic and copies ran while one was open for 17% of the time, Pallas kernels for 11%

profile of v1, /device:TPU:102, one launch (start us, length us, event | category | flops | bytes accessed | tf_op | source)
XLA Modules:
  0.0 86.5 jit_solution(25095793543443997)
XLA Ops:
  0.0 1.0 %copy.19.refs_1_ = bf16[4,4,20,384]{3,2,1,0:T(8,128)(2,1)S(1)} copy(bf16[4,4,20,384]{3,1,2,0:T(4,128)(2,1)} %param.11) | data formatting | bytes 491520 | tf_op args[0]
  1.0 0.9 %copy.25 = bf16[1,2,4,20,384]{4,3,2,1,0:T(8,128)(2,1)S(1)} copy(bf16[1,2,4,20,384]{4,2,3,1,0:T(4,128)(2,1)} %param.15) | data formatting | bytes 245760 | tf_op args[4]
  2.0 0.8 pad_maximum_fusion.2
  2.8 2.5 %collective-permute-start = (bf16[6,3,20,384]{3,2,1,0:T(8,128)(2,1)}, bf16[6,3,20,384]{3,2,1,0:T(8,128)(2,1)S(1)}, u32[]{:S(2)}, u32[]{:S(2)}) collective-permute-start(bf16[6,3,20,384]{3,2,1,0:T(8,128)(2,1)} %pad_maximum_fusion.2), channel_id=1, source_target_pairs={{0,112},{16,0},{32,16},{48,32},{64,48},{80,64},{96,80},{112,96},{1... | collective-permute-start | bytes 829448 | tf_op jit(solution)/shard_map/ppermute | solution.py:248
  5.2 1.4 %fusion.45 = (bf16[2,1,40,192]{3,2,1,0:T(8,128)(2,1)}, bf16[2,1,40,192]{3,2,1,0:T(8,128)(2,1)}) fusion(bf16[2,8,40,192]{3,2,1,0:T(8,128)(2,1)} %param.19), kind=kLoop, calls=%fused_computation.82 | loop fusion | bytes 122880 | tf_op jit(solution)/shard_map/slice | solution.py:312
  6.6 1.9 %collective-permute-start.9 = (bf16[2,1,40,192]{3,2,1,0:T(8,128)(2,1)}, bf16[2,1,40,192]{3,2,1,0:T(8,128)(2,1)}, u32[]{:S(2)}, u32[]{:S(2)}) collective-permute-start(bf16[2,1,40,192]{3,2,1,0:T(8,128)(2,1)} %get-tuple-element.28), channel_id=1, source_target_pairs={{0,16},{16,32},{32,48},{48,64},{64,80},{80,96},{96,112},{1,17},{17... | collective-permute-start | bytes 92168 | tf_op jit(solution)/shard_map/ppermute | solution.py:311
  8.5 1.3 %collective-permute-start.10 = (bf16[2,1,40,192]{3,2,1,0:T(8,128)(2,1)}, bf16[2,1,40,192]{3,2,1,0:T(8,128)(2,1)}, u32[]{:S(2)}, u32[]{:S(2)}) collective-permute-start(bf16[2,1,40,192]{3,2,1,0:T(8,128)(2,1)} %get-tuple-element.27), channel_id=1, source_target_pairs={{16,0},{32,16},{48,32},{64,48},{80,64},{96,80},{112,96},{17,1},{33... | collective-permute-start | bytes 92168 | tf_op jit(solution)/shard_map/ppermute | solution.py:312
  9.8 2.5 %copy.23 = bf16[3,3,384,192]{3,2,1,0:T(8,128)(2,1)S(1)} copy(bf16[3,3,384,192]{2,3,1,0:T(8,128)(2,1)} %param.16) | data formatting | bytes 2654208 | tf_op args[5]
  12.4 0.3 convert_element_type.27
  12.7 0.3 slice_add_fusion.1
  13.1 0.9 %fusion.36 = (bf16[384,192]{1,0:T(8,128)(2,1)S(1)}, bf16[384,192]{1,0:T(8,128)(2,1)}, bf16[384,192]{1,0:T(8,128)(2,1)S(1)}, bf16[384,192]{1,0:T(8,128)(2,1)S(1)}) fusion(f32[1,3,384,192]{3,2,1,0:T(8,128)S(1)} %get-tuple-element.13, f32[1,3,384,192]{3,2,1,0:T(8,128)S(1)} %get-tuple-element.14), kind=kLoop, calls=%fused_computation.65 | loop fusion | flops 589824 | bytes 2359296 | tf_op jit(solution)/shard_map/convert.54
  14.0 0.9 %fusion.37 = (bf16[384,192]{1,0:T(8,128)(2,1)S(1)}, bf16[384,192]{1,0:T(8,128)(2,1)}, bf16[384,192]{1,0:T(8,128)(2,1)}, bf16[384,192]{1,0:T(8,128)(2,1)S(1)}) fusion(f32[3,3,384,192]{3,2,1,0:T(8,128)S(1)} %convert_element_type.27), kind=kLoop, calls=%fused_computation.66 | loop fusion | flops 589824 | bytes 2359296 | tf_op jit(solution)/shard_map/convert.50
  15.0 0.8 fusion.29
  15.8 0.1 fusion.13
  15.9 0.8 copy-done.11
  16.7 0.1 copy-done.13
  16.8 1.1 %fusion.17 = bf16[1,384,1024]{2,1,0:T(8,128)(2,1)S(1)} fusion(bf16[384,192]{1,0:T(8,128)(2,1)S(1)} %copy-done.11, bf16[384,192]{1,0:T(8,128)(2,1)S(1)} %copy-done.13, bf16[384,192]{1,0:T(8,128)(2,1)} %get-tuple-element.16, bf16[384,192]{1,0:T(8,128)(2,1)S(1)} %get-tuple-element.18), kind=kLoop, calls=%fused_computation.26 | loop fusion | flops 7864320 | bytes 1376256 | tf_op jit(solution)/shard_map/stack | solution.py:328
  17.9 1.0 %fusion.21 = bf16[1,384,1024]{2,1,0:T(8,128)(2,1)} fusion(bf16[384,192]{1,0:T(8,128)(2,1)S(1)} %get-tuple-element.30, bf16[384,192]{1,0:T(8,128)(2,1)S(1)} %get-tuple-element.32, bf16[384,192]{1,0:T(8,128)(2,1)S(1)} %copy-done.12, bf16[384,192]{1,0:T(8,128)(2,1)S(1)} %copy-done.10), kind=kLoop, calls=%fused_computation.30 | loop fusion | flops 7864320 | bytes 1376256 | tf_op jit(solution)/shard_map/stack | solution.py:328
  19.0 1.0 %fusion.25 = bf16[1,384,1024]{2,1,0:T(8,128)(2,1)} fusion(bf16[384,192]{1,0:T(8,128)(2,1)S(1)} %get-tuple-element.31, bf16[384,192]{1,0:T(8,128)(2,1)S(1)} %get-tuple-element.29, bf16[384,192]{1,0:T(8,128)(2,1)S(1)} %get-tuple-element.8, bf16[384,192]{1,0:T(8,128)(2,1)S(1)} %copy-done.9), kind=kLoop, calls=%fused_computation.34 | loop fusion | flops 7864320 | bytes 1376256 | tf_op jit(solution)/shard_map/stack | solution.py:328
  20.1 0.8 constant_dynamic-update-slice_fusion.2
  20.9 0.1 pad_maximum_fusion.7
  21.0 0.1 reshape.44
  21.1 5.9 %collective-permute-start.1 = (bf16[128,384]{1,0:T(8,128)(2,1)S(1)}, bf16[128,384]{1,0:T(8,128)(2,1)S(1)}, u32[]{:S(2)}, u32[]{:S(2)}) collective-permute-start(bf16[128,384]{1,0:T(8,128)(2,1)S(1)} %pad.79), channel_id=1, source_target_pairs={{0,1},{1,2},{2,3},{3,4},{4,5},{5,6},{6,7},{7,8},{8,9},{9,10},{10,1... | collective-permute-start | bytes 294920 | tf_op jit(solution)/shard_map/ppermute | solution.py:254
  27.0 0.1 reshape.46
  27.1 1.9 %collective-permute-start.2 = (bf16[128,384]{1,0:T(8,128)(2,1)S(1)}, bf16[128,384]{1,0:T(8,128)(2,1)S(1)}, u32[]{:S(2)}, u32[]{:S(2)}) collective-permute-start(bf16[128,384]{1,0:T(8,128)(2,1)S(1)} %pad.80), channel_id=1, source_target_pairs={{1,0},{2,1},{3,2},{4,3},{5,4},{6,5},{7,6},{8,7},{9,8},{10,9},{11,1... | collective-permute-start | bytes 294920 | tf_op jit(solution)/shard_map/ppermute | solution.py:255
  29.1 0.8 constant_dynamic-update-slice_fusion
  29.9 0.2 collective-permute-done.1.refs_4_
  30.0 8.1 %collective-permute-done.2.refs_5_ = bf16[128,384]{1,0:T(8,128)(2,1)S(1)} collective-permute-done((bf16[128,384]{1,0:T(8,128)(2,1)S(1)}, bf16[128,384]{1,0:T(8,128)(2,1)S(1)}, u32[]{:S(2)}, u32[]{:S(2)}) %collective-permute-start.2) | collective-permute-done | bytes 98336 | tf_op jit(solution)/shard_map/ppermute | solution.py:255
  38.2 3.3 %copy-done = bf16[1,3,3,3,384,384]{5,4,3,2,1,0:T(8,128)(2,1)S(1)} copy-done((bf16[1,3,3,3,384,384]{5,4,3,2,1,0:T(8,128)(2,1)S(1)}, bf16[1,3,3,3,384,384]{5,4,3,2,1,0:T(8,128)(2,1)}, u32[]{:S(2)}) %copy-start) | copy-done | bytes 7962648
  41.5 0.5 shard_map.109
  42.0 1.3 %collective-permute-start.4 = (bf16[2,4,24,384]{3,2,1,0:T(8,128)(2,1)S(1)}, bf16[2,4,24,384]{3,2,1,0:T(8,128)(2,1)S(1)}, u32[]{:S(2)}, u32[]{:S(2)}) collective-permute-start(bf16[2,4,24,384]{3,2,1,0:T(8,128)(2,1)S(1)} %shard_map.109), channel_id=1, source_target_pairs={{112,128},{113,129},{114,130},{115,131},{116,132},{117,133},{118,1... | collective-permute-start | bytes 442376 | tf_op jit(solution)/shard_map/ppermute | solution.py:270
  43.3 1.3 %collective-permute-start.5 = (bf16[2,4,24,384]{3,2,1,0:T(8,128)(2,1)S(1)}, bf16[2,4,24,384]{3,2,1,0:T(8,128)(2,1)S(1)}, u32[]{:S(2)}, u32[]{:S(2)}) collective-permute-start(bf16[2,4,24,384]{3,2,1,0:T(8,128)(2,1)S(1)} %shard_map.109), channel_id=1, source_target_pairs={{0,128},{1,129},{2,130},{3,131},{4,132},{5,133},{6,134},{7,135},{8... | collective-permute-start | bytes 442376 | tf_op jit(solution)/shard_map/ppermute | solution.py:270
  44.7 0.6 slice.156
  45.4 0.8 fusion.27.c
  46.2 1.9 %collective-permute-start.3 = (bf16[2,2,24,384]{3,2,1,0:T(8,128)(2,1)S(1)}, bf16[2,2,24,384]{3,2,1,0:T(8,128)(2,1)S(1)}, u32[]{:S(2)}, u32[]{:S(2)}) collective-permute-start(bf16[2,2,24,384]{3,2,1,0:T(8,128)(2,1)S(1)} %slice.159), channel_id=1, source_target_pairs={{128,144},{129,145},{130,146},{131,147},{132,148},{133,149},{134,1... | collective-permute-start | bytes 221192 | tf_op jit(solution)/shard_map/ppermute | solution.py:276
  48.2 2.2 %collective-permute-start.11 = (bf16[2,10,1,192]{3,2,1,0:T(2,128)(2,1)S(1)}, bf16[2,10,1,192]{3,2,1,0:T(2,128)(2,1)S(1)}, u32[]{:S(2)}, u32[]{:S(2)}) collective-permute-start(bf16[2,10,1,192]{3,2,1,0:T(2,128)(2,1)S(1)} %get-tuple-element.25), channel_id=1, source_target_pairs={{0,1},{1,2},{2,3},{3,4},{4,5},{5,6},{6,7},{7,8},{8,9},{9,10},{10,1... | collective-permute-start | bytes 23048 | tf_op jit(solution)/shard_map/ppermute | solution.py:311
  50.4 5.1 %collective-permute-start.12 = (bf16[2,10,1,192]{3,2,1,0:T(2,128)(2,1)S(1)}, bf16[2,10,1,192]{3,2,1,0:T(2,128)(2,1)S(1)}, u32[]{:S(2)}, u32[]{:S(2)}) collective-permute-start(bf16[2,10,1,192]{3,2,1,0:T(2,128)(2,1)S(1)} %get-tuple-element.26), channel_id=1, source_target_pairs={{1,0},{2,1},{3,2},{4,3},{5,4},{6,5},{7,6},{8,7},{9,8},{10,9},{11,1... | collective-permute-start | bytes 23048 | tf_op jit(solution)/shard_map/ppermute | solution.py:312
  55.5 3.3 %copy-done.1 = bf16[1,3,3,3,384,384]{5,4,3,2,1,0:T(8,128)(2,1)S(1)} copy-done((bf16[1,3,3,3,384,384]{5,4,3,2,1,0:T(8,128)(2,1)S(1)}, bf16[1,3,3,3,384,384]{5,4,3,2,1,0:T(8,128)(2,1)}, u32[]{:S(2)}) %copy-start.1) | copy-done | bytes 7962648
  58.8 0.5 shard_map.111
  59.4 1.3 %collective-permute-start.6 = (bf16[2,4,24,384]{3,2,1,0:T(8,128)(2,1)S(1)}, bf16[2,4,24,384]{3,2,1,0:T(8,128)(2,1)S(1)}, u32[]{:S(2)}, u32[]{:S(2)}) collective-permute-start(bf16[2,4,24,384]{3,2,1,0:T(8,128)(2,1)S(1)} %shard_map.111), channel_id=1, source_target_pairs={{112,128},{113,129},{114,130},{115,131},{116,132},{117,133},{118,1... | collective-permute-start | bytes 442376 | tf_op jit(solution)/shard_map/ppermute | solution.py:272
  60.7 1.3 %collective-permute-start.7 = (bf16[2,4,24,384]{3,2,1,0:T(8,128)(2,1)S(1)}, bf16[2,4,24,384]{3,2,1,0:T(8,128)(2,1)S(1)}, u32[]{:S(2)}, u32[]{:S(2)}) collective-permute-start(bf16[2,4,24,384]{3,2,1,0:T(8,128)(2,1)S(1)} %shard_map.111), channel_id=1, source_target_pairs={{0,128},{1,129},{2,130},{3,131},{4,132},{5,133},{6,134},{7,135},{8... | collective-permute-start | bytes 442376 | tf_op jit(solution)/shard_map/ppermute | solution.py:272
  62.0 3.3 %copy-done.2 = bf16[1,3,3,3,384,384]{5,4,3,2,1,0:T(8,128)(2,1)S(1)} copy-done((bf16[1,3,3,3,384,384]{5,4,3,2,1,0:T(8,128)(2,1)S(1)}, bf16[1,3,3,3,384,384]{5,4,3,2,1,0:T(8,128)(2,1)}, u32[]{:S(2)}) %copy-start.2) | copy-done | bytes 7962648
  65.2 4.6 %shard_map.110.lead = bf16[2,144,384]{2,1,0:T(8,128)(2,1)S(1)} custom-call(s32[3]{0:T(128)S(1)} %pad_add_fusion.refs_0_.i.info, bf16[2,6,24,384]{3,2,1,0:T(8,128)(2,1)S(1)} %fusion.27.c, bf16[2,2,24,384]{3,2,1,0:T(8,128)(2,1)S(1)} %collective-permute-done.3.ab, bf16[2,4,24,384]{3,2,1,0:T(8,128)(2,1)S(1)} %collective-permute-done.4.ta, ...), custom_call_target="tpu_custom_call" | custom-call | tf_op jit(solution)/shard_map/pallas_call | solution.py:222
  69.9 3.4 %collective-permute-start.8 = (bf16[2,144,384]{2,1,0:T(8,128)(2,1)S(1)}, bf16[2,144,384]{2,1,0:T(8,128)(2,1)S(1)}, u32[]{:S(2)}, u32[]{:S(2)}) collective-permute-start(bf16[2,144,384]{2,1,0:T(8,128)(2,1)S(1)} %shard_map.110.lead), channel_id=1, source_target_pairs={{128,0},{129,1},{130,2},{131,3},{132,4},{133,5},{134,6},{135,7},{1... | collective-permute-start | bytes 663560 | tf_op jit(solution)/shard_map/ppermute | solution.py:298
  73.3 0.4 pad_maximum_fusion.w_up
  73.9 0.3 pad_maximum_fusion.1.cache
  74.2 4.7 %shard_map.112.main = bf16[2,144,384]{2,1,0:T(8,128)(2,1)S(1)} custom-call(s32[3]{0:T(128)S(1)} %pad_add_fusion.refs_0_.i.info, bf16[2,4,24,384]{3,2,1,0:T(8,128)(2,1)S(1)} %collective-permute-done.4.ta, bf16[2,4,24,384]{3,2,1,0:T(8,128)(2,1)S(1)} %collective-permute-done.5.la, bf16[2,4,24,384]{3,2,1,0:T(8,128)(2,1)S(1)} %collective-permute-done.6.tb, ...), custom_call_target="tpu_custom_call" | custom-call | tf_op jit(solution)/shard_map/pallas_call | solution.py:222
  78.9 7.6 %shard_map.113 = bf16[2,8,40,192]{3,2,1,0:T(8,128)(2,1)} custom-call(s32[3]{0:T(128)S(1)} %pad_add_fusion.refs_0_.i.info, bf16[2,144,384]{2,1,0:T(8,128)(2,1)S(1)} %shard_map.110.lead, bf16[2,144,384]{2,1,0:T(8,128)(2,1)S(1)} %shard_map.112.main, bf16[2,144,384]{2,1,0:T(8,128)(2,1)S(1)} %collective-permute-done.8.returned, ...), custom_call_target="tpu_custom_call" | custom-call | tf_op jit(solution)/shard_map/pallas_call | solution.py:222
  (54 shorter events, 0.5 us)
Async XLA Ops:
  2.8 18.1 %collective-permute-start = (bf16[6,3,20,384]{3,2,1,0:T(8,128)(2,1)}, bf16[6,3,20,384]{3,2,1,0:T(8,128)(2,1)S(1)}, u32[]{:S(2)}, u32[]{:S(2)}) collective-permute-start(bf16[6,3,20,384]{3,2,1,0:T(8,128)(2,1)} %pad_maximum_fusion.2), channel_id=1, source_target_pairs={{0,112},{16,0},{32,16},{48,32},{64,48},{80,64},{96,80},{112,96},{1... | collective-permute-start | bytes 829448 | tf_op jit(solution)/shard_map/ppermute | solution.py:248
  6.6 13.4 %collective-permute-start.9 = (bf16[2,1,40,192]{3,2,1,0:T(8,128)(2,1)}, bf16[2,1,40,192]{3,2,1,0:T(8,128)(2,1)}, u32[]{:S(2)}, u32[]{:S(2)}) collective-permute-start(bf16[2,1,40,192]{3,2,1,0:T(8,128)(2,1)} %get-tuple-element.28), channel_id=1, source_target_pairs={{0,16},{16,32},{32,48},{48,64},{64,80},{80,96},{96,112},{1,17},{17... | collective-permute-start | bytes 92168 | tf_op jit(solution)/shard_map/ppermute | solution.py:311
  8.5 20.5 %collective-permute-start.10 = (bf16[2,1,40,192]{3,2,1,0:T(8,128)(2,1)}, bf16[2,1,40,192]{3,2,1,0:T(8,128)(2,1)}, u32[]{:S(2)}, u32[]{:S(2)}) collective-permute-start(bf16[2,1,40,192]{3,2,1,0:T(8,128)(2,1)} %get-tuple-element.27), channel_id=1, source_target_pairs={{16,0},{32,16},{48,32},{64,48},{80,64},{96,80},{112,96},{17,1},{33... | collective-permute-start | bytes 92168 | tf_op jit(solution)/shard_map/ppermute | solution.py:312
  15.8 0.9 %copy-start.11 = (bf16[384,192]{1,0:T(8,128)(2,1)S(1)}, bf16[384,192]{1,0:T(8,128)(2,1)}, u32[]{:S(2)}) copy-start(bf16[384,192]{1,0:T(8,128)(2,1)} %get-tuple-element.7) | copy-start | bytes 442372
  15.8 1.0 %copy-start.13 = (bf16[384,192]{1,0:T(8,128)(2,1)S(1)}, bf16[384,192]{1,0:T(8,128)(2,1)}, u32[]{:S(2)}) copy-start(bf16[384,192]{1,0:T(8,128)(2,1)} %get-tuple-element.10) | copy-start | bytes 442372
  15.8 2.1 %copy-start.10 = (bf16[384,192]{1,0:T(8,128)(2,1)S(1)}, bf16[384,192]{1,0:T(8,128)(2,1)}, u32[]{:S(2)}) copy-start(bf16[384,192]{1,0:T(8,128)(2,1)} %get-tuple-element.6) | copy-start | bytes 442372
  15.8 2.1 %copy-start.12 = (bf16[384,192]{1,0:T(8,128)(2,1)S(1)}, bf16[384,192]{1,0:T(8,128)(2,1)}, u32[]{:S(2)}) copy-start(bf16[384,192]{1,0:T(8,128)(2,1)} %get-tuple-element.12) | copy-start | bytes 442372
  16.8 2.1 %copy-start.9 = (bf16[384,192]{1,0:T(8,128)(2,1)S(1)}, bf16[384,192]{1,0:T(8,128)(2,1)}, u32[]{:S(2)}) copy-start(bf16[384,192]{1,0:T(8,128)(2,1)} %get-tuple-element.11) | copy-start | bytes 442372
  17.9 2.9 %copy-start.14 = (bf16[2,8,40,192]{3,2,1,0:T(8,128)(2,1)S(1)}, bf16[2,8,40,192]{3,2,1,0:T(8,128)(2,1)}, u32[]{:S(2)}) copy-start(bf16[2,8,40,192]{3,2,1,0:T(8,128)(2,1)} %param.19) | copy-start | bytes 737284
  20.0 18.2 %copy-start.4 = (f32[1,384]{1,0:T(1,128)S(1)}, f32[1,384]{1,0:T(1,128)}, u32[]{:S(2)}) copy-start(f32[1,384]{1,0:T(1,128)} %refs_1_.5) | copy-start | bytes 4612
  20.0 18.2 %copy-start.5 = (f32[1,384]{1,0:T(1,128)S(1)}, f32[1,384]{1,0:T(1,128)}, u32[]{:S(2)}) copy-start(f32[1,384]{1,0:T(1,128)} %refs_2_.3) | copy-start | bytes 4612
  21.1 8.9 %collective-permute-start.1 = (bf16[128,384]{1,0:T(8,128)(2,1)S(1)}, bf16[128,384]{1,0:T(8,128)(2,1)S(1)}, u32[]{:S(2)}, u32[]{:S(2)}) collective-permute-start(bf16[128,384]{1,0:T(8,128)(2,1)S(1)} %pad.79), channel_id=1, source_target_pairs={{0,1},{1,2},{2,3},{3,4},{4,5},{5,6},{6,7},{7,8},{8,9},{9,10},{10,1... | collective-permute-start | bytes 294920 | tf_op jit(solution)/shard_map/ppermute | solution.py:254
  27.1 11.1 %collective-permute-start.2 = (bf16[128,384]{1,0:T(8,128)(2,1)S(1)}, bf16[128,384]{1,0:T(8,128)(2,1)S(1)}, u32[]{:S(2)}, u32[]{:S(2)}) collective-permute-start(bf16[128,384]{1,0:T(8,128)(2,1)S(1)} %pad.80), channel_id=1, source_target_pairs={{1,0},{2,1},{3,2},{4,3},{5,4},{6,5},{7,6},{8,7},{9,8},{10,9},{11,1... | collective-permute-start | bytes 294920 | tf_op jit(solution)/shard_map/ppermute | solution.py:255
  38.2 3.3 %copy-start = (bf16[1,3,3,3,384,384]{5,4,3,2,1,0:T(8,128)(2,1)S(1)}, bf16[1,3,3,3,384,384]{5,4,3,2,1,0:T(8,128)(2,1)}, u32[]{:S(2)}) copy-start(bf16[1,3,3,3,384,384]{5,4,3,2,1,0:T(8,128)(2,1)} %param.12) | copy-start | bytes 23887876
  42.0 18.7 %collective-permute-start.4 = (bf16[2,4,24,384]{3,2,1,0:T(8,128)(2,1)S(1)}, bf16[2,4,24,384]{3,2,1,0:T(8,128)(2,1)S(1)}, u32[]{:S(2)}, u32[]{:S(2)}) collective-permute-start(bf16[2,4,24,384]{3,2,1,0:T(8,128)(2,1)S(1)} %shard_map.109), channel_id=1, source_target_pairs={{112,128},{113,129},{114,130},{115,131},{116,132},{117,133},{118,1... | collective-permute-start | bytes 442376 | tf_op jit(solution)/shard_map/ppermute | solution.py:270
  43.3 18.7 %collective-permute-start.5 = (bf16[2,4,24,384]{3,2,1,0:T(8,128)(2,1)S(1)}, bf16[2,4,24,384]{3,2,1,0:T(8,128)(2,1)S(1)}, u32[]{:S(2)}, u32[]{:S(2)}) collective-permute-start(bf16[2,4,24,384]{3,2,1,0:T(8,128)(2,1)S(1)} %shard_map.109), channel_id=1, source_target_pairs={{0,128},{1,129},{2,130},{3,131},{4,132},{5,133},{6,134},{7,135},{8... | collective-permute-start | bytes 442376 | tf_op jit(solution)/shard_map/ppermute | solution.py:270
  46.2 13.1 %collective-permute-start.3 = (bf16[2,2,24,384]{3,2,1,0:T(8,128)(2,1)S(1)}, bf16[2,2,24,384]{3,2,1,0:T(8,128)(2,1)S(1)}, u32[]{:S(2)}, u32[]{:S(2)}) collective-permute-start(bf16[2,2,24,384]{3,2,1,0:T(8,128)(2,1)S(1)} %slice.159), channel_id=1, source_target_pairs={{128,144},{129,145},{130,146},{131,147},{132,148},{133,149},{134,1... | collective-permute-start | bytes 221192 | tf_op jit(solution)/shard_map/ppermute | solution.py:276
  48.2 25.7 %collective-permute-start.11 = (bf16[2,10,1,192]{3,2,1,0:T(2,128)(2,1)S(1)}, bf16[2,10,1,192]{3,2,1,0:T(2,128)(2,1)S(1)}, u32[]{:S(2)}, u32[]{:S(2)}) collective-permute-start(bf16[2,10,1,192]{3,2,1,0:T(2,128)(2,1)S(1)} %get-tuple-element.25), channel_id=1, source_target_pairs={{0,1},{1,2},{2,3},{3,4},{4,5},{5,6},{6,7},{7,8},{8,9},{9,10},{10,1... | collective-permute-start | bytes 23048 | tf_op jit(solution)/shard_map/ppermute | solution.py:311
  50.4 23.5 %collective-permute-start.12 = (bf16[2,10,1,192]{3,2,1,0:T(2,128)(2,1)S(1)}, bf16[2,10,1,192]{3,2,1,0:T(2,128)(2,1)S(1)}, u32[]{:S(2)}, u32[]{:S(2)}) collective-permute-start(bf16[2,10,1,192]{3,2,1,0:T(2,128)(2,1)S(1)} %get-tuple-element.26), channel_id=1, source_target_pairs={{1,0},{2,1},{3,2},{4,3},{5,4},{6,5},{7,6},{8,7},{9,8},{10,9},{11,1... | collective-permute-start | bytes 23048 | tf_op jit(solution)/shard_map/ppermute | solution.py:312
  55.5 3.3 %copy-start.1 = (bf16[1,3,3,3,384,384]{5,4,3,2,1,0:T(8,128)(2,1)S(1)}, bf16[1,3,3,3,384,384]{5,4,3,2,1,0:T(8,128)(2,1)}, u32[]{:S(2)}) copy-start(bf16[1,3,3,3,384,384]{5,4,3,2,1,0:T(8,128)(2,1)} %param.12) | copy-start | bytes 23887876
  58.8 14.5 %copy-start.7 = (bf16[1,384,1024]{2,1,0:T(8,128)(2,1)S(1)}, bf16[1,384,1024]{2,1,0:T(8,128)(2,1)}, u32[]{:S(2)}) copy-start(bf16[1,384,1024]{2,1,0:T(8,128)(2,1)} %fusion.21) | copy-start | bytes 2359300
  58.8 14.5 %copy-start.8 = (bf16[1,384,1024]{2,1,0:T(8,128)(2,1)S(1)}, bf16[1,384,1024]{2,1,0:T(8,128)(2,1)}, u32[]{:S(2)}) copy-start(bf16[1,384,1024]{2,1,0:T(8,128)(2,1)} %fusion.25) | copy-start | bytes 2359300
  59.4 14.8 %collective-permute-start.6 = (bf16[2,4,24,384]{3,2,1,0:T(8,128)(2,1)S(1)}, bf16[2,4,24,384]{3,2,1,0:T(8,128)(2,1)S(1)}, u32[]{:S(2)}, u32[]{:S(2)}) collective-permute-start(bf16[2,4,24,384]{3,2,1,0:T(8,128)(2,1)S(1)} %shard_map.111), channel_id=1, source_target_pairs={{112,128},{113,129},{114,130},{115,131},{116,132},{117,133},{118,1... | collective-permute-start | bytes 442376 | tf_op jit(solution)/shard_map/ppermute | solution.py:272
  60.7 13.5 %collective-permute-start.7 = (bf16[2,4,24,384]{3,2,1,0:T(8,128)(2,1)S(1)}, bf16[2,4,24,384]{3,2,1,0:T(8,128)(2,1)S(1)}, u32[]{:S(2)}, u32[]{:S(2)}) collective-permute-start(bf16[2,4,24,384]{3,2,1,0:T(8,128)(2,1)S(1)} %shard_map.111), channel_id=1, source_target_pairs={{0,128},{1,129},{2,130},{3,131},{4,132},{5,133},{6,134},{7,135},{8... | collective-permute-start | bytes 442376 | tf_op jit(solution)/shard_map/ppermute | solution.py:272
  62.0 3.3 %copy-start.2 = (bf16[1,3,3,3,384,384]{5,4,3,2,1,0:T(8,128)(2,1)S(1)}, bf16[1,3,3,3,384,384]{5,4,3,2,1,0:T(8,128)(2,1)}, u32[]{:S(2)}) copy-start(bf16[1,3,3,3,384,384]{5,4,3,2,1,0:T(8,128)(2,1)} %param.12) | copy-start | bytes 23887876
  69.9 3.9 %copy-start.15 = (f32[192]{0:T(256)S(1)}, f32[192]{0:T(256)}, u32[]{:S(2)}) copy-start(f32[192]{0:T(256)} %param.17) | copy-start | bytes 2308
  69.9 3.9 %copy-start.16 = (f32[192]{0:T(256)S(1)}, f32[192]{0:T(256)}, u32[]{:S(2)}) copy-start(f32[192]{0:T(256)} %param.18) | copy-start | bytes 2308
  69.9 9.0 %collective-permute-start.8 = (bf16[2,144,384]{2,1,0:T(8,128)(2,1)S(1)}, bf16[2,144,384]{2,1,0:T(8,128)(2,1)S(1)}, u32[]{:S(2)}, u32[]{:S(2)}) collective-permute-start(bf16[2,144,384]{2,1,0:T(8,128)(2,1)S(1)} %shard_map.110.lead), channel_id=1, source_target_pairs={{128,0},{129,1},{130,2},{131,3},{132,4},{133,5},{134,6},{135,7},{1... | collective-permute-start | bytes 663560 | tf_op jit(solution)/shard_map/ppermute | solution.py:298
  74.1 4.8 %copy-start.6 = (f32[192]{0:T(256)S(1)}, f32[192]{0:T(256)}, u32[]{:S(2)}) copy-start(f32[192]{0:T(256)} %param.21) | copy-start | bytes 2308
  74.2 4.7 %copy-start.3 = (bf16[3,3,3,192,192]{4,3,2,1,0:T(8,128)(2,1)S(1)}, bf16[3,3,3,192,192]{4,3,2,1,0:T(8,128)(2,1)}, u32[]{:S(2)}) copy-start(bf16[3,3,3,192,192]{4,3,2,1,0:T(8,128)(2,1)} %param.20) | copy-start | bytes 5971972

commit v2 on v0

v2 whole, which is shorter than its diff:
```python
import jax
import jax.numpy as jnp
from jax import lax
from jax.experimental import pallas as pl
from jax.experimental.pallas import tpu as pltpu
from jax.sharding import PartitionSpec as P

F32 = jnp.float32
BF16 = jnp.bfloat16
CM = 384
CF = 192
AXES = ("segment", "ha", "wa")
N_HA = 8
N_WA = 16
GRID_ROWS = 32
GRID_COLS = 320
ROWS = 4
COLS = 20
PITCH = 24
WIDE = 26
HALF = 56
RING = 2 * 6 * PITCH


def normed(values, gain_vec, channels):
    inv_rms = lax.rsqrt(jnp.sum(values * values, axis=-1, keepdims=True) * (1.0 / channels) + 1e-06)
    scaled = values * inv_rms * gain_vec
    return scaled / (1.0 + jnp.exp(-scaled))


def conv_frames(patches, w, length):
    total = None
    for a in range(3):
        for pq in range(9):
            lhs = patches[a : a + 2, pq].reshape(2 * length, CM)
            part = jnp.dot(lhs, w[a * 9 + pq], preferred_element_type=F32)
            total = part if total is None else total + part
    return total


def frame_pair(first, second):
    return jnp.concatenate([first.astype(F32), second.astype(F32)], axis=1)


def pack_rows(info, latent, cache, fine, to_above, to_below, side):
    def put(at, line):
        side[at : at + line.shape[0]] = line.astype(F32)

    for f in range(2):
        for row in range(3):
            put(((4 + f) * 3 + row) * COLS, cache[f, row])

    @pl.when(info[0] == 0)
    def _():
        for f in range(4):
            for row in range(3):
                put((f * 3 + row) * COLS, latent[f, row])
        to_above[...] = side[...].astype(BF16)

    @pl.when(info[0] == 1)
    def _():
        put(0, frame_pair(fine[0, 0], fine[1, 0]))
        to_above[...] = side[...].astype(BF16)
        for f in range(2):
            for row in range(2):
                put((f * 2 + row) * COLS, cache[f, 2 + row])
        put(80, frame_pair(fine[0, 7], fine[1, 7]))
        to_below[...] = side[0:128].astype(BF16)


def pack_columns(info, latent, cache, fine, below, above, _, left_0, right_0, left_1, right_1, far, side):
    far[0] = below[...].astype(F32)

    @pl.when(info[0] == 0)
    def _():
        for f in range(6):
            for row in range(1, 7):
                if row < ROWS:
                    line = (latent[f, row] if f < 4 else cache[f - 4, row]).astype(F32)
                    first, final = line[:3], line[17:20]
                else:
                    base = (f * 3 + row - ROWS) * COLS
                    first, final = far[0, base : base + 3], far[0, base + 17 : base + 20]
                at = (f * 6 + row - 1) * 3
                side[0, at : at + 3] = first
                side[1, at : at + 3] = final
        left_0[...] = side[0].astype(BF16)
        right_0[...] = side[1].astype(BF16)

    @pl.when(info[0] == 1)
    def _():
        far[1, 0:128] = above[...].astype(F32)
        for t in range(2):
            for u in range(8):
                if 2 <= u < 6:
                    line = cache[t, u - 2].astype(F32)
                    first, final = line[:2], line[18:20]
                else:
                    k, base = (1, (t * 2 + u) * COLS) if u < 2 else (0, ((4 + t) * 3 + u - 6) * COLS)
                    first, final = far[k, base : base + 2], far[k, base + 18 : base + 20]
                at = (t * 8 + u) * 2
                side[0, at : at + 2] = first
                side[1, at : at + 2] = final
        for e in range(10):
            if 1 <= e <= 8:
                line = frame_pair(fine[0, e - 1], fine[1, e - 1])
                first, final = line[0:1], line[39:40]
            else:
                k, base = (1, 80) if e == 0 else (0, 0)
                first, final = far[k, base : base + 1], far[k, base + 39 : base + 40]
            side[0, 32 + e : 33 + e] = first
            side[1, 32 + e : 33 + e] = final
        left_1[...] = side[0, 0:48].astype(BF16)
        right_1[...] = side[1, 0:48].astype(BF16)


def fold_weights(w_up_hbm, w_up, sem, out):
    copy = pltpu.make_async_copy(w_up_hbm, w_up, sem)
    copy.start()
    copy.wait()
    zeros = jnp.zeros((CM, 64), F32)
    taps = [jnp.transpose(w_up[k].astype(F32)) for k in range(9)]
    for br in range(2):
        for bc in range(2):
            place = br * 2 + bc
            for du in range(2):
                ps = ((0, 1), (2,))[du] if br == 0 else ((0,), (1, 2))[du]
                for dv in range(2):
                    qs = ((0, 1), (2,))[dv] if bc == 0 else ((0,), (1, 2))[dv]
                    total = None
                    for p in ps:
                        for q in qs:
                            part = taps[p * 3 + q]
                            total = part if total is None else total + part
                    both = jnp.concatenate([total, zeros], axis=1).astype(BF16)
                    out[du * 2 + dv, :, place * 256 : place * 256 + 256] = both


def first_section(group, info, latent, cache, below, left, right, w, b, g, out, raw, act, side, far, patches):
    last = info[1] == N_HA - 1
    side[0] = left[...].astype(F32)
    side[1] = right[...].astype(F32)
    far[...] = below[...].astype(F32)
    slots = [(1, False), (2, False), (3, False), (4, True), (3, True), (4, False), (5, False), (6, False)]
    for f in range(4):
        lead = group == 0 and f < 2
        frame = f if group == 1 else (4 + f if lead else f - 2)
        for slot, (row, hide) in enumerate(slots):
            if row >= ROWS:
                base = (frame * 3 + row - ROWS) * COLS
                line = far[base : base + COLS]
            else:
                line = (latent[frame, row] if frame < 4 else cache[frame - 4, row]).astype(F32)
            at = (frame * 6 + row - 1) * 3
            before = side[0, at : at + 3]
            after = side[1, at : at + 3]
            if hide:
                line, before, after = (jnp.where(last, 0.0, v) for v in (line, before, after))
            base = slot * WIDE
            raw[f, base : base + 3] = before
            raw[f, base + 3 : base + 3 + COLS] = line
            raw[f, base + 3 + COLS : base + WIDE] = after
        raw[f, 8 * WIDE : 216] = jnp.zeros((8, CM), F32)
        for lo in range(0, 216, 72):
            part = raw[f, lo : lo + 72]
            act[f, lo : lo + 72] = part if lead else normed(part, g[...], CM)
        for p in range(3):
            for q in range(3):
                top = p * WIDE + q
                low = top + 4 * WIDE
                both = jnp.concatenate([act[f, top : top + HALF], act[f, low : low + HALF]], axis=0)
                patches[f, p * 3 + q] = both.astype(BF16)
    total = conv_frames(patches, w, 2 * HALF) + b[...]
    cols = lax.broadcasted_iota(jnp.int32, (PITCH, 1), 0) + (info[2] * COLS - 2)
    inside = (cols >= 0) & (cols < GRID_COLS)
    act[0, 0 : 2 * HALF] = total[: 2 * HALF]
    act[1, 0 : 2 * HALF] = total[2 * HALF :]
    for t in range(2):
        for r in range(4):
            src = (r // 2) * HALF + (r % 2) * WIDE
            res = ((r // 2) * 4 + r % 2 + 1) * WIDE + 1
            value = act[t, src : src + PITCH] + raw[2 + t, res : res + PITCH]
            out[t, r] = jnp.where(inside, value, 0.0).astype(BF16)


def first_early(info, latent, cache, below, left, right, w, b, g, out, *scratch):
    @pl.when(info[0] == 0)
    def _():
        first_section(0, info, latent, cache, below, left, right, w, b, g, out, *scratch)


def first_late(info, latent, below, left, right, w, b, g, w_up_hbm, out, folded, *scratch):
    *scratch, w_up, sems = scratch

    @pl.when(info[0] == 0)
    def _():
        first_section(1, info, latent, None, below, left, right, w, b, g, out, *scratch)

    @pl.when(info[0] == 1)
    def _():
        fold_weights(w_up_hbm, w_up, sems.at[0], folded)


def second_section(info, caches, earlier, later, w, b, g, out, raw, act, side, far, patches):
    first, last = info[1] == 0, info[1] == N_HA - 1
    if caches is not None:
        cache, below, above, left, right = caches
        side[0, 0:48] = left[...].astype(F32)
        side[1, 0:48] = right[...].astype(F32)
        far[0] = below[...].astype(F32)
        far[1, 0:128] = above[...].astype(F32)
    for f in range(4):
        lead = caches is not None and f < 2
        t = f % 2
        for u in range(8):
            base = u * PITCH
            hide = first if u < 2 else (last if u > 5 else None)
            if lead:
                if 2 <= u < 6:
                    line = cache[t, u - 2].astype(F32)
                else:
                    k, at = (1, (t * 2 + u) * COLS) if u < 2 else (0, ((4 + t) * 3 + u - 6) * COLS)
                    line = far[k, at : at + COLS]
                at = (t * 8 + u) * 2
                before = side[0, at : at + 2]
                after = side[1, at : at + 2]
                if hide is not None:
                    line, before, after = (jnp.where(hide, 0.0, v) for v in (line, before, after))
                raw[f, base : base + 2] = before
                raw[f, base + 2 : base + 22] = line
                raw[f, base + 22 : base + 24] = after
            else:
                low, top = earlier if caches is not None or f < 2 else later
                line = (top[t, u] if u < 4 else low[t, u - 4]).astype(F32)
                raw[f, base : base + PITCH] = line if hide is None else jnp.where(hide, 0.0, line)
        raw[f, 8 * PITCH : 200] = jnp.zeros((8, CM), F32)
        for lo, hi in ((0, 96), (96, 200)):
            part = raw[f, lo:hi]
            act[f, lo:hi] = part if lead else normed(part, g[...], CM)
        for p in range(3):
            for q in range(3):
                at = p * PITCH + q
                patches[f, p * 3 + q] = act[f, at : at + 144].astype(BF16)
    total = conv_frames(patches, w, 144) + b[...]
    cell = lax.broadcasted_iota(jnp.int32, (PITCH, 1), 0)
    cols = cell + (info[2] * COLS - 1)
    inside = (cols >= 0) & (cols < GRID_COLS) & (cell < 22)
    for t in range(2):
        for i in range(6):
            row_at = info[1] * ROWS - 1 + i
            fits = inside & (row_at >= 0) & (row_at < GRID_ROWS)
            res = (i + 1) * PITCH + 1
            at = t * 144 + i * PITCH
            value = total[at : at + PITCH] + raw[2 + t, res : res + PITCH]
            out[at : at + PITCH] = jnp.where(fits, value, 0.0).astype(BF16)


def second_early(info, cache, below, above, left, right, low, top, w, b, g, w_up_hbm, out, folded, *scratch):
    *scratch, ring, w_up, sems = scratch

    @pl.when(info[0] == 1)
    def _():
        second_section(info, (cache, below, above, left, right), (low, top), None, w, b, g, out, *scratch)
        first, last = info[1] == 0, info[1] == N_HA - 1
        side, far = scratch[2:4]
        ring[...] = jnp.zeros((112, CM), F32)
        for at, e, line, hide in ((0, 0, far[1, 80:120], first), (48, 9, far[0, 0:40], last)):
            ring[at : at + 1] = jnp.where(hide, 0.0, side[0, 32 + e : 33 + e])
            ring[at + 1 : at + 41] = jnp.where(hide, 0.0, line)
            ring[at + 41 : at + 42] = jnp.where(hide, 0.0, side[1, 32 + e : 33 + e])
        ring[96:104] = side[0, 33:41]
        ring[104:112] = side[1, 33:41]
        out[RING : RING + 112] = ring[...].astype(BF16)

    @pl.when(info[0] == 0)
    def _():
        fold_weights(w_up_hbm, w_up, sems.at[0], folded)


def second_late(info, low_a, top_a, low_b, top_b, w, b, g, out, *scratch):
    @pl.when(info[0] == 1)
    def _():
        second_section(info, None, (low_a, top_a), (low_b, top_b), w, b, g, out, *scratch)


def last_section(info, lead, main, returned, cache, folded_0, folded_1, b_up, g, w_hbm, b,
                 out, coarse, ups, act, rows, ring, patches, wide, w, sems):
    copy = pltpu.make_async_copy(w_hbm, w, sems.at[0])
    copy.start()
    lanes = lambda ref: jnp.concatenate([ref[...], jnp.zeros((1, 64), F32)], axis=1)
    bias, gain = lanes(b_up), lanes(g)

    def upsample(src, w_up, slot, keep):
        for t in range(2):
            coarse[t, 0:144] = src[t * 144 : t * 144 + 144].astype(F32)
            coarse[t, 144:160] = jnp.zeros((16, CM), F32)
        lhs = [
            jnp.concatenate([coarse[t, du * PITCH + dv : du * PITCH + dv + 128].astype(BF16) for t in range(2)], axis=0)
            for du in range(2)
            for dv in range(2)
        ]
        cell = lax.broadcasted_iota(jnp.int32, (128, 1), 0)
        col = lax.rem(cell, PITCH)
        for phase in range(4):
            br, bc = phase // 2, phase % 2
            total = None
            for k in range(4):
                part = jnp.dot(lhs[k], w_up[k, :, phase * 256 : phase * 256 + 256], preferred_element_type=F32)
                total = part if total is None else total + part
            value = (total + bias).astype(BF16).astype(F32)
            if br == 0:
                outside = (cell < PITCH) & (info[1] == 0)
            else:
                outside = (cell >= 4 * PITCH) & (info[1] == N_HA - 1)
            if bc == 0:
                outside |= (col == 0) & (info[2] == 0)
            else:
                outside |= (col == COLS) & (info[2] == N_WA - 1)
            unit = normed(value, gain, CF)
            for t in range(2):
                if keep:
                    ups[t, phase] = value[t * 128 : t * 128 + 128]
                act[slot + t, phase] = jnp.where(outside, 0.0, unit[t * 128 : t * 128 + 128])

    @pl.when(info[0] == 0)
    def _():
        ring[...] = returned[RING : RING + 112].astype(F32)
        for t in range(2):
            part = slice(t * CF, t * CF + CF)
            for e in range(10):
                if e == 0 or e == 9:
                    at = 0 if e == 0 else 48
                    line = ring[at : at + 48][:, part]
                    rows[0, 0:48] = line[:, :128]
                    rows[1, 0:48, 0:64] = line[:, 128:]
                else:
                    line = cache[t, e - 1].astype(F32)
                    rows[0, 1:41] = line[:, :128]
                    rows[1, 1:41, 0:64] = line[:, 128:]
                    for at, col in ((95 + e, 0), (103 + e, 41)):
                        end = ring[at : at + 1][:, part]
                        rows[0, col : col + 1] = end[:, :128]
                        rows[1, col : col + 1, 0:64] = end[:, 128:]
                br, u = e % 2, e // 2
                for bc in range(2):
                    for c in range(2):
                        act[t, br * 2 + bc, u * PITCH : (u + 1) * PITCH, c * 128 : c * 128 + 128] = rows[
                            c, pl.ds(bc, PITCH, 2), :
                        ]
        upsample(returned, folded_0, 2, True)

    @pl.when(info[0] == 1)
    def _():
        upsample(lead, folded_1, 0, False)
        upsample(main, folded_1, 2, True)

    for f in range(4):
        for plane in range(4):
            for s in range(4):
                at = (s // 2) * PITCH + s % 2
                patches[f, plane * 4 + s] = act[f, plane, at : at + 96].astype(BF16)
    copy.wait()
    for yb in range(2):
        for xb in range(2):
            total = None
            for a in range(3):
                for p in range(3):
                    for q in range(3):
                        plane = ((yb + p) % 2) * 2 + (xb + q) % 2
                        block = plane * 4 + ((yb + p) // 2) * 2 + (xb + q) // 2
                        lhs = patches[a : a + 2, block].reshape(192, 256)[:, :CF]
                        part = jnp.dot(lhs, w[a * 9 + p * 3 + q], preferred_element_type=F32)
                        total = part if total is None else total + part
            total = total + b[...]
            plane = ((yb + 1) % 2) * 2 + (xb + 1) % 2
            at = ((yb + 1) // 2) * PITCH + (xb + 1) // 2
            for t in range(2):
                value = total[t * 96 : t * 96 + 96] + ups[t, plane, at : at + 96][:, :CF]
                for y in range(4):
                    line = value[y * PITCH : y * PITCH + COLS]
                    wide[0, t, 2 * y + yb, pl.ds(xb, COLS, 2), :] = line[:, :128]
                    wide[1, t, 2 * y + yb, pl.ds(xb, COLS, 2), :] = jnp.concatenate(
                        [line[:, 128:], line[:, 128:]], axis=1
                    )
    for t in range(2):
        for y in range(8):
            out[t, y, :, :128] = wide[0, t, y].astype(BF16)
            out[t, y, :, 128:] = wide[1, t, y][:, :64].astype(BF16)


VMEM = pl.BlockSpec(memory_space=pltpu.VMEM)
SMEM = pl.BlockSpec(memory_space=pltpu.SMEM)
HBM = pl.BlockSpec(memory_space=pltpu.HBM)


def call(body, specs, outs, scratch, *operands, flops=0, megabytes=20):
    kinds = {"s": SMEM, "v": VMEM, "h": HBM}
    return pl.pallas_call(
        body,
        out_shape=[jax.ShapeDtypeStruct(shape, BF16) for shape in outs],
        in_specs=[kinds[c] for c in specs],
        out_specs=[VMEM] * len(outs),
        scratch_shapes=scratch,
        compiler_params=pltpu.CompilerParams(vmem_limit_bytes=megabytes * 2**20),
        cost_estimate=pl.CostEstimate(flops=flops, bytes_accessed=2**20, transcendentals=0),
    )(*operands)


def device_at(s, h, w):
    return (s * N_HA + h) * N_WA + w


def pairs_between(src_seg, dst_seg, dh, dw, wrap=False):
    pairs = []
    for h in range(N_HA):
        for w in range(N_WA):
            if (wrap or 0 <= h - dh < N_HA) and 0 <= w - dw < N_WA:
                pairs.append((device_at(src_seg, (h - dh) % N_HA, w - dw), device_at(dst_seg, h, w)))
    return pairs


def shards(latent, w_mid, b_mid, g_mid, cache_mid, w_up, b_up, g_fine, cache_fine, w_fine, b_fine):
    info = jnp.stack([lax.axis_index(axis) for axis in AXES]).astype(jnp.int32)
    kernel = w_mid.reshape(27, CM, CM)
    up_kernel = jnp.swapaxes(w_up, 2, 3).reshape(9, CF, CM)
    dma = pltpu.SemaphoreType.DMA

    cache = cache_mid[0]
    side = pltpu.VMEM((2, 112, CM), F32)
    far = lambda count: pltpu.VMEM((count, 368, CM) if count > 1 else (368, CM), F32)
    to_above, to_below = call(
        pack_rows, "svvv", [(368, CM), (128, CM)], [far(1)], info, latent, cache, cache_fine, megabytes=3
    )
    below = lax.ppermute(to_above, "ha", [(i, (i - 1) % N_HA) for i in range(N_HA)])
    above = lax.ppermute(to_below, AXES, pairs_between(1, 1, 1, 0))
    sides = call(
        pack_columns, "svvvvvv", [(112, CM)] * 2 + [(48, CM)] * 2, [far(2), side],
        info, latent, cache, cache_fine, below, above, kernel, megabytes=3,
    )
    right_0, left_0 = (lax.ppermute(sides[k], AXES, pairs_between(0, 0, 0, 2 * k - 1)) for k in range(2))
    right_1, left_1 = (lax.ppermute(sides[2 + k], AXES, pairs_between(1, 1, 0, 2 * k - 1)) for k in range(2))

    up_scratch = [pltpu.VMEM((9, CF, CM), BF16), dma((1,))]
    folded_shape = (4, CM, 1024)
    first_scratch = [
        pltpu.VMEM((4, 216, CM), F32),
        pltpu.VMEM((4, 216, CM), F32),
        side,
        far(1),
        pltpu.VMEM((4, 9, 2 * HALF, CM), BF16),
    ]
    first_shape = (2, ROWS, PITCH, CM)
    first_flops = 2 * 224 * 27 * CM * CM
    spread = lambda tile: [lax.ppermute(tile, AXES, pairs_between(0, 1, dh, 0, True)) for dh in range(2)]
    (early,) = call(
        first_early, "svvvvvvvv", [first_shape], first_scratch,
        info, latent, cache, below, left_0, right_0, kernel, b_mid, g_mid, flops=first_flops, megabytes=16,
    )
    group_a = spread(early)
    late, folded_1 = call(
        first_late, "svvvvvvvh", [first_shape, folded_shape], first_scratch + up_scratch,
        info, latent, below, left_0, right_0, kernel, b_mid, g_mid, up_kernel, flops=first_flops, megabytes=16,
    )
    group_b = spread(late)

    second_scratch = [
        pltpu.VMEM((4, 200, CM), F32),
        pltpu.VMEM((4, 200, CM), F32),
        side,
        far(2),
        pltpu.VMEM((4, 9, 144, CM), BF16),
    ]
    second_flops = 2 * 288 * 27 * CM * CM
    second_a, folded_0 = call(
        second_early, "svvvvvvvvvvh", [(RING + 112, CM), folded_shape],
        second_scratch + [pltpu.VMEM((112, CM), F32)] + up_scratch,
        info, cache, below, above, left_1, right_1, *group_a, kernel, b_mid, g_mid, up_kernel, flops=second_flops, megabytes=16,
    )
    returned = lax.ppermute(second_a, "segment", [(1, 0)])
    (second_b,) = call(
        second_late, "svvvvvvv", [(RING, CM)], second_scratch,
        info, *group_a, *group_b, kernel, b_mid, g_mid, flops=second_flops, megabytes=16,
    )
    (decoded,) = call(
        last_section, "svvvvvvvvhv", [(2, 8, 40, CF)],
        [
            pltpu.VMEM((2, 160, CM), F32),
            pltpu.VMEM((2, 4, 128, 256), F32),
            pltpu.VMEM((4, 4, 128, 256), F32),
            pltpu.VMEM((2, 56, 128), F32),
            pltpu.VMEM((112, CM), F32),
            pltpu.VMEM((4, 16, 96, 256), BF16),
            pltpu.VMEM((2, 2, 8, 40, 128), F32),
            pltpu.VMEM((27, CF, CF), BF16),
            dma((1,)),
        ],
        info, second_a, second_b, returned, cache_fine, folded_0, folded_1,
        b_up[None], g_fine[None], w_fine.reshape(27, CF, CF), b_fine[None],
        flops=2 * 768 * 27 * CF * CF, megabytes=16,
    )
    return decoded


def solution(mesh):
    return jax.shard_map(
        shards,
        mesh=mesh,
        in_specs=(
            P(None, "ha", "wa", None),
            P("segment", None, None, None, None, None),
            P("segment", None),
            P("segment", None),
            P("segment", None, "ha", "wa", None),
            P(),
            P(),
            P(),
            P(None, "ha", "wa", None),
            P(),
            P(),
        ),
        out_specs=P("segment", "ha", "wa", None),
        check_vma=False,
    )
```

time: 143 us -> 63.6 us (0.44)
  the two profiles are of different devices: /device:TPU:65 before, /device:TPU:125 now
where the time goes in v2:
time: 63.6 us; the launch traced here: 63.2 us
  waiting for transfers between devices  21.3 us (33%)
  Pallas kernels  18.6 us (29%)
  starting transfers between devices  16.6 us (26%)
  local copies, waits for them, and re-layouts  6.19 us (10%)
    pallas_call x7, Pallas kernels, call(): pl.pallas_call(body, out_shape=[jax.ShapeDtypeStruct(shape, BF16) for sha...  18.6 us
    ppermute x1, waiting for transfers between devices, shards(): returned = lax.ppermute(second_a, 'segment', [(1, 0)])  8.67 us
    ppermute x2, starting transfers between devices, shards(): lax.ppermute(sides[k], AXES, pairs_between(0, 0, 0, 2 * k - 1))  7.05 us
    unnamed x24, local copies, waits for them, and re-layouts  6.19 us
    ppermute x1, waiting for transfers between devices, shards(): lax.ppermute(to_above, 'ha', [(i, (i - 1) % N_HA) for i in range(N_HA)])  5.88 us
    ppermute x2, waiting for transfers between devices, shards(): lax.ppermute(sides[k], AXES, pairs_between(0, 0, 0, 2 * k - 1))  5.25 us
    ppermute x4, starting transfers between devices, shards(): lax.ppermute(tile, AXES, pairs_between(0, 1, dh, 0, True))  5.19 us
    ppermute x1, starting transfers between devices, shards(): returned = lax.ppermute(second_a, 'segment', [(1, 0)])  1.56 us
  transfers between devices with their start and end apart: 11, of which 4 were waited for; matrix products, arithmetic and copies ran while one was open for 0% of the time, Pallas kernels for 16%

profile of v2, /device:TPU:125, one launch (start us, length us, event | category | flops | bytes accessed | tf_op | source)
XLA Modules:
  0.0 63.2 jit_solution(14872732936620035433)
XLA Ops:
  0.0 0.9 %copy.18 = bf16[1,2,4,20,384]{4,3,2,1,0:T(8,128)(2,1)S(1)} copy(bf16[1,2,4,20,384]{4,2,3,1,0:T(4,128)(2,1)} %param.15) | data formatting | bytes 245760 | tf_op args[4]
  0.9 1.0 %copy.13.latent = bf16[4,4,20,384]{3,2,1,0:T(8,128)(2,1)S(1)} copy(bf16[4,4,20,384]{3,1,2,0:T(4,128)(2,1)} %param.11) | data formatting | bytes 491520 | tf_op args[0]
  1.9 0.1 pad_add_fusion.info
  2.0 1.0 %copy-done.3 = bf16[2,8,40,192]{3,2,1,0:T(8,128)(2,1)S(1)} copy-done((bf16[2,8,40,192]{3,2,1,0:T(8,128)(2,1)S(1)}, bf16[2,8,40,192]{3,2,1,0:T(8,128)(2,1)}, u32[]{:S(2)}) %copy-start.3) | copy-done | bytes 245784
  3.0 0.6 shard_map.109
  3.6 0.7 %collective-permute-start = (bf16[368,384]{1,0:T(8,128)(2,1)S(1)}, bf16[368,384]{1,0:T(8,128)(2,1)S(1)}, u32[]{:S(2)}, u32[]{:S(2)}) collective-permute-start(bf16[368,384]{1,0:T(8,128)(2,1)S(1)} %get-tuple-element.15), channel_id=1, source_target_pairs={{0,112},{16,0},{32,16},{48,32},{64,48},{80,64},{96,80},{112,96},{1... | collective-permute-start | bytes 847880 | tf_op jit(solution)/shard_map/ppermute | solution.py:434
  4.3 0.7 %collective-permute-start.1 = (bf16[128,384]{1,0:T(8,128)(2,1)S(1)}, bf16[128,384]{1,0:T(8,128)(2,1)S(1)}, u32[]{:S(2)}, u32[]{:S(2)}) collective-permute-start(bf16[128,384]{1,0:T(8,128)(2,1)S(1)} %get-tuple-element.16), channel_id=1, source_target_pairs={{128,144},{129,145},{130,146},{131,147},{132,148},{133,149},{134,1... | collective-permute-start | bytes 294920 | tf_op jit(solution)/shard_map/ppermute | solution.py:435
  4.9 0.0 collective-permute-done.1.above
  4.9 5.9 %collective-permute-done.below = bf16[368,384]{1,0:T(8,128)(2,1)S(1)} collective-permute-done((bf16[368,384]{1,0:T(8,128)(2,1)S(1)}, bf16[368,384]{1,0:T(8,128)(2,1)S(1)}, u32[]{:S(2)}, u32[]{:S(2)}) %collective-permute-start) | collective-permute-done | bytes 282656 | tf_op jit(solution)/shard_map/ppermute | solution.py:434
  10.8 3.3 %copy-done = bf16[1,3,3,3,384,384]{5,4,3,2,1,0:T(8,128)(2,1)S(1)} copy-done((bf16[1,3,3,3,384,384]{5,4,3,2,1,0:T(8,128)(2,1)S(1)}, bf16[1,3,3,3,384,384]{5,4,3,2,1,0:T(8,128)(2,1)}, u32[]{:S(2)}) %copy-start) | copy-done | bytes 7962648
  14.1 0.7 %shard_map.110 = (bf16[112,384]{1,0:T(8,128)(2,1)S(1)}, bf16[112,384]{1,0:T(8,128)(2,1)S(1)}, bf16[48,384]{1,0:T(8,128)(2,1)S(1)}, bf16[48,384]{1,0:T(8,128)(2,1)S(1)}) custom-call(s32[3]{0:T(128)S(1)} %pad_add_fusion.info, bf16[4,4,20,384]{3,2,1,0:T(8,128)(2,1)S(1)} %copy.13.latent, bf16[2,4,20,384]{3,2,1,0:T(8,128)(2,1)S(1)} %bitcast.22, ...), custom_call_target="tpu_custom_call" | custom-call | bytes 1048576 | tf_op jit(solution)/shard_map/pallas_call | solution.py:398
  14.8 5.0 %collective-permute-start.4 = (bf16[112,384]{1,0:T(8,128)(2,1)S(1)}, bf16[112,384]{1,0:T(8,128)(2,1)S(1)}, u32[]{:S(2)}, u32[]{:S(2)}) collective-permute-start(bf16[112,384]{1,0:T(8,128)(2,1)S(1)} %get-tuple-element.19), channel_id=1, source_target_pairs={{0,1},{1,2},{2,3},{3,4},{4,5},{5,6},{6,7},{7,8},{8,9},{9,10},{10,1... | collective-permute-start | bytes 258056 | tf_op jit(solution)/shard_map/ppermute | solution.py:440
  19.7 2.1 %collective-permute-start.5 = (bf16[112,384]{1,0:T(8,128)(2,1)S(1)}, bf16[112,384]{1,0:T(8,128)(2,1)S(1)}, u32[]{:S(2)}, u32[]{:S(2)}) collective-permute-start(bf16[112,384]{1,0:T(8,128)(2,1)S(1)} %get-tuple-element.20), channel_id=1, source_target_pairs={{1,0},{2,1},{3,2},{4,3},{5,4},{6,5},{7,6},{8,7},{9,8},{10,9},{11,1... | collective-permute-start | bytes 258056 | tf_op jit(solution)/shard_map/ppermute | solution.py:440
  21.8 0.7 %collective-permute-start.2 = (bf16[48,384]{1,0:T(8,128)(2,1)S(1)}, bf16[48,384]{1,0:T(8,128)(2,1)S(1)}, u32[]{:S(2)}, u32[]{:S(2)}) collective-permute-start(bf16[48,384]{1,0:T(8,128)(2,1)S(1)} %get-tuple-element.17), channel_id=1, source_target_pairs={{128,129},{129,130},{130,131},{131,132},{132,133},{133,134},{134,1... | collective-permute-start | bytes 110600 | tf_op jit(solution)/shard_map/ppermute | solution.py:441
  22.5 0.0 copy-start.2
  22.5 0.8 %collective-permute-start.3 = (bf16[48,384]{1,0:T(8,128)(2,1)S(1)}, bf16[48,384]{1,0:T(8,128)(2,1)S(1)}, u32[]{:S(2)}, u32[]{:S(2)}) collective-permute-start(bf16[48,384]{1,0:T(8,128)(2,1)S(1)} %get-tuple-element.18), channel_id=1, source_target_pairs={{129,128},{130,129},{131,130},{132,131},{133,132},{134,133},{135,1... | collective-permute-start | bytes 110600 | tf_op jit(solution)/shard_map/ppermute | solution.py:441
  23.3 0.0 collective-permute-done.4.left
  23.3 5.3 %collective-permute-done.5.right = bf16[112,384]{1,0:T(8,128)(2,1)S(1)} collective-permute-done((bf16[112,384]{1,0:T(8,128)(2,1)S(1)}, bf16[112,384]{1,0:T(8,128)(2,1)S(1)}, u32[]{:S(2)}, u32[]{:S(2)}) %collective-permute-start.5) | collective-permute-done | bytes 86048 | tf_op jit(solution)/shard_map/ppermute | solution.py:440
  28.6 0.0 copy-done.1
  28.6 0.0 copy-done.6
  28.6 0.0 copy-done.7
  28.6 4.0 %shard_map.111 = bf16[2,4,24,384]{3,2,1,0:T(8,128)(2,1)S(1)} custom-call(s32[3]{0:T(128)S(1)} %pad_add_fusion.info, bf16[4,4,20,384]{3,2,1,0:T(8,128)(2,1)S(1)} %copy.13.latent, bf16[2,4,20,384]{3,2,1,0:T(8,128)(2,1)S(1)} %bitcast.23, bf16[368,384]{1,0:T(8,128)(2,1)S(1)} %collective-permute-done.below, bf16[112,384]{1,0:T(8,128)(2,1)S(1)} %collective-permute-done.4.left, ...), custom_call_target="tpu_custom_call" | custom-call | flops 1783627776 | bytes 1048576 | tf_op jit(solution)/shard_map/pallas_call | solution.py:398
  32.6 1.3 %collective-permute-start.7 = (bf16[2,4,24,384]{3,2,1,0:T(8,128)(2,1)S(1)}, bf16[2,4,24,384]{3,2,1,0:T(8,128)(2,1)S(1)}, u32[]{:S(2)}, u32[]{:S(2)}) collective-permute-start(bf16[2,4,24,384]{3,2,1,0:T(8,128)(2,1)S(1)} %shard_map.111), channel_id=1, source_target_pairs={{112,128},{113,129},{114,130},{115,131},{116,132},{117,133},{118,1... | collective-permute-start | bytes 442376 | tf_op jit(solution)/shard_map/ppermute | solution.py:454
  33.9 1.3 %collective-permute-start.6 = (bf16[2,4,24,384]{3,2,1,0:T(8,128)(2,1)S(1)}, bf16[2,4,24,384]{3,2,1,0:T(8,128)(2,1)S(1)}, u32[]{:S(2)}, u32[]{:S(2)}) collective-permute-start(bf16[2,4,24,384]{3,2,1,0:T(8,128)(2,1)S(1)} %shard_map.111), channel_id=1, source_target_pairs={{0,128},{1,129},{2,130},{3,131},{4,132},{5,133},{6,134},{7,135},{8... | collective-permute-start | bytes 442376 | tf_op jit(solution)/shard_map/ppermute | solution.py:454
  35.2 0.0 copy-done.2
  35.2 4.2 %shard_map.113 = (bf16[2,4,24,384]{3,2,1,0:T(8,128)(2,1)S(1)}, bf16[4,384,1024]{2,1,0:T(8,128)(2,1)S(1)}) custom-call(s32[3]{0:T(128)S(1)} %pad_add_fusion.info, bf16[4,4,20,384]{3,2,1,0:T(8,128)(2,1)S(1)} %copy.13.latent, bf16[368,384]{1,0:T(8,128)(2,1)S(1)} %collective-permute-done.below, bf16[112,384]{1,0:T(8,128)(2,1)S(1)} %collective-permute-done.4.left, ...), custom_call_target="tpu_custom_call" | custom-call | flops 1783627776 | bytes 1048576 | tf_op jit(solution)/shard_map/pallas_call | solution.py:398
  39.4 1.3 %collective-permute-start.9 = (bf16[2,4,24,384]{3,2,1,0:T(8,128)(2,1)S(1)}, bf16[2,4,24,384]{3,2,1,0:T(8,128)(2,1)S(1)}, u32[]{:S(2)}, u32[]{:S(2)}) collective-permute-start(bf16[2,4,24,384]{3,2,1,0:T(8,128)(2,1)S(1)} %get-tuple-element.22), channel_id=1, source_target_pairs={{112,128},{113,129},{114,130},{115,131},{116,132},{117,133},{118,1... | collective-permute-start | bytes 442376 | tf_op jit(solution)/shard_map/ppermute | solution.py:454
  40.7 0.0 collective-permute-done.2.left
  40.8 1.3 %collective-permute-start.8 = (bf16[2,4,24,384]{3,2,1,0:T(8,128)(2,1)S(1)}, bf16[2,4,24,384]{3,2,1,0:T(8,128)(2,1)S(1)}, u32[]{:S(2)}, u32[]{:S(2)}) collective-permute-start(bf16[2,4,24,384]{3,2,1,0:T(8,128)(2,1)S(1)} %get-tuple-element.22), channel_id=1, source_target_pairs={{0,128},{1,129},{2,130},{3,131},{4,132},{5,133},{6,134},{7,135},{8... | collective-permute-start | bytes 442376 | tf_op jit(solution)/shard_map/ppermute | solution.py:454
  42.1 0.0 collective-permute-done.3.right
  42.1 0.0 collective-permute-done.7.top.top_a
  42.1 0.0 collective-permute-done.6.low.low_a
  42.1 1.7 %shard_map.112 = (bf16[400,384]{1,0:T(8,128)(2,1)S(1)}, bf16[4,384,1024]{2,1,0:T(8,128)(2,1)S(1)}) custom-call(s32[3]{0:T(128)S(1)} %pad_add_fusion.info, bf16[2,4,20,384]{3,2,1,0:T(8,128)(2,1)S(1)} %bitcast.24, bf16[368,384]{1,0:T(8,128)(2,1)S(1)} %collective-permute-done.below, bf16[128,384]{1,0:T(8,128)(2,1)S(1)} %collective-permute-done.1.above, ...), custom_call_target="tpu_custom_call" | custom-call | flops 2293235712 | bytes 1048576 | tf_op jit(solution)/shard_map/pallas_call | solution.py:398
  43.8 0.0 copy-start.4
  43.8 0.0 copy-start.5
  43.8 0.0 copy-start.8
  43.8 0.0 copy-start.9
  43.8 0.0 copy-start.10
  43.8 1.6 %collective-permute-start.10 = (bf16[400,384]{1,0:T(8,128)(2,1)S(1)}, bf16[400,384]{1,0:T(8,128)(2,1)S(1)}, u32[]{:S(2)}, u32[]{:S(2)}) collective-permute-start(bf16[400,384]{1,0:T(8,128)(2,1)S(1)} %get-tuple-element.21.lead), channel_id=1, source_target_pairs={{128,0},{129,1},{130,2},{131,3},{132,4},{133,5},{134,6},{135,7},{1... | collective-permute-start | bytes 921608 | tf_op jit(solution)/shard_map/ppermute | solution.py:479
  45.4 0.0 collective-permute-done.9.top_b
  45.4 1.5 %collective-permute-done.8.low_b = bf16[2,4,24,384]{3,2,1,0:T(8,128)(2,1)S(1)} collective-permute-done((bf16[2,4,24,384]{3,2,1,0:T(8,128)(2,1)S(1)}, bf16[2,4,24,384]{3,2,1,0:T(8,128)(2,1)S(1)}, u32[]{:S(2)}, u32[]{:S(2)}) %collective-permute-start.8) | collective-permute-done | bytes 147488 | tf_op jit(solution)/shard_map/ppermute | solution.py:454
  46.9 0.5 shard_map.114.main
  47.5 8.7 %collective-permute-done.10.returned = bf16[400,384]{1,0:T(8,128)(2,1)S(1)} collective-permute-done((bf16[400,384]{1,0:T(8,128)(2,1)S(1)}, bf16[400,384]{1,0:T(8,128)(2,1)S(1)}, u32[]{:S(2)}, u32[]{:S(2)}) %collective-permute-start.10) | collective-permute-done | bytes 307232 | tf_op jit(solution)/shard_map/ppermute | solution.py:479
  56.1 0.0 copy-done.4
  56.1 0.0 copy-done.8
  56.1 0.0 copy-done.9
  56.1 0.0 copy-done.10
  56.2 6.9 %shard_map.115 = bf16[2,8,40,192]{3,2,1,0:T(8,128)(2,1)} custom-call(s32[3]{0:T(128)S(1)} %pad_add_fusion.info, bf16[400,384]{1,0:T(8,128)(2,1)S(1)} %get-tuple-element.21.lead, bf16[288,384]{1,0:T(8,128)(2,1)S(1)} %shard_map.114.main, bf16[400,384]{1,0:T(8,128)(2,1)S(1)} %collective-permute-done.10.returned, bf16[2,8,40,192]{3,2,1,0:T(8,128)(2,1)S(1)} %copy-done.4, ...), custom_call_target="tpu_custom_call" | custom-call | flops 1528823808 | bytes 1048576 | tf_op jit(solution)/shard_map/pallas_call | solution.py:398
  (6 shorter events, 0.0 us)
Async XLA Ops:
  2.0 1.0 %copy-start.3 = (bf16[2,8,40,192]{3,2,1,0:T(8,128)(2,1)S(1)}, bf16[2,8,40,192]{3,2,1,0:T(8,128)(2,1)}, u32[]{:S(2)}) copy-start(bf16[2,8,40,192]{3,2,1,0:T(8,128)(2,1)} %cache.1) | copy-start | bytes 737284
  3.6 7.2 %collective-permute-start = (bf16[368,384]{1,0:T(8,128)(2,1)S(1)}, bf16[368,384]{1,0:T(8,128)(2,1)S(1)}, u32[]{:S(2)}, u32[]{:S(2)}) collective-permute-start(bf16[368,384]{1,0:T(8,128)(2,1)S(1)} %get-tuple-element.15), channel_id=1, source_target_pairs={{0,112},{16,0},{32,16},{48,32},{64,48},{80,64},{96,80},{112,96},{1... | collective-permute-start | bytes 847880 | tf_op jit(solution)/shard_map/ppermute | solution.py:434
  4.3 0.7 %collective-permute-start.1 = (bf16[128,384]{1,0:T(8,128)(2,1)S(1)}, bf16[128,384]{1,0:T(8,128)(2,1)S(1)}, u32[]{:S(2)}, u32[]{:S(2)}) collective-permute-start(bf16[128,384]{1,0:T(8,128)(2,1)S(1)} %get-tuple-element.16), channel_id=1, source_target_pairs={{128,144},{129,145},{130,146},{131,147},{132,148},{133,149},{134,1... | collective-permute-start | bytes 294920 | tf_op jit(solution)/shard_map/ppermute | solution.py:435
  10.8 3.3 %copy-start = (bf16[1,3,3,3,384,384]{5,4,3,2,1,0:T(8,128)(2,1)S(1)}, bf16[1,3,3,3,384,384]{5,4,3,2,1,0:T(8,128)(2,1)}, u32[]{:S(2)}) copy-start(bf16[1,3,3,3,384,384]{5,4,3,2,1,0:T(8,128)(2,1)} %param.12) | copy-start | bytes 23887876
  14.1 14.5 %copy-start.1 = (bf16[1,3,3,3,384,384]{5,4,3,2,1,0:T(8,128)(2,1)S(1)}, bf16[1,3,3,3,384,384]{5,4,3,2,1,0:T(8,128)(2,1)}, u32[]{:S(2)}) copy-start(bf16[1,3,3,3,384,384]{5,4,3,2,1,0:T(8,128)(2,1)} %param.12) | copy-start | bytes 23887876
  14.1 14.5 %copy-start.6 = (f32[1,384]{1,0:T(1,128)S(1)}, f32[1,384]{1,0:T(1,128)}, u32[]{:S(2)}) copy-start(f32[1,384]{1,0:T(1,128)} %b.7) | copy-start | bytes 4612
  14.1 14.5 %copy-start.7 = (f32[1,384]{1,0:T(1,128)S(1)}, f32[1,384]{1,0:T(1,128)}, u32[]{:S(2)}) copy-start(f32[1,384]{1,0:T(1,128)} %g.7) | copy-start | bytes 4612
  14.8 8.6 %collective-permute-start.4 = (bf16[112,384]{1,0:T(8,128)(2,1)S(1)}, bf16[112,384]{1,0:T(8,128)(2,1)S(1)}, u32[]{:S(2)}, u32[]{:S(2)}) collective-permute-start(bf16[112,384]{1,0:T(8,128)(2,1)S(1)} %get-tuple-element.19), channel_id=1, source_target_pairs={{0,1},{1,2},{2,3},{3,4},{4,5},{5,6},{6,7},{7,8},{8,9},{9,10},{10,1... | collective-permute-start | bytes 258056 | tf_op jit(solution)/shard_map/ppermute | solution.py:440
  19.7 8.8 %collective-permute-start.5 = (bf16[112,384]{1,0:T(8,128)(2,1)S(1)}, bf16[112,384]{1,0:T(8,128)(2,1)S(1)}, u32[]{:S(2)}, u32[]{:S(2)}) collective-permute-start(bf16[112,384]{1,0:T(8,128)(2,1)S(1)} %get-tuple-element.20), channel_id=1, source_target_pairs={{1,0},{2,1},{3,2},{4,3},{5,4},{6,5},{7,6},{8,7},{9,8},{10,9},{11,1... | collective-permute-start | bytes 258056 | tf_op jit(solution)/shard_map/ppermute | solution.py:440
  21.8 18.9 %collective-permute-start.2 = (bf16[48,384]{1,0:T(8,128)(2,1)S(1)}, bf16[48,384]{1,0:T(8,128)(2,1)S(1)}, u32[]{:S(2)}, u32[]{:S(2)}) collective-permute-start(bf16[48,384]{1,0:T(8,128)(2,1)S(1)} %get-tuple-element.17), channel_id=1, source_target_pairs={{128,129},{129,130},{130,131},{131,132},{132,133},{133,134},{134,1... | collective-permute-start | bytes 110600 | tf_op jit(solution)/shard_map/ppermute | solution.py:441
  22.5 12.7 %copy-start.2 = (bf16[3,3,384,192]{2,3,1,0:T(8,128)(2,1)S(1)}, bf16[3,3,384,192]{2,3,1,0:T(8,128)(2,1)}, u32[]{:S(2)}) copy-start(bf16[3,3,384,192]{2,3,1,0:T(8,128)(2,1)} %param.16) | copy-start | bytes 3981316
  22.5 19.5 %collective-permute-start.3 = (bf16[48,384]{1,0:T(8,128)(2,1)S(1)}, bf16[48,384]{1,0:T(8,128)(2,1)S(1)}, u32[]{:S(2)}, u32[]{:S(2)}) collective-permute-start(bf16[48,384]{1,0:T(8,128)(2,1)S(1)} %get-tuple-element.18), channel_id=1, source_target_pairs={{129,128},{130,129},{131,130},{132,131},{133,132},{134,133},{135,1... | collective-permute-start | bytes 110600 | tf_op jit(solution)/shard_map/ppermute | solution.py:441
  32.6 9.5 %collective-permute-start.7 = (bf16[2,4,24,384]{3,2,1,0:T(8,128)(2,1)S(1)}, bf16[2,4,24,384]{3,2,1,0:T(8,128)(2,1)S(1)}, u32[]{:S(2)}, u32[]{:S(2)}) collective-permute-start(bf16[2,4,24,384]{3,2,1,0:T(8,128)(2,1)S(1)} %shard_map.111), channel_id=1, source_target_pairs={{112,128},{113,129},{114,130},{115,131},{116,132},{117,133},{118,1... | collective-permute-start | bytes 442376 | tf_op jit(solution)/shard_map/ppermute | solution.py:454
  33.9 8.2 %collective-permute-start.6 = (bf16[2,4,24,384]{3,2,1,0:T(8,128)(2,1)S(1)}, bf16[2,4,24,384]{3,2,1,0:T(8,128)(2,1)S(1)}, u32[]{:S(2)}, u32[]{:S(2)}) collective-permute-start(bf16[2,4,24,384]{3,2,1,0:T(8,128)(2,1)S(1)} %shard_map.111), channel_id=1, source_target_pairs={{0,128},{1,129},{2,130},{3,131},{4,132},{5,133},{6,134},{7,135},{8... | collective-permute-start | bytes 442376 | tf_op jit(solution)/shard_map/ppermute | solution.py:454
  39.4 6.0 %collective-permute-start.9 = (bf16[2,4,24,384]{3,2,1,0:T(8,128)(2,1)S(1)}, bf16[2,4,24,384]{3,2,1,0:T(8,128)(2,1)S(1)}, u32[]{:S(2)}, u32[]{:S(2)}) collective-permute-start(bf16[2,4,24,384]{3,2,1,0:T(8,128)(2,1)S(1)} %get-tuple-element.22), channel_id=1, source_target_pairs={{112,128},{113,129},{114,130},{115,131},{116,132},{117,133},{118,1... | collective-permute-start | bytes 442376 | tf_op jit(solution)/shard_map/ppermute | solution.py:454
  40.8 6.1 %collective-permute-start.8 = (bf16[2,4,24,384]{3,2,1,0:T(8,128)(2,1)S(1)}, bf16[2,4,24,384]{3,2,1,0:T(8,128)(2,1)S(1)}, u32[]{:S(2)}, u32[]{:S(2)}) collective-permute-start(bf16[2,4,24,384]{3,2,1,0:T(8,128)(2,1)S(1)} %get-tuple-element.22), channel_id=1, source_target_pairs={{0,128},{1,129},{2,130},{3,131},{4,132},{5,133},{6,134},{7,135},{8... | collective-permute-start | bytes 442376 | tf_op jit(solution)/shard_map/ppermute | solution.py:454
  43.8 12.3 %copy-start.4 = (bf16[2,8,40,192]{3,2,1,0:T(8,128)(2,1)S(1)}, bf16[2,8,40,192]{3,2,1,0:T(8,128)(2,1)}, u32[]{:S(2)}) copy-start(bf16[2,8,40,192]{3,2,1,0:T(8,128)(2,1)} %cache.1) | copy-start | bytes 737284
  43.8 12.3 %copy-start.5 = (bf16[3,3,3,192,192]{4,3,2,1,0:T(8,128)(2,1)S(1)}, bf16[3,3,3,192,192]{4,3,2,1,0:T(8,128)(2,1)}, u32[]{:S(2)}) copy-start(bf16[3,3,3,192,192]{4,3,2,1,0:T(8,128)(2,1)} %param.20) | copy-start | bytes 5971972
  43.8 12.3 %copy-start.8 = (f32[192]{0:T(256)S(1)}, f32[192]{0:T(256)}, u32[]{:S(2)}) copy-start(f32[192]{0:T(256)} %param.17) | copy-start | bytes 2308
  43.8 12.3 %copy-start.9 = (f32[192]{0:T(256)S(1)}, f32[192]{0:T(256)}, u32[]{:S(2)}) copy-start(f32[192]{0:T(256)} %param.18) | copy-start | bytes 2308
  43.8 12.3 %copy-start.10 = (f32[192]{0:T(256)S(1)}, f32[192]{0:T(256)}, u32[]{:S(2)}) copy-start(f32[192]{0:T(256)} %param.21) | copy-start | bytes 2308
  43.8 12.3 %collective-permute-start.10 = (bf16[400,384]{1,0:T(8,128)(2,1)S(1)}, bf16[400,384]{1,0:T(8,128)(2,1)S(1)}, u32[]{:S(2)}, u32[]{:S(2)}) collective-permute-start(bf16[400,384]{1,0:T(8,128)(2,1)S(1)} %get-tuple-element.21.lead), channel_id=1, source_target_pairs={{128,0},{129,1},{130,2},{131,3},{132,4},{133,5},{134,6},{135,7},{1... | collective-permute-start | bytes 921608 | tf_op jit(solution)/shard_map/ppermute | solution.py:479

commit v3 on v2

--- a/solution.py
+++ b/solution.py
@@ -25,16 +25,16 @@
 def normed(values, gain_vec, channels):
     inv_rms = lax.rsqrt(jnp.sum(values * values, axis=-1, keepdims=True) * (1.0 / channels) + 1e-06)
     scaled = values * inv_rms * gain_vec
-    return scaled / (1.0 + jnp.exp(-scaled))
-
-
-def conv_frames(patches, w, length):
+    half = 0.5 * scaled
+    return half + half * jnp.tanh(half)
+
+
+def conv_frames(stores, w):
     total = None
     for a in range(3):
-        for pq in range(9):
-            lhs = patches[a : a + 2, pq].reshape(2 * length, CM)
-            part = jnp.dot(lhs, w[a * 9 + pq], preferred_element_type=F32)
-            total = part if total is None else total + part
+        lhs = jnp.concatenate([stores[a][...], stores[a + 1][...]], axis=0)
+        part = jnp.dot(lhs, w[a], preferred_element_type=F32)
+        total = part if total is None else total + part
     return total
 
 
@@ -68,7 +68,7 @@
         to_below[...] = side[0:128].astype(BF16)
 
 
-def pack_columns(info, latent, cache, fine, below, above, _, left_0, right_0, left_1, right_1, far, side):
+def pack_columns(info, latent, cache, fine, below, above, left_0, right_0, left_1, right_1, far, side):
     far[0] = below[...].astype(F32)
 
     @pl.when(info[0] == 0)
@@ -133,16 +133,19 @@
                             part = taps[p * 3 + q]
                             total = part if total is None else total + part
                     both = jnp.concatenate([total, zeros], axis=1).astype(BF16)
-                    out[du * 2 + dv, :, place * 256 : place * 256 + 256] = both
-
-
-def first_section(group, info, latent, cache, below, left, right, w, b, g, out, raw, act, side, far, patches):
+                    out[(du * 2 + dv) * CM : (du * 2 + dv + 1) * CM, place * 256 : place * 256 + 256] = both
+
+
+def first_section(group, info, latent, cache, below, left, right, w, b, g, out, kept, raw, act, side, far, patches):
+    stores = [patches.at[0], patches.at[1], kept.at[0], kept.at[1]]
+    if group == 1:
+        stores = stores[2:] + stores[:2]
     last = info[1] == N_HA - 1
     side[0] = left[...].astype(F32)
     side[1] = right[...].astype(F32)
     far[...] = below[...].astype(F32)
     slots = [(1, False), (2, False), (3, False), (4, True), (3, True), (4, False), (5, False), (6, False)]
-    for f in range(4):
+    for f in range(2 * group, 4):
         lead = group == 0 and f < 2
         frame = f if group == 1 else (4 + f if lead else f - 2)
         for slot, (row, hide) in enumerate(slots):
@@ -169,8 +172,8 @@
                 top = p * WIDE + q
                 low = top + 4 * WIDE
                 both = jnp.concatenate([act[f, top : top + HALF], act[f, low : low + HALF]], axis=0)
-                patches[f, p * 3 + q] = both.astype(BF16)
-    total = conv_frames(patches, w, 2 * HALF) + b[...]
+                stores[f][:, (p * 3 + q) * CM : (p * 3 + q + 1) * CM] = both.astype(BF16)
+    total = conv_frames(stores, w) + b[...]
     cols = lax.broadcasted_iota(jnp.int32, (PITCH, 1), 0) + (info[2] * COLS - 2)
     inside = (cols >= 0) & (cols < GRID_COLS)
     act[0, 0 : 2 * HALF] = total[: 2 * HALF]
@@ -183,25 +186,28 @@
             out[t, r] = jnp.where(inside, value, 0.0).astype(BF16)
 
 
-def first_early(info, latent, cache, below, left, right, w, b, g, out, *scratch):
+def first_early(info, latent, cache, below, left, right, w, b, g, out, kept, *scratch):
     @pl.when(info[0] == 0)
     def _():
-        first_section(0, info, latent, cache, below, left, right, w, b, g, out, *scratch)
-
-
-def first_late(info, latent, below, left, right, w, b, g, w_up_hbm, out, folded, *scratch):
+        first_section(0, info, latent, cache, below, left, right, w, b, g, out, kept, *scratch)
+
+
+def first_late(info, latent, below, left, right, kept, w, b, g, w_up_hbm, out, folded, *scratch):
     *scratch, w_up, sems = scratch
 
     @pl.when(info[0] == 0)
     def _():
-        first_section(1, info, latent, None, below, left, right, w, b, g, out, *scratch)
+        first_section(1, info, latent, None, below, left, right, w, b, g, out, kept, *scratch)
 
     @pl.when(info[0] == 1)
     def _():
         fold_weights(w_up_hbm, w_up, sems.at[0], folded)
 
 
-def second_section(info, caches, earlier, later, w, b, g, out, raw, act, side, far, patches):
+def second_section(info, caches, tiles, w, b, g, out, kept, raw, act, side, far, patches):
+    stores = [patches.at[0], patches.at[1], kept.at[0], kept.at[1]]
+    if caches is None:
+        stores = stores[2:] + stores[:2]
     first, last = info[1] == 0, info[1] == N_HA - 1
     if caches is not None:
         cache, below, above, left, right = caches
@@ -209,7 +215,7 @@
         side[1, 0:48] = right[...].astype(F32)
         far[0] = below[...].astype(F32)
         far[1, 0:128] = above[...].astype(F32)
-    for f in range(4):
+    for f in range(0 if caches is not None else 2, 4):
         lead = caches is not None and f < 2
         t = f % 2
         for u in range(8):
@@ -230,7 +236,7 @@
                 raw[f, base + 2 : base + 22] = line
                 raw[f, base + 22 : base + 24] = after
             else:
-                low, top = earlier if caches is not None or f < 2 else later
+                low, top = tiles
                 line = (top[t, u] if u < 4 else low[t, u - 4]).astype(F32)
                 raw[f, base : base + PITCH] = line if hide is None else jnp.where(hide, 0.0, line)
         raw[f, 8 * PITCH : 200] = jnp.zeros((8, CM), F32)
@@ -240,8 +246,8 @@
         for p in range(3):
             for q in range(3):
                 at = p * PITCH + q
-                patches[f, p * 3 + q] = act[f, at : at + 144].astype(BF16)
-    total = conv_frames(patches, w, 144) + b[...]
+                stores[f][:, (p * 3 + q) * CM : (p * 3 + q + 1) * CM] = act[f, at : at + 144].astype(BF16)
+    total = conv_frames(stores, w) + b[...]
     cell = lax.broadcasted_iota(jnp.int32, (PITCH, 1), 0)
     cols = cell + (info[2] * COLS - 1)
     inside = (cols >= 0) & (cols < GRID_COLS) & (cell < 22)
@@ -255,12 +261,12 @@
             out[at : at + PITCH] = jnp.where(fits, value, 0.0).astype(BF16)
 
 
-def second_early(info, cache, below, above, left, right, low, top, w, b, g, w_up_hbm, out, folded, *scratch):
+def second_early(info, cache, below, above, left, right, low, top, w, b, g, w_up_hbm, out, kept, folded, *scratch):
     *scratch, ring, w_up, sems = scratch
 
     @pl.when(info[0] == 1)
     def _():
-        second_section(info, (cache, below, above, left, right), (low, top), None, w, b, g, out, *scratch)
+        second_section(info, (cache, below, above, left, right), (low, top), w, b, g, out, kept, *scratch)
         first, last = info[1] == 0, info[1] == N_HA - 1
         side, far = scratch[2:4]
         ring[...] = jnp.zeros((112, CM), F32)
@@ -277,16 +283,18 @@
         fold_weights(w_up_hbm, w_up, sems.at[0], folded)
 
 
-def second_late(info, low_a, top_a, low_b, top_b, w, b, g, out, *scratch):
+def second_late(info, low, top, kept, w, b, g, out, *scratch):
     @pl.when(info[0] == 1)
     def _():
-        second_section(info, None, (low_a, top_a), (low_b, top_b), w, b, g, out, *scratch)
+        second_section(info, None, (low, top), w, b, g, out, kept, *scratch)
 
 
 def last_section(info, lead, main, returned, cache, folded_0, folded_1, b_up, g, w_hbm, b,
                  out, coarse, ups, act, rows, ring, patches, wide, w, sems):
-    copy = pltpu.make_async_copy(w_hbm, w, sems.at[0])
+    copy = pltpu.make_async_copy(w_hbm, w.at[:, pl.ds(0, CF)], sems.at[0])
     copy.start()
+    for k in range(27):
+        w[k, CF:256] = jnp.zeros((64, CF), BF16)
     lanes = lambda ref: jnp.concatenate([ref[...], jnp.zeros((1, 64), F32)], axis=1)
     bias, gain = lanes(b_up), lanes(g)
 
@@ -299,14 +307,12 @@
             for du in range(2)
             for dv in range(2)
         ]
+        lhs = jnp.concatenate(lhs, axis=1)
         cell = lax.broadcasted_iota(jnp.int32, (128, 1), 0)
         col = lax.rem(cell, PITCH)
         for phase in range(4):
             br, bc = phase // 2, phase % 2
-            total = None
-            for k in range(4):
-                part = jnp.dot(lhs[k], w_up[k, :, phase * 256 : phase * 256 + 256], preferred_element_type=F32)
-                total = part if total is None else total + part
+            total = jnp.dot(lhs, w_up[:, phase * 256 : phase * 256 + 256], preferred_element_type=F32)
             value = (total + bias).astype(BF16).astype(F32)
             if br == 0:
                 outside = (cell < PITCH) & (info[1] == 0)
@@ -324,6 +330,7 @@
 
     @pl.when(info[0] == 0)
     def _():
+        rows[...] = jnp.zeros((2, 56, 128), F32)
         ring[...] = returned[RING : RING + 112].astype(F32)
         for t in range(2):
             part = slice(t * CF, t * CF + CF)
@@ -363,14 +370,16 @@
     for yb in range(2):
         for xb in range(2):
             total = None
+            blocks = [
+                (((yb + p) % 2) * 2 + (xb + q) % 2) * 4 + ((yb + p) // 2) * 2 + (xb + q) // 2
+                for p in range(3)
+                for q in range(3)
+            ]
             for a in range(3):
-                for p in range(3):
-                    for q in range(3):
-                        plane = ((yb + p) % 2) * 2 + (xb + q) % 2
-                        block = plane * 4 + ((yb + p) // 2) * 2 + (xb + q) // 2
-                        lhs = patches[a : a + 2, block].reshape(192, 256)[:, :CF]
-                        part = jnp.dot(lhs, w[a * 9 + p * 3 + q], preferred_element_type=F32)
-                        total = part if total is None else total + part
+                lhs = jnp.concatenate([patches[a : a + 2, block].reshape(192, 256) for block in blocks], axis=1)
+                taps = w[a * 9 : a * 9 + 9].reshape(9 * 256, CF)
+                part = jnp.dot(lhs, taps, preferred_element_type=F32)
+                total = part if total is None else total + part
             total = total + b[...]
             plane = ((yb + 1) % 2) * 2 + (xb + 1) % 2
             at = ((yb + 1) // 2) * PITCH + (xb + 1) // 2
@@ -421,7 +430,7 @@
 
 def shards(latent, w_mid, b_mid, g_mid, cache_mid, w_up, b_up, g_fine, cache_fine, w_fine, b_fine):
     info = jnp.stack([lax.axis_index(axis) for axis in AXES]).astype(jnp.int32)
-    kernel = w_mid.reshape(27, CM, CM)
+    kernel = w_mid.reshape(3, 9 * CM, CM)
     up_kernel = jnp.swapaxes(w_up, 2, 3).reshape(9, CF, CM)
     dma = pltpu.SemaphoreType.DMA
 
@@ -434,32 +443,32 @@
     below = lax.ppermute(to_above, "ha", [(i, (i - 1) % N_HA) for i in range(N_HA)])
     above = lax.ppermute(to_below, AXES, pairs_between(1, 1, 1, 0))
     sides = call(
-        pack_columns, "svvvvvv", [(112, CM)] * 2 + [(48, CM)] * 2, [far(2), side],
-        info, latent, cache, cache_fine, below, above, kernel, megabytes=3,
+        pack_columns, "svvvvv", [(112, CM)] * 2 + [(48, CM)] * 2, [far(2), side],
+        info, latent, cache, cache_fine, below, above, megabytes=3, flops=2 * 10**9,
     )
     right_0, left_0 = (lax.ppermute(sides[k], AXES, pairs_between(0, 0, 0, 2 * k - 1)) for k in range(2))
     right_1, left_1 = (lax.ppermute(sides[2 + k], AXES, pairs_between(1, 1, 0, 2 * k - 1)) for k in range(2))
 
     up_scratch = [pltpu.VMEM((9, CF, CM), BF16), dma((1,))]
-    folded_shape = (4, CM, 1024)
+    folded_shape = (4 * CM, 1024)
     first_scratch = [
         pltpu.VMEM((4, 216, CM), F32),
         pltpu.VMEM((4, 216, CM), F32),
         side,
         far(1),
-        pltpu.VMEM((4, 9, 2 * HALF, CM), BF16),
+        pltpu.VMEM((2, 2 * HALF, 9 * CM), BF16),
     ]
     first_shape = (2, ROWS, PITCH, CM)
     first_flops = 2 * 224 * 27 * CM * CM
     spread = lambda tile: [lax.ppermute(tile, AXES, pairs_between(0, 1, dh, 0, True)) for dh in range(2)]
-    (early,) = call(
-        first_early, "svvvvvvvv", [first_shape], first_scratch,
+    early, kept = call(
+        first_early, "svvvvvvvv", [first_shape, (2, 2 * HALF, 9 * CM)], first_scratch,
         info, latent, cache, below, left_0, right_0, kernel, b_mid, g_mid, flops=first_flops, megabytes=16,
     )
     group_a = spread(early)
     late, folded_1 = call(
-        first_late, "svvvvvvvh", [first_shape, folded_shape], first_scratch + up_scratch,
-        info, latent, below, left_0, right_0, kernel, b_mid, g_mid, up_kernel, flops=first_flops, megabytes=16,
+        first_late, "svvvvvvvvh", [first_shape, folded_shape], first_scratch + up_scratch,
+        info, latent, below, left_0, right_0, kept, kernel, b_mid, g_mid, up_kernel, flops=first_flops, megabytes=16,
     )
     group_b = spread(late)
 
@@ -468,18 +477,18 @@
         pltpu.VMEM((4, 200, CM), F32),
         side,
         far(2),
-        pltpu.VMEM((4, 9, 144, CM), BF16),
+        pltpu.VMEM((2, 144, 9 * CM), BF16),
     ]
     second_flops = 2 * 288 * 27 * CM * CM
-    second_a, folded_0 = call(
-        second_early, "svvvvvvvvvvh", [(RING + 112, CM), folded_shape],
+    second_a, kept, folded_0 = call(
+        second_early, "svvvvvvvvvvh", [(RING + 112, CM), (2, 144, 9 * CM), folded_shape],
         second_scratch + [pltpu.VMEM((112, CM), F32)] + up_scratch,
         info, cache, below, above, left_1, right_1, *group_a, kernel, b_mid, g_mid, up_kernel, flops=second_flops, megabytes=16,
     )
     returned = lax.ppermute(second_a, "segment", [(1, 0)])
     (second_b,) = call(
-        second_late, "svvvvvvv", [(RING, CM)], second_scratch,
-        info, *group_a, *group_b, kernel, b_mid, g_mid, flops=second_flops, megabytes=16,
+        second_late, "svvvvvv", [(RING, CM)], second_scratch,
+        info, *group_b, kept, kernel, b_mid, g_mid, flops=second_flops, megabytes=16,
     )
     (decoded,) = call(
         last_section, "svvvvvvvvhv", [(2, 8, 40, CF)],
@@ -491,7 +500,7 @@
             pltpu.VMEM((112, CM), F32),
             pltpu.VMEM((4, 16, 96, 256), BF16),
             pltpu.VMEM((2, 2, 8, 40, 128), F32),
-            pltpu.VMEM((27, CF, CF), BF16),
+            pltpu.VMEM((27, 256, CF), BF16),
             dma((1,)),
         ],
         info, second_a, second_b, returned, cache_fine, folded_0, folded_1,

time: 63.6 us -> 58.7 us (0.923)
  local copies, waits for them, and re-layouts: 6.19 us -> 2.91 us
  Pallas kernels: 18.6 us -> 17 us
    unnamed x24 -> x22, local copies, waits for them, and re-layouts: 6.19 us -> 2.91 us
    pallas_call x7, Pallas kernels: 18.6 us -> 17 us  [call(): pl.pallas_call(body, out_shape=[jax.ShapeDtypeStruct(shape, BF16) for sha...]
where the time goes in v3:
time: 58.7 us; the launch traced here: 58.4 us
  waiting for transfers between devices  21.8 us (37%)
  Pallas kernels  17 us (29%)
  starting transfers between devices  16.3 us (28%)
  local copies, waits for them, and re-layouts  2.91 us (5%)
    pallas_call x7, Pallas kernels, call(): pl.pallas_call(body, out_shape=[jax.ShapeDtypeStruct(shape, BF16) for sha...  17 us
    ppermute x1, waiting for transfers between devices, shards(): returned = lax.ppermute(second_a, 'segment', [(1, 0)])  8.65 us
    ppermute x2, starting transfers between devices, shards(): lax.ppermute(sides[k], AXES, pairs_between(0, 0, 0, 2 * k - 1))  6.79 us
    ppermute x1, waiting for transfers between devices, shards(): lax.ppermute(to_above, 'ha', [(i, (i - 1) % N_HA) for i in range(N_HA)])  5.74 us
    ppermute x2, waiting for transfers between devices, shards(): lax.ppermute(sides[k], AXES, pairs_between(0, 0, 0, 2 * k - 1))  5.4 us
    ppermute x4, starting transfers between devices, shards(): lax.ppermute(tile, AXES, pairs_between(0, 1, dh, 0, True))  5.19 us
    unnamed x22, local copies, waits for them, and re-layouts  2.91 us
    ppermute x4, waiting for transfers between devices, shards(): lax.ppermute(tile, AXES, pairs_between(0, 1, dh, 0, True))  1.95 us
  transfers between devices with their start and end apart: 11, of which 4 were waited for; matrix products, arithmetic and copies ran while one was open for 0% of the time, Pallas kernels for 16%

profile of v3, /device:TPU:125, one launch (start us, length us, event | category | flops | bytes accessed | tf_op | source)
XLA Modules:
  0.0 58.4 jit_solution(2534821659730446562)
XLA Ops:
  0.0 0.9 %copy.18 = bf16[1,2,4,20,384]{4,3,2,1,0:T(8,128)(2,1)S(1)} copy(bf16[1,2,4,20,384]{4,2,3,1,0:T(4,128)(2,1)} %param.15) | data formatting | bytes 245760 | tf_op args[4]
  0.9 1.0 %copy.13.latent = bf16[4,4,20,384]{3,2,1,0:T(8,128)(2,1)S(1)} copy(bf16[4,4,20,384]{3,1,2,0:T(4,128)(2,1)} %param.11) | data formatting | bytes 491520 | tf_op args[0]
  1.9 0.1 pad_add_fusion.info
  2.0 0.0 copy-start.3
  2.0 1.0 %copy-done.3 = bf16[2,8,40,192]{3,2,1,0:T(8,128)(2,1)S(1)} copy-done((bf16[2,8,40,192]{3,2,1,0:T(8,128)(2,1)S(1)}, bf16[2,8,40,192]{3,2,1,0:T(8,128)(2,1)}, u32[]{:S(2)}) %copy-start.3) | copy-done | bytes 245784
  3.0 0.0 copy-start
  3.0 0.6 %shard_map.109 = (bf16[368,384]{1,0:T(8,128)(2,1)S(1)}, bf16[128,384]{1,0:T(8,128)(2,1)S(1)}) custom-call(s32[3]{0:T(128)S(1)} %pad_add_fusion.info, bf16[4,4,20,384]{3,2,1,0:T(8,128)(2,1)S(1)} %copy.13.latent, bf16[2,4,20,384]{3,2,1,0:T(8,128)(2,1)S(1)} %bitcast.21, bf16[2,8,40,192]{3,2,1,0:T(8,128)(2,1)S(1)} %copy-done.3), custom_call_target="tpu_custom_call" | custom-call | bytes 1048576 | tf_op jit(solution)/shard_map/pallas_call | solution.py:407
  3.6 0.7 %collective-permute-start = (bf16[368,384]{1,0:T(8,128)(2,1)S(1)}, bf16[368,384]{1,0:T(8,128)(2,1)S(1)}, u32[]{:S(2)}, u32[]{:S(2)}) collective-permute-start(bf16[368,384]{1,0:T(8,128)(2,1)S(1)} %get-tuple-element.18), channel_id=1, source_target_pairs={{0,112},{16,0},{32,16},{48,32},{64,48},{80,64},{96,80},{112,96},{1... | collective-permute-start | bytes 847880 | tf_op jit(solution)/shard_map/ppermute | solution.py:443
  4.3 0.0 copy-start.5
  4.3 0.0 copy-start.6
  4.3 0.8 %collective-permute-start.1 = (bf16[128,384]{1,0:T(8,128)(2,1)S(1)}, bf16[128,384]{1,0:T(8,128)(2,1)S(1)}, u32[]{:S(2)}, u32[]{:S(2)}) collective-permute-start(bf16[128,384]{1,0:T(8,128)(2,1)S(1)} %get-tuple-element.19), channel_id=1, source_target_pairs={{128,144},{129,145},{130,146},{131,147},{132,148},{133,149},{134,1... | collective-permute-start | bytes 294920 | tf_op jit(solution)/shard_map/ppermute | solution.py:444
  5.1 0.0 collective-permute-done.1.above
  5.1 5.7 %collective-permute-done.below = bf16[368,384]{1,0:T(8,128)(2,1)S(1)} collective-permute-done((bf16[368,384]{1,0:T(8,128)(2,1)S(1)}, bf16[368,384]{1,0:T(8,128)(2,1)S(1)}, u32[]{:S(2)}, u32[]{:S(2)}) %collective-permute-start) | collective-permute-done | bytes 282656 | tf_op jit(solution)/shard_map/ppermute | solution.py:443
  10.8 0.7 %shard_map.110 = (bf16[112,384]{1,0:T(8,128)(2,1)S(1)}, bf16[112,384]{1,0:T(8,128)(2,1)S(1)}, bf16[48,384]{1,0:T(8,128)(2,1)S(1)}, bf16[48,384]{1,0:T(8,128)(2,1)S(1)}) custom-call(s32[3]{0:T(128)S(1)} %pad_add_fusion.info, bf16[4,4,20,384]{3,2,1,0:T(8,128)(2,1)S(1)} %copy.13.latent, bf16[2,4,20,384]{3,2,1,0:T(8,128)(2,1)S(1)} %bitcast.22, ...), custom_call_target="tpu_custom_call" | custom-call | flops 2000000000 | bytes 1048576 | tf_op jit(solution)/shard_map/pallas_call | solution.py:407
  11.5 4.7 %collective-permute-start.4 = (bf16[112,384]{1,0:T(8,128)(2,1)S(1)}, bf16[112,384]{1,0:T(8,128)(2,1)S(1)}, u32[]{:S(2)}, u32[]{:S(2)}) collective-permute-start(bf16[112,384]{1,0:T(8,128)(2,1)S(1)} %get-tuple-element.22), channel_id=1, source_target_pairs={{0,1},{1,2},{2,3},{3,4},{4,5},{5,6},{6,7},{7,8},{8,9},{9,10},{10,1... | collective-permute-start | bytes 258056 | tf_op jit(solution)/shard_map/ppermute | solution.py:449
  16.2 2.1 %collective-permute-start.5 = (bf16[112,384]{1,0:T(8,128)(2,1)S(1)}, bf16[112,384]{1,0:T(8,128)(2,1)S(1)}, u32[]{:S(2)}, u32[]{:S(2)}) collective-permute-start(bf16[112,384]{1,0:T(8,128)(2,1)S(1)} %get-tuple-element.23), channel_id=1, source_target_pairs={{1,0},{2,1},{3,2},{4,3},{5,4},{6,5},{7,6},{8,7},{9,8},{10,9},{11,1... | collective-permute-start | bytes 258056 | tf_op jit(solution)/shard_map/ppermute | solution.py:449
  18.3 0.7 %collective-permute-start.2 = (bf16[48,384]{1,0:T(8,128)(2,1)S(1)}, bf16[48,384]{1,0:T(8,128)(2,1)S(1)}, u32[]{:S(2)}, u32[]{:S(2)}) collective-permute-start(bf16[48,384]{1,0:T(8,128)(2,1)S(1)} %get-tuple-element.20), channel_id=1, source_target_pairs={{128,129},{129,130},{130,131},{131,132},{132,133},{133,134},{134,1... | collective-permute-start | bytes 110600 | tf_op jit(solution)/shard_map/ppermute | solution.py:450
  19.0 0.7 %collective-permute-start.3 = (bf16[48,384]{1,0:T(8,128)(2,1)S(1)}, bf16[48,384]{1,0:T(8,128)(2,1)S(1)}, u32[]{:S(2)}, u32[]{:S(2)}) collective-permute-start(bf16[48,384]{1,0:T(8,128)(2,1)S(1)} %get-tuple-element.21), channel_id=1, source_target_pairs={{129,128},{130,129},{131,130},{132,131},{133,132},{134,133},{135,1... | collective-permute-start | bytes 110600 | tf_op jit(solution)/shard_map/ppermute | solution.py:450
  19.7 0.0 collective-permute-done.4.left
  19.7 5.4 %collective-permute-done.5.right = bf16[112,384]{1,0:T(8,128)(2,1)S(1)} collective-permute-done((bf16[112,384]{1,0:T(8,128)(2,1)S(1)}, bf16[112,384]{1,0:T(8,128)(2,1)S(1)}, u32[]{:S(2)}, u32[]{:S(2)}) %collective-permute-start.5) | collective-permute-done | bytes 86048 | tf_op jit(solution)/shard_map/ppermute | solution.py:449
  25.1 0.0 copy-done
  25.1 0.0 copy-done.5
  25.1 0.0 copy-done.6
  25.1 0.0 copy-start.1
  25.1 3.7 %shard_map.111 = (bf16[2,4,24,384]{3,2,1,0:T(8,128)(2,1)S(1)}, bf16[2,112,3456]{2,1,0:T(8,128)(2,1)S(1)}) custom-call(s32[3]{0:T(128)S(1)} %pad_add_fusion.info, bf16[4,4,20,384]{3,2,1,0:T(8,128)(2,1)S(1)} %copy.13.latent, bf16[2,4,20,384]{3,2,1,0:T(8,128)(2,1)S(1)} %bitcast.23, bf16[368,384]{1,0:T(8,128)(2,1)S(1)} %collective-permute-done.below, ...), custom_call_target="tpu_custom_call" | custom-call | flops 1783627776 | bytes 1048576 | tf_op jit(solution)/shard_map/pallas_call | solution.py:407
  28.8 1.3 %collective-permute-start.7 = (bf16[2,4,24,384]{3,2,1,0:T(8,128)(2,1)S(1)}, bf16[2,4,24,384]{3,2,1,0:T(8,128)(2,1)S(1)}, u32[]{:S(2)}, u32[]{:S(2)}) collective-permute-start(bf16[2,4,24,384]{3,2,1,0:T(8,128)(2,1)S(1)} %get-tuple-element.24), channel_id=1, source_target_pairs={{112,128},{113,129},{114,130},{115,131},{116,132},{117,133},{118,1... | collective-permute-start | bytes 442376 | tf_op jit(solution)/shard_map/ppermute | solution.py:463
  30.1 1.3 %collective-permute-start.6 = (bf16[2,4,24,384]{3,2,1,0:T(8,128)(2,1)S(1)}, bf16[2,4,24,384]{3,2,1,0:T(8,128)(2,1)S(1)}, u32[]{:S(2)}, u32[]{:S(2)}) collective-permute-start(bf16[2,4,24,384]{3,2,1,0:T(8,128)(2,1)S(1)} %get-tuple-element.24), channel_id=1, source_target_pairs={{0,128},{1,129},{2,130},{3,131},{4,132},{5,133},{6,134},{7,135},{8... | collective-permute-start | bytes 442376 | tf_op jit(solution)/shard_map/ppermute | solution.py:463
  31.4 0.0 copy-done.1
  31.4 3.5 %shard_map.113 = (bf16[2,4,24,384]{3,2,1,0:T(8,128)(2,1)S(1)}, bf16[1536,1024]{1,0:T(8,128)(2,1)S(1)}) custom-call(s32[3]{0:T(128)S(1)} %pad_add_fusion.info, bf16[4,4,20,384]{3,2,1,0:T(8,128)(2,1)S(1)} %copy.13.latent, bf16[368,384]{1,0:T(8,128)(2,1)S(1)} %collective-permute-done.below, bf16[112,384]{1,0:T(8,128)(2,1)S(1)} %collective-permute-done.4.left, ...), custom_call_target="tpu_custom_call" | custom-call | flops 1783627776 | bytes 1048576 | tf_op jit(solution)/shard_map/pallas_call | solution.py:407
  35.0 1.3 %collective-permute-start.9 = (bf16[2,4,24,384]{3,2,1,0:T(8,128)(2,1)S(1)}, bf16[2,4,24,384]{3,2,1,0:T(8,128)(2,1)S(1)}, u32[]{:S(2)}, u32[]{:S(2)}) collective-permute-start(bf16[2,4,24,384]{3,2,1,0:T(8,128)(2,1)S(1)} %get-tuple-element.27), channel_id=1, source_target_pairs={{112,128},{113,129},{114,130},{115,131},{116,132},{117,133},{118,1... | collective-permute-start | bytes 442376 | tf_op jit(solution)/shard_map/ppermute | solution.py:463
  36.3 0.0 collective-permute-done.2.left
  36.3 1.3 %collective-permute-start.8 = (bf16[2,4,24,384]{3,2,1,0:T(8,128)(2,1)S(1)}, bf16[2,4,24,384]{3,2,1,0:T(8,128)(2,1)S(1)}, u32[]{:S(2)}, u32[]{:S(2)}) collective-permute-start(bf16[2,4,24,384]{3,2,1,0:T(8,128)(2,1)S(1)} %get-tuple-element.27), channel_id=1, source_target_pairs={{0,128},{1,129},{2,130},{3,131},{4,132},{5,133},{6,134},{7,135},{8... | collective-permute-start | bytes 442376 | tf_op jit(solution)/shard_map/ppermute | solution.py:463
  37.6 0.0 collective-permute-done.3.right
  37.6 0.0 collective-permute-done.7.top
  37.6 0.0 collective-permute-done.6.low
  37.6 1.5 %shard_map.112 = (bf16[400,384]{1,0:T(8,128)(2,1)S(1)}, bf16[2,144,3456]{2,1,0:T(8,128)(2,1)S(1)}, bf16[1536,1024]{1,0:T(8,128)(2,1)S(1)}) custom-call(s32[3]{0:T(128)S(1)} %pad_add_fusion.info, bf16[2,4,20,384]{3,2,1,0:T(8,128)(2,1)S(1)} %bitcast.24, bf16[368,384]{1,0:T(8,128)(2,1)S(1)} %collective-permute-done.below, ...), custom_call_target="tpu_custom_call" | custom-call | flops 2293235712 | bytes 1048576 | tf_op jit(solution)/shard_map/pallas_call | solution.py:407
  39.1 1.5 %collective-permute-start.10 = (bf16[400,384]{1,0:T(8,128)(2,1)S(1)}, bf16[400,384]{1,0:T(8,128)(2,1)S(1)}, u32[]{:S(2)}, u32[]{:S(2)}) collective-permute-start(bf16[400,384]{1,0:T(8,128)(2,1)S(1)} %get-tuple-element.25.lead), channel_id=1, source_target_pairs={{128,0},{129,1},{130,2},{131,3},{132,4},{133,5},{134,6},{135,7},{1... | collective-permute-start | bytes 921608 | tf_op jit(solution)/shard_map/ppermute | solution.py:488
  40.6 0.0 collective-permute-done.9.top
  40.6 1.9 %collective-permute-done.8.low = bf16[2,4,24,384]{3,2,1,0:T(8,128)(2,1)S(1)} collective-permute-done((bf16[2,4,24,384]{3,2,1,0:T(8,128)(2,1)S(1)}, bf16[2,4,24,384]{3,2,1,0:T(8,128)(2,1)S(1)}, u32[]{:S(2)}, u32[]{:S(2)}) %collective-permute-start.8) | collective-permute-done | bytes 147488 | tf_op jit(solution)/shard_map/ppermute | solution.py:463
  42.6 0.0 copy-start.2
  42.6 0.6 shard_map.114.main
  43.1 8.7 %collective-permute-done.10.returned = bf16[400,384]{1,0:T(8,128)(2,1)S(1)} collective-permute-done((bf16[400,384]{1,0:T(8,128)(2,1)S(1)}, bf16[400,384]{1,0:T(8,128)(2,1)S(1)}, u32[]{:S(2)}, u32[]{:S(2)}) %collective-permute-start.10) | collective-permute-done | bytes 307232 | tf_op jit(solution)/shard_map/ppermute | solution.py:488
  51.8 0.0 copy-done.2
  51.8 0.0 copy-done.4
  51.8 0.0 copy-done.7
  51.8 0.0 copy-done.8
  51.8 0.0 copy-done.9
  51.8 6.4 %shard_map.115 = bf16[2,8,40,192]{3,2,1,0:T(8,128)(2,1)} custom-call(s32[3]{0:T(128)S(1)} %pad_add_fusion.info, bf16[400,384]{1,0:T(8,128)(2,1)S(1)} %get-tuple-element.25.lead, bf16[288,384]{1,0:T(8,128)(2,1)S(1)} %shard_map.114.main, bf16[400,384]{1,0:T(8,128)(2,1)S(1)} %collective-permute-done.10.returned, bf16[2,8,40,192]{3,2,1,0:T(8,128)(2,1)S(1)} %copy-done.4, ...), custom_call_target="tpu_custom_call" | custom-call | flops 1528823808 | bytes 1048576 | tf_op jit(solution)/shard_map/pallas_call | solution.py:407
  (4 shorter events, 0.0 us)
Async XLA Ops:
  2.0 1.0 %copy-start.3 = (bf16[2,8,40,192]{3,2,1,0:T(8,128)(2,1)S(1)}, bf16[2,8,40,192]{3,2,1,0:T(8,128)(2,1)}, u32[]{:S(2)}) copy-start(bf16[2,8,40,192]{3,2,1,0:T(8,128)(2,1)} %cache.1) | copy-start | bytes 737284
  3.0 22.1 %copy-start = (bf16[1,3,3,3,384,384]{5,4,3,2,1,0:T(8,128)(2,1)S(1)}, bf16[1,3,3,3,384,384]{5,4,3,2,1,0:T(8,128)(2,1)}, u32[]{:S(2)}) copy-start(bf16[1,3,3,3,384,384]{5,4,3,2,1,0:T(8,128)(2,1)} %param.12) | copy-start | bytes 23887876
  3.6 7.2 %collective-permute-start = (bf16[368,384]{1,0:T(8,128)(2,1)S(1)}, bf16[368,384]{1,0:T(8,128)(2,1)S(1)}, u32[]{:S(2)}, u32[]{:S(2)}) collective-permute-start(bf16[368,384]{1,0:T(8,128)(2,1)S(1)} %get-tuple-element.18), channel_id=1, source_target_pairs={{0,112},{16,0},{32,16},{48,32},{64,48},{80,64},{96,80},{112,96},{1... | collective-permute-start | bytes 847880 | tf_op jit(solution)/shard_map/ppermute | solution.py:443
  4.3 20.8 %copy-start.5 = (f32[1,384]{1,0:T(1,128)S(1)}, f32[1,384]{1,0:T(1,128)}, u32[]{:S(2)}) copy-start(f32[1,384]{1,0:T(1,128)} %b.7) | copy-start | bytes 4612
  4.3 20.8 %copy-start.6 = (f32[1,384]{1,0:T(1,128)S(1)}, f32[1,384]{1,0:T(1,128)}, u32[]{:S(2)}) copy-start(f32[1,384]{1,0:T(1,128)} %g.7) | copy-start | bytes 4612
  4.3 0.8 %collective-permute-start.1 = (bf16[128,384]{1,0:T(8,128)(2,1)S(1)}, bf16[128,384]{1,0:T(8,128)(2,1)S(1)}, u32[]{:S(2)}, u32[]{:S(2)}) collective-permute-start(bf16[128,384]{1,0:T(8,128)(2,1)S(1)} %get-tuple-element.19), channel_id=1, source_target_pairs={{128,144},{129,145},{130,146},{131,147},{132,148},{133,149},{134,1... | collective-permute-start | bytes 294920 | tf_op jit(solution)/shard_map/ppermute | solution.py:444
  11.5 8.1 %collective-permute-start.4 = (bf16[112,384]{1,0:T(8,128)(2,1)S(1)}, bf16[112,384]{1,0:T(8,128)(2,1)S(1)}, u32[]{:S(2)}, u32[]{:S(2)}) collective-permute-start(bf16[112,384]{1,0:T(8,128)(2,1)S(1)} %get-tuple-element.22), channel_id=1, source_target_pairs={{0,1},{1,2},{2,3},{3,4},{4,5},{5,6},{6,7},{7,8},{8,9},{9,10},{10,1... | collective-permute-start | bytes 258056 | tf_op jit(solution)/shard_map/ppermute | solution.py:449
  16.2 8.8 %collective-permute-start.5 = (bf16[112,384]{1,0:T(8,128)(2,1)S(1)}, bf16[112,384]{1,0:T(8,128)(2,1)S(1)}, u32[]{:S(2)}, u32[]{:S(2)}) collective-permute-start(bf16[112,384]{1,0:T(8,128)(2,1)S(1)} %get-tuple-element.23), channel_id=1, source_target_pairs={{1,0},{2,1},{3,2},{4,3},{5,4},{6,5},{7,6},{8,7},{9,8},{10,9},{11,1... | collective-permute-start | bytes 258056 | tf_op jit(solution)/shard_map/ppermute | solution.py:449
  18.3 18.0 %collective-permute-start.2 = (bf16[48,384]{1,0:T(8,128)(2,1)S(1)}, bf16[48,384]{1,0:T(8,128)(2,1)S(1)}, u32[]{:S(2)}, u32[]{:S(2)}) collective-permute-start(bf16[48,384]{1,0:T(8,128)(2,1)S(1)} %get-tuple-element.20), channel_id=1, source_target_pairs={{128,129},{129,130},{130,131},{131,132},{132,133},{133,134},{134,1... | collective-permute-start | bytes 110600 | tf_op jit(solution)/shard_map/ppermute | solution.py:450
  19.0 18.6 %collective-permute-start.3 = (bf16[48,384]{1,0:T(8,128)(2,1)S(1)}, bf16[48,384]{1,0:T(8,128)(2,1)S(1)}, u32[]{:S(2)}, u32[]{:S(2)}) collective-permute-start(bf16[48,384]{1,0:T(8,128)(2,1)S(1)} %get-tuple-element.21), channel_id=1, source_target_pairs={{129,128},{130,129},{131,130},{132,131},{133,132},{134,133},{135,1... | collective-permute-start | bytes 110600 | tf_op jit(solution)/shard_map/ppermute | solution.py:450
  25.1 6.3 %copy-start.1 = (bf16[3,3,384,192]{2,3,1,0:T(8,128)(2,1)S(1)}, bf16[3,3,384,192]{2,3,1,0:T(8,128)(2,1)}, u32[]{:S(2)}) copy-start(bf16[3,3,384,192]{2,3,1,0:T(8,128)(2,1)} %param.16) | copy-start | bytes 3981316
  28.8 8.8 %collective-permute-start.7 = (bf16[2,4,24,384]{3,2,1,0:T(8,128)(2,1)S(1)}, bf16[2,4,24,384]{3,2,1,0:T(8,128)(2,1)S(1)}, u32[]{:S(2)}, u32[]{:S(2)}) collective-permute-start(bf16[2,4,24,384]{3,2,1,0:T(8,128)(2,1)S(1)} %get-tuple-element.24), channel_id=1, source_target_pairs={{112,128},{113,129},{114,130},{115,131},{116,132},{117,133},{118,1... | collective-permute-start | bytes 442376 | tf_op jit(solution)/shard_map/ppermute | solution.py:463
  30.1 7.5 %collective-permute-start.6 = (bf16[2,4,24,384]{3,2,1,0:T(8,128)(2,1)S(1)}, bf16[2,4,24,384]{3,2,1,0:T(8,128)(2,1)S(1)}, u32[]{:S(2)}, u32[]{:S(2)}) collective-permute-start(bf16[2,4,24,384]{3,2,1,0:T(8,128)(2,1)S(1)} %get-tuple-element.24), channel_id=1, source_target_pairs={{0,128},{1,129},{2,130},{3,131},{4,132},{5,133},{6,134},{7,135},{8... | collective-permute-start | bytes 442376 | tf_op jit(solution)/shard_map/ppermute | solution.py:463
  35.0 5.6 %collective-permute-start.9 = (bf16[2,4,24,384]{3,2,1,0:T(8,128)(2,1)S(1)}, bf16[2,4,24,384]{3,2,1,0:T(8,128)(2,1)S(1)}, u32[]{:S(2)}, u32[]{:S(2)}) collective-permute-start(bf16[2,4,24,384]{3,2,1,0:T(8,128)(2,1)S(1)} %get-tuple-element.27), channel_id=1, source_target_pairs={{112,128},{113,129},{114,130},{115,131},{116,132},{117,133},{118,1... | collective-permute-start | bytes 442376 | tf_op jit(solution)/shard_map/ppermute | solution.py:463
  36.3 6.3 %collective-permute-start.8 = (bf16[2,4,24,384]{3,2,1,0:T(8,128)(2,1)S(1)}, bf16[2,4,24,384]{3,2,1,0:T(8,128)(2,1)S(1)}, u32[]{:S(2)}, u32[]{:S(2)}) collective-permute-start(bf16[2,4,24,384]{3,2,1,0:T(8,128)(2,1)S(1)} %get-tuple-element.27), channel_id=1, source_target_pairs={{0,128},{1,129},{2,130},{3,131},{4,132},{5,133},{6,134},{7,135},{8... | collective-permute-start | bytes 442376 | tf_op jit(solution)/shard_map/ppermute | solution.py:463
  39.1 12.7 %collective-permute-start.10 = (bf16[400,384]{1,0:T(8,128)(2,1)S(1)}, bf16[400,384]{1,0:T(8,128)(2,1)S(1)}, u32[]{:S(2)}, u32[]{:S(2)}) collective-permute-start(bf16[400,384]{1,0:T(8,128)(2,1)S(1)} %get-tuple-element.25.lead), channel_id=1, source_target_pairs={{128,0},{129,1},{130,2},{131,3},{132,4},{133,5},{134,6},{135,7},{1... | collective-permute-start | bytes 921608 | tf_op jit(solution)/shard_map/ppermute | solution.py:488
  42.6 9.2 %copy-start.2 = (bf16[3,3,3,192,192]{4,3,2,1,0:T(8,128)(2,1)S(1)}, bf16[3,3,3,192,192]{4,3,2,1,0:T(8,128)(2,1)}, u32[]{:S(2)}) copy-start(bf16[3,3,3,192,192]{4,3,2,1,0:T(8,128)(2,1)} %param.20) | copy-start | bytes 5971972
  42.6 9.2 %copy-start.4 = (bf16[2,8,40,192]{3,2,1,0:T(8,128)(2,1)S(1)}, bf16[2,8,40,192]{3,2,1,0:T(8,128)(2,1)}, u32[]{:S(2)}) copy-start(bf16[2,8,40,192]{3,2,1,0:T(8,128)(2,1)} %cache.1) | copy-start | bytes 737284
  42.6 9.2 %copy-start.7 = (f32[192]{0:T(256)S(1)}, f32[192]{0:T(256)}, u32[]{:S(2)}) copy-start(f32[192]{0:T(256)} %param.17) | copy-start | bytes 2308
  42.6 9.2 %copy-start.8 = (f32[192]{0:T(256)S(1)}, f32[192]{0:T(256)}, u32[]{:S(2)}) copy-start(f32[192]{0:T(256)} %param.18) | copy-start | bytes 2308
  42.6 9.2 %copy-start.9 = (f32[192]{0:T(256)S(1)}, f32[192]{0:T(256)}, u32[]{:S(2)}) copy-start(f32[192]{0:T(256)} %param.21) | copy-start | bytes 2308

commit v4 on v3

--- a/solution.py
+++ b/solution.py
@@ -42,33 +42,36 @@
     return jnp.concatenate([first.astype(F32), second.astype(F32)], axis=1)
 
 
-def pack_rows(info, latent, cache, fine, to_above, to_below, side):
-    def put(at, line):
-        side[at : at + line.shape[0]] = line.astype(F32)
-
+def pack_rows(info, latent, cache, to_above, side):
     for f in range(2):
         for row in range(3):
-            put(((4 + f) * 3 + row) * COLS, cache[f, row])
+            at = ((4 + f) * 3 + row) * COLS
+            side[at : at + COLS] = cache[f, row].astype(F32)
 
     @pl.when(info[0] == 0)
     def _():
         for f in range(4):
             for row in range(3):
-                put((f * 3 + row) * COLS, latent[f, row])
-        to_above[...] = side[...].astype(BF16)
-
+                at = (f * 3 + row) * COLS
+                side[at : at + COLS] = latent[f, row].astype(F32)
+
+    to_above[...] = side[...].astype(BF16)
+
+
+def pack_caches(info, cache, fine, _, to_below, fine_up, side):
     @pl.when(info[0] == 1)
     def _():
-        put(0, frame_pair(fine[0, 0], fine[1, 0]))
-        to_above[...] = side[...].astype(BF16)
         for f in range(2):
             for row in range(2):
-                put((f * 2 + row) * COLS, cache[f, 2 + row])
-        put(80, frame_pair(fine[0, 7], fine[1, 7]))
-        to_below[...] = side[0:128].astype(BF16)
-
-
-def pack_columns(info, latent, cache, fine, below, above, left_0, right_0, left_1, right_1, far, side):
+                at = (f * 2 + row) * COLS
+                side[at : at + COLS] = cache[f, 2 + row].astype(F32)
+        side[80:120] = frame_pair(fine[0, 7], fine[1, 7])
+        to_below[...] = side[...].astype(BF16)
+        side[0:40] = frame_pair(fine[0, 0], fine[1, 0])
+        fine_up[...] = side[0:48].astype(BF16)
+
+
+def pack_columns(info, latent, cache, fine, below, above, under, left_0, right_0, left_1, right_1, far, side):
     far[0] = below[...].astype(F32)
 
     @pl.when(info[0] == 0)
@@ -90,6 +93,7 @@
     @pl.when(info[0] == 1)
     def _():
         far[1, 0:128] = above[...].astype(F32)
+        far[1, 128:176] = under[...].astype(F32)
         for t in range(2):
             for u in range(8):
                 if 2 <= u < 6:
@@ -106,7 +110,7 @@
                 line = frame_pair(fine[0, e - 1], fine[1, e - 1])
                 first, final = line[0:1], line[39:40]
             else:
-                k, base = (1, 80) if e == 0 else (0, 0)
+                k, base = (1, 80) if e == 0 else (1, 128)
                 first, final = far[k, base : base + 1], far[k, base + 39 : base + 40]
             side[0, 32 + e : 33 + e] = first
             side[1, 32 + e : 33 + e] = final
@@ -210,7 +214,8 @@
         stores = stores[2:] + stores[:2]
     first, last = info[1] == 0, info[1] == N_HA - 1
     if caches is not None:
-        cache, below, above, left, right = caches
+        cache, below, above, under, left, right = caches
+        far[1, 128:176] = under[...].astype(F32)
         side[0, 0:48] = left[...].astype(F32)
         side[1, 0:48] = right[...].astype(F32)
         far[0] = below[...].astype(F32)
@@ -261,16 +266,16 @@
             out[at : at + PITCH] = jnp.where(fits, value, 0.0).astype(BF16)
 
 
-def second_early(info, cache, below, above, left, right, low, top, w, b, g, w_up_hbm, out, kept, folded, *scratch):
+def second_early(info, cache, below, above, under, left, right, low, top, w, b, g, w_up_hbm, out, kept, folded, *scratch):
     *scratch, ring, w_up, sems = scratch
 
     @pl.when(info[0] == 1)
     def _():
-        second_section(info, (cache, below, above, left, right), (low, top), w, b, g, out, kept, *scratch)
+        second_section(info, (cache, below, above, under, left, right), (low, top), w, b, g, out, kept, *scratch)
         first, last = info[1] == 0, info[1] == N_HA - 1
         side, far = scratch[2:4]
         ring[...] = jnp.zeros((112, CM), F32)
-        for at, e, line, hide in ((0, 0, far[1, 80:120], first), (48, 9, far[0, 0:40], last)):
+        for at, e, line, hide in ((0, 0, far[1, 80:120], first), (48, 9, far[1, 128:168], last)):
             ring[at : at + 1] = jnp.where(hide, 0.0, side[0, 32 + e : 33 + e])
             ring[at + 1 : at + 41] = jnp.where(hide, 0.0, line)
             ring[at + 41 : at + 42] = jnp.where(hide, 0.0, side[1, 32 + e : 33 + e])
@@ -437,14 +442,17 @@
     cache = cache_mid[0]
     side = pltpu.VMEM((2, 112, CM), F32)
     far = lambda count: pltpu.VMEM((count, 368, CM) if count > 1 else (368, CM), F32)
-    to_above, to_below = call(
-        pack_rows, "svvv", [(368, CM), (128, CM)], [far(1)], info, latent, cache, cache_fine, megabytes=3
-    )
+    (to_above,) = call(pack_rows, "svv", [(368, CM)], [far(1)], info, latent, cache, megabytes=3)
     below = lax.ppermute(to_above, "ha", [(i, (i - 1) % N_HA) for i in range(N_HA)])
+    to_below, fine_up = call(
+        pack_caches, "svvv", [(128, CM), (48, CM)], [pltpu.VMEM((128, CM), F32)], info, cache, cache_fine, to_above,
+        megabytes=3,
+    )
     above = lax.ppermute(to_below, AXES, pairs_between(1, 1, 1, 0))
+    under = lax.ppermute(fine_up, AXES, pairs_between(1, 1, -1, 0))
     sides = call(
-        pack_columns, "svvvvv", [(112, CM)] * 2 + [(48, CM)] * 2, [far(2), side],
-        info, latent, cache, cache_fine, below, above, megabytes=3, flops=2 * 10**9,
+        pack_columns, "svvvvvv", [(112, CM)] * 2 + [(48, CM)] * 2, [far(2), side],
+        info, latent, cache, cache_fine, below, above, under, megabytes=3, flops=2 * 10**9,
     )
     right_0, left_0 = (lax.ppermute(sides[k], AXES, pairs_between(0, 0, 0, 2 * k - 1)) for k in range(2))
     right_1, left_1 = (lax.ppermute(sides[2 + k], AXES, pairs_between(1, 1, 0, 2 * k - 1)) for k in range(2))
@@ -481,9 +489,9 @@
     ]
     second_flops = 2 * 288 * 27 * CM * CM
     second_a, kept, folded_0 = call(
-        second_early, "svvvvvvvvvvh", [(RING + 112, CM), (2, 144, 9 * CM), folded_shape],
+        second_early, "svvvvvvvvvvvh", [(RING + 112, CM), (2, 144, 9 * CM), folded_shape],
         second_scratch + [pltpu.VMEM((112, CM), F32)] + up_scratch,
-        info, cache, below, above, left_1, right_1, *group_a, kernel, b_mid, g_mid, up_kernel, flops=second_flops, megabytes=16,
+        info, cache, below, above, under, left_1, right_1, *group_a, kernel, b_mid, g_mid, up_kernel, flops=second_flops, megabytes=16,
     )
     returned = lax.ppermute(second_a, "segment", [(1, 0)])
     (second_b,) = call(

time: 58.7 us -> 57.6 us (0.981)
  waiting for transfers between devices: 21.8 us -> 19.4 us
  starting transfers between devices: 16.3 us -> 17.1 us
    ppermute x1, waiting for transfers between devices: 5.74 us -> 3.37 us  [shards(): lax.ppermute(to_above, 'ha', [(i, (i - 1) % N_HA) for i in range(N_HA)])]
    ppermute x0 -> x1, starting transfers between devices: none -> 0.8 us  [shards(): under = lax.ppermute(fine_up, AXES, pairs_between(1, 1, -1, 0))]
    pallas_call x7 -> x8, Pallas kernels: 17 us -> 17.3 us  [call(): pl.pallas_call(body, out_shape=[jax.ShapeDtypeStruct(shape, BF16) for sha...]
  transfers between devices with their start and end apart: 11 -> 12, of which waited for: 4 -> 4; matrix products, arithmetic and copies ran while one was open for 0% -> 0% of each run, Pallas kernels for 16% -> 17%
where the time goes in v4:
time: 57.6 us; the launch traced here: 57.2 us
  waiting for transfers between devices  19.4 us (34%)
  Pallas kernels  17.3 us (30%)
  starting transfers between devices  17.1 us (30%)
  local copies, waits for them, and re-layouts  2.92 us (5%)
    pallas_call x8, Pallas kernels, call(): pl.pallas_call(body, out_shape=[jax.ShapeDtypeStruct(shape, BF16) for sha...  17.3 us
    ppermute x1, waiting for transfers between devices, shards(): returned = lax.ppermute(second_a, 'segment', [(1, 0)])  8.57 us
    ppermute x2, starting transfers between devices, shards(): lax.ppermute(sides[k], AXES, pairs_between(0, 0, 0, 2 * k - 1))  6.79 us
    ppermute x2, waiting for transfers between devices, shards(): lax.ppermute(sides[k], AXES, pairs_between(0, 0, 0, 2 * k - 1))  5.4 us
    ppermute x4, starting transfers between devices, shards(): lax.ppermute(tile, AXES, pairs_between(0, 1, dh, 0, True))  5.19 us
    ppermute x1, waiting for transfers between devices, shards(): lax.ppermute(to_above, 'ha', [(i, (i - 1) % N_HA) for i in range(N_HA)])  3.37 us
    unnamed x22, local copies, waits for them, and re-layouts  2.92 us
    ppermute x4, waiting for transfers between devices, shards(): lax.ppermute(tile, AXES, pairs_between(0, 1, dh, 0, True))  2.08 us
  transfers between devices with their start and end apart: 12, of which 4 were waited for; matrix products, arithmetic and copies ran while one was open for 0% of the time, Pallas kernels for 17%

profile of v4, /device:TPU:125, one launch (start us, length us, event | category | flops | bytes accessed | tf_op | source)
XLA Modules:
  0.0 57.2 jit_solution(12203258658304963352)
XLA Ops:
  0.0 0.9 %copy.18 = bf16[1,2,4,20,384]{4,3,2,1,0:T(8,128)(2,1)S(1)} copy(bf16[1,2,4,20,384]{4,2,3,1,0:T(4,128)(2,1)} %param.15) | data formatting | bytes 245760 | tf_op args[4]
  0.9 1.0 %copy.13.latent = bf16[4,4,20,384]{3,2,1,0:T(8,128)(2,1)S(1)} copy(bf16[4,4,20,384]{3,1,2,0:T(4,128)(2,1)} %param.11) | data formatting | bytes 491520 | tf_op args[0]
  1.9 0.1 pad_add_fusion.info
  2.0 0.6 %shard_map.109._ = bf16[368,384]{1,0:T(8,128)(2,1)S(1)} custom-call(s32[3]{0:T(128)S(1)} %pad_add_fusion.info, bf16[4,4,20,384]{3,2,1,0:T(8,128)(2,1)S(1)} %copy.13.latent, bf16[2,4,20,384]{3,2,1,0:T(8,128)(2,1)S(1)} %bitcast.20), custom_call_target="tpu_custom_call" | custom-call | bytes 1048576 | tf_op jit(solution)/shard_map/pallas_call | solution.py:412
  2.6 0.7 %collective-permute-start = (bf16[368,384]{1,0:T(8,128)(2,1)S(1)}, bf16[368,384]{1,0:T(8,128)(2,1)S(1)}, u32[]{:S(2)}, u32[]{:S(2)}) collective-permute-start(bf16[368,384]{1,0:T(8,128)(2,1)S(1)} %shard_map.109._), channel_id=1, source_target_pairs={{0,112},{16,0},{32,16},{48,32},{64,48},{80,64},{96,80},{112,96},{1... | collective-permute-start | bytes 847880 | tf_op jit(solution)/shard_map/ppermute | solution.py:446
  3.3 1.0 %copy-done.3 = bf16[2,8,40,192]{3,2,1,0:T(8,128)(2,1)S(1)} copy-done((bf16[2,8,40,192]{3,2,1,0:T(8,128)(2,1)S(1)}, bf16[2,8,40,192]{3,2,1,0:T(8,128)(2,1)}, u32[]{:S(2)}) %copy-start.3) | copy-done | bytes 245784
  4.3 0.5 shard_map.110
  4.8 0.8 %collective-permute-start.1 = (bf16[128,384]{1,0:T(8,128)(2,1)S(1)}, bf16[128,384]{1,0:T(8,128)(2,1)S(1)}, u32[]{:S(2)}, u32[]{:S(2)}) collective-permute-start(bf16[128,384]{1,0:T(8,128)(2,1)S(1)} %get-tuple-element.18), channel_id=1, source_target_pairs={{128,144},{129,145},{130,146},{131,147},{132,148},{133,149},{134,1... | collective-permute-start | bytes 294920 | tf_op jit(solution)/shard_map/ppermute | solution.py:451
  5.6 0.0 copy-start.5
  5.7 0.0 copy-start.6
  5.7 0.8 %collective-permute-start.2 = (bf16[48,384]{1,0:T(8,128)(2,1)S(1)}, bf16[48,384]{1,0:T(8,128)(2,1)S(1)}, u32[]{:S(2)}, u32[]{:S(2)}) collective-permute-start(bf16[48,384]{1,0:T(8,128)(2,1)S(1)} %get-tuple-element.19), channel_id=1, source_target_pairs={{144,128},{145,129},{146,130},{147,131},{148,132},{149,133},{150,1... | collective-permute-start | bytes 110600 | tf_op jit(solution)/shard_map/ppermute | solution.py:452
  6.5 0.0 collective-permute-done.2.under
  6.5 0.0 collective-permute-done.1.above
  6.5 3.4 %collective-permute-done.below = bf16[368,384]{1,0:T(8,128)(2,1)S(1)} collective-permute-done((bf16[368,384]{1,0:T(8,128)(2,1)S(1)}, bf16[368,384]{1,0:T(8,128)(2,1)S(1)}, u32[]{:S(2)}, u32[]{:S(2)}) %collective-permute-start) | collective-permute-done | bytes 282656 | tf_op jit(solution)/shard_map/ppermute | solution.py:446
  9.9 0.7 %shard_map.111 = (bf16[112,384]{1,0:T(8,128)(2,1)S(1)}, bf16[112,384]{1,0:T(8,128)(2,1)S(1)}, bf16[48,384]{1,0:T(8,128)(2,1)S(1)}, bf16[48,384]{1,0:T(8,128)(2,1)S(1)}) custom-call(s32[3]{0:T(128)S(1)} %pad_add_fusion.info, bf16[4,4,20,384]{3,2,1,0:T(8,128)(2,1)S(1)} %copy.13.latent, bf16[2,4,20,384]{3,2,1,0:T(8,128)(2,1)S(1)} %bitcast.22, ...), custom_call_target="tpu_custom_call" | custom-call | flops 2000000000 | bytes 1048576 | tf_op jit(solution)/shard_map/pallas_call | solution.py:412
  10.5 4.7 %collective-permute-start.5 = (bf16[112,384]{1,0:T(8,128)(2,1)S(1)}, bf16[112,384]{1,0:T(8,128)(2,1)S(1)}, u32[]{:S(2)}, u32[]{:S(2)}) collective-permute-start(bf16[112,384]{1,0:T(8,128)(2,1)S(1)} %get-tuple-element.22), channel_id=1, source_target_pairs={{0,1},{1,2},{2,3},{3,4},{4,5},{5,6},{6,7},{7,8},{8,9},{9,10},{10,1... | collective-permute-start | bytes 258056 | tf_op jit(solution)/shard_map/ppermute | solution.py:457
  15.2 2.1 %collective-permute-start.6 = (bf16[112,384]{1,0:T(8,128)(2,1)S(1)}, bf16[112,384]{1,0:T(8,128)(2,1)S(1)}, u32[]{:S(2)}, u32[]{:S(2)}) collective-permute-start(bf16[112,384]{1,0:T(8,128)(2,1)S(1)} %get-tuple-element.23), channel_id=1, source_target_pairs={{1,0},{2,1},{3,2},{4,3},{5,4},{6,5},{7,6},{8,7},{9,8},{10,9},{11,1... | collective-permute-start | bytes 258056 | tf_op jit(solution)/shard_map/ppermute | solution.py:457
  17.3 0.7 %collective-permute-start.3 = (bf16[48,384]{1,0:T(8,128)(2,1)S(1)}, bf16[48,384]{1,0:T(8,128)(2,1)S(1)}, u32[]{:S(2)}, u32[]{:S(2)}) collective-permute-start(bf16[48,384]{1,0:T(8,128)(2,1)S(1)} %get-tuple-element.20), channel_id=1, source_target_pairs={{128,129},{129,130},{130,131},{131,132},{132,133},{133,134},{134,1... | collective-permute-start | bytes 110600 | tf_op jit(solution)/shard_map/ppermute | solution.py:458
  18.0 0.7 %collective-permute-start.4 = (bf16[48,384]{1,0:T(8,128)(2,1)S(1)}, bf16[48,384]{1,0:T(8,128)(2,1)S(1)}, u32[]{:S(2)}, u32[]{:S(2)}) collective-permute-start(bf16[48,384]{1,0:T(8,128)(2,1)S(1)} %get-tuple-element.21), channel_id=1, source_target_pairs={{129,128},{130,129},{131,130},{132,131},{133,132},{134,133},{135,1... | collective-permute-start | bytes 110600 | tf_op jit(solution)/shard_map/ppermute | solution.py:458
  18.7 0.0 collective-permute-done.5.left
  18.7 5.4 %collective-permute-done.6.right = bf16[112,384]{1,0:T(8,128)(2,1)S(1)} collective-permute-done((bf16[112,384]{1,0:T(8,128)(2,1)S(1)}, bf16[112,384]{1,0:T(8,128)(2,1)S(1)}, u32[]{:S(2)}, u32[]{:S(2)}) %collective-permute-start.6) | collective-permute-done | bytes 86048 | tf_op jit(solution)/shard_map/ppermute | solution.py:457
  24.1 0.0 copy-done
  24.1 0.0 copy-done.5
  24.1 0.0 copy-done.6
  24.1 0.0 copy-start.1
  24.1 3.6 %shard_map.112 = (bf16[2,4,24,384]{3,2,1,0:T(8,128)(2,1)S(1)}, bf16[2,112,3456]{2,1,0:T(8,128)(2,1)S(1)}) custom-call(s32[3]{0:T(128)S(1)} %pad_add_fusion.info, bf16[4,4,20,384]{3,2,1,0:T(8,128)(2,1)S(1)} %copy.13.latent, bf16[2,4,20,384]{3,2,1,0:T(8,128)(2,1)S(1)} %bitcast.23, bf16[368,384]{1,0:T(8,128)(2,1)S(1)} %collective-permute-done.below, ...), custom_call_target="tpu_custom_call" | custom-call | flops 1783627776 | bytes 1048576 | tf_op jit(solution)/shard_map/pallas_call | solution.py:412
  27.7 1.3 %collective-permute-start.8 = (bf16[2,4,24,384]{3,2,1,0:T(8,128)(2,1)S(1)}, bf16[2,4,24,384]{3,2,1,0:T(8,128)(2,1)S(1)}, u32[]{:S(2)}, u32[]{:S(2)}) collective-permute-start(bf16[2,4,24,384]{3,2,1,0:T(8,128)(2,1)S(1)} %get-tuple-element.24), channel_id=1, source_target_pairs={{112,128},{113,129},{114,130},{115,131},{116,132},{117,133},{118,1... | collective-permute-start | bytes 442376 | tf_op jit(solution)/shard_map/ppermute | solution.py:471
  29.0 1.3 %collective-permute-start.7 = (bf16[2,4,24,384]{3,2,1,0:T(8,128)(2,1)S(1)}, bf16[2,4,24,384]{3,2,1,0:T(8,128)(2,1)S(1)}, u32[]{:S(2)}, u32[]{:S(2)}) collective-permute-start(bf16[2,4,24,384]{3,2,1,0:T(8,128)(2,1)S(1)} %get-tuple-element.24), channel_id=1, source_target_pairs={{0,128},{1,129},{2,130},{3,131},{4,132},{5,133},{6,134},{7,135},{8... | collective-permute-start | bytes 442376 | tf_op jit(solution)/shard_map/ppermute | solution.py:471
  30.3 0.0 copy-done.1
  30.3 3.4 %shard_map.114 = (bf16[2,4,24,384]{3,2,1,0:T(8,128)(2,1)S(1)}, bf16[1536,1024]{1,0:T(8,128)(2,1)S(1)}) custom-call(s32[3]{0:T(128)S(1)} %pad_add_fusion.info, bf16[4,4,20,384]{3,2,1,0:T(8,128)(2,1)S(1)} %copy.13.latent, bf16[368,384]{1,0:T(8,128)(2,1)S(1)} %collective-permute-done.below, bf16[112,384]{1,0:T(8,128)(2,1)S(1)} %collective-permute-done.5.left, ...), custom_call_target="tpu_custom_call" | custom-call | flops 1783627776 | bytes 1048576 | tf_op jit(solution)/shard_map/pallas_call | solution.py:412
  33.7 1.3 %collective-permute-start.10 = (bf16[2,4,24,384]{3,2,1,0:T(8,128)(2,1)S(1)}, bf16[2,4,24,384]{3,2,1,0:T(8,128)(2,1)S(1)}, u32[]{:S(2)}, u32[]{:S(2)}) collective-permute-start(bf16[2,4,24,384]{3,2,1,0:T(8,128)(2,1)S(1)} %get-tuple-element.27), channel_id=1, source_target_pairs={{112,128},{113,129},{114,130},{115,131},{116,132},{117,133},{118,1... | collective-permute-start | bytes 442376 | tf_op jit(solution)/shard_map/ppermute | solution.py:471
  35.0 0.0 collective-permute-done.3.left
  35.1 1.3 %collective-permute-start.9 = (bf16[2,4,24,384]{3,2,1,0:T(8,128)(2,1)S(1)}, bf16[2,4,24,384]{3,2,1,0:T(8,128)(2,1)S(1)}, u32[]{:S(2)}, u32[]{:S(2)}) collective-permute-start(bf16[2,4,24,384]{3,2,1,0:T(8,128)(2,1)S(1)} %get-tuple-element.27), channel_id=1, source_target_pairs={{0,128},{1,129},{2,130},{3,131},{4,132},{5,133},{6,134},{7,135},{8... | collective-permute-start | bytes 442376 | tf_op jit(solution)/shard_map/ppermute | solution.py:471
  36.4 0.0 collective-permute-done.4.right
  36.4 0.0 collective-permute-done.8.top
  36.4 0.0 collective-permute-done.7.low
  36.4 1.5 %shard_map.113 = (bf16[400,384]{1,0:T(8,128)(2,1)S(1)}, bf16[2,144,3456]{2,1,0:T(8,128)(2,1)S(1)}, bf16[1536,1024]{1,0:T(8,128)(2,1)S(1)}) custom-call(s32[3]{0:T(128)S(1)} %pad_add_fusion.info, bf16[2,4,20,384]{3,2,1,0:T(8,128)(2,1)S(1)} %bitcast.24, bf16[368,384]{1,0:T(8,128)(2,1)S(1)} %collective-permute-done.below, ...), custom_call_target="tpu_custom_call" | custom-call | flops 2293235712 | bytes 1048576 | tf_op jit(solution)/shard_map/pallas_call | solution.py:412
  37.9 1.5 %collective-permute-start.11 = (bf16[400,384]{1,0:T(8,128)(2,1)S(1)}, bf16[400,384]{1,0:T(8,128)(2,1)S(1)}, u32[]{:S(2)}, u32[]{:S(2)}) collective-permute-start(bf16[400,384]{1,0:T(8,128)(2,1)S(1)} %get-tuple-element.25.lead), channel_id=1, source_target_pairs={{128,0},{129,1},{130,2},{131,3},{132,4},{133,5},{134,6},{135,7},{1... | collective-permute-start | bytes 921608 | tf_op jit(solution)/shard_map/ppermute | solution.py:496
  39.4 0.0 collective-permute-done.10.top
  39.4 2.1 %collective-permute-done.9.low = bf16[2,4,24,384]{3,2,1,0:T(8,128)(2,1)S(1)} collective-permute-done((bf16[2,4,24,384]{3,2,1,0:T(8,128)(2,1)S(1)}, bf16[2,4,24,384]{3,2,1,0:T(8,128)(2,1)S(1)}, u32[]{:S(2)}, u32[]{:S(2)}) %collective-permute-start.9) | collective-permute-done | bytes 147488 | tf_op jit(solution)/shard_map/ppermute | solution.py:471
  41.5 0.6 shard_map.115.main
  42.0 8.6 %collective-permute-done.11.returned = bf16[400,384]{1,0:T(8,128)(2,1)S(1)} collective-permute-done((bf16[400,384]{1,0:T(8,128)(2,1)S(1)}, bf16[400,384]{1,0:T(8,128)(2,1)S(1)}, u32[]{:S(2)}, u32[]{:S(2)}) %collective-permute-start.11) | collective-permute-done | bytes 307232 | tf_op jit(solution)/shard_map/ppermute | solution.py:496
  50.6 0.0 copy-done.2
  50.6 0.0 copy-done.4
  50.6 0.0 copy-done.7
  50.6 0.0 copy-done.8
  50.6 0.0 copy-done.9
  50.6 6.4 %shard_map.116 = bf16[2,8,40,192]{3,2,1,0:T(8,128)(2,1)} custom-call(s32[3]{0:T(128)S(1)} %pad_add_fusion.info, bf16[400,384]{1,0:T(8,128)(2,1)S(1)} %get-tuple-element.25.lead, bf16[288,384]{1,0:T(8,128)(2,1)S(1)} %shard_map.115.main, bf16[400,384]{1,0:T(8,128)(2,1)S(1)} %collective-permute-done.11.returned, bf16[2,8,40,192]{3,2,1,0:T(8,128)(2,1)S(1)} %copy-done.4, ...), custom_call_target="tpu_custom_call" | custom-call | flops 1528823808 | bytes 1048576 | tf_op jit(solution)/shard_map/pallas_call | solution.py:412
  (7 shorter events, 0.0 us)
Async XLA Ops:
  2.6 7.2 %collective-permute-start = (bf16[368,384]{1,0:T(8,128)(2,1)S(1)}, bf16[368,384]{1,0:T(8,128)(2,1)S(1)}, u32[]{:S(2)}, u32[]{:S(2)}) collective-permute-start(bf16[368,384]{1,0:T(8,128)(2,1)S(1)} %shard_map.109._), channel_id=1, source_target_pairs={{0,112},{16,0},{32,16},{48,32},{64,48},{80,64},{96,80},{112,96},{1... | collective-permute-start | bytes 847880 | tf_op jit(solution)/shard_map/ppermute | solution.py:446
  3.3 1.0 %copy-start.3 = (bf16[2,8,40,192]{3,2,1,0:T(8,128)(2,1)S(1)}, bf16[2,8,40,192]{3,2,1,0:T(8,128)(2,1)}, u32[]{:S(2)}) copy-start(bf16[2,8,40,192]{3,2,1,0:T(8,128)(2,1)} %cache.1) | copy-start | bytes 737284
  4.3 19.8 %copy-start = (bf16[1,3,3,3,384,384]{5,4,3,2,1,0:T(8,128)(2,1)S(1)}, bf16[1,3,3,3,384,384]{5,4,3,2,1,0:T(8,128)(2,1)}, u32[]{:S(2)}) copy-start(bf16[1,3,3,3,384,384]{5,4,3,2,1,0:T(8,128)(2,1)} %param.12) | copy-start | bytes 23887876
  4.8 1.6 %collective-permute-start.1 = (bf16[128,384]{1,0:T(8,128)(2,1)S(1)}, bf16[128,384]{1,0:T(8,128)(2,1)S(1)}, u32[]{:S(2)}, u32[]{:S(2)}) collective-permute-start(bf16[128,384]{1,0:T(8,128)(2,1)S(1)} %get-tuple-element.18), channel_id=1, source_target_pairs={{128,144},{129,145},{130,146},{131,147},{132,148},{133,149},{134,1... | collective-permute-start | bytes 294920 | tf_op jit(solution)/shard_map/ppermute | solution.py:451
  5.6 18.4 %copy-start.5 = (f32[1,384]{1,0:T(1,128)S(1)}, f32[1,384]{1,0:T(1,128)}, u32[]{:S(2)}) copy-start(f32[1,384]{1,0:T(1,128)} %b.7) | copy-start | bytes 4612
  5.7 18.4 %copy-start.6 = (f32[1,384]{1,0:T(1,128)S(1)}, f32[1,384]{1,0:T(1,128)}, u32[]{:S(2)}) copy-start(f32[1,384]{1,0:T(1,128)} %g.7) | copy-start | bytes 4612
  5.7 0.8 %collective-permute-start.2 = (bf16[48,384]{1,0:T(8,128)(2,1)S(1)}, bf16[48,384]{1,0:T(8,128)(2,1)S(1)}, u32[]{:S(2)}, u32[]{:S(2)}) collective-permute-start(bf16[48,384]{1,0:T(8,128)(2,1)S(1)} %get-tuple-element.19), channel_id=1, source_target_pairs={{144,128},{145,129},{146,130},{147,131},{148,132},{149,133},{150,1... | collective-permute-start | bytes 110600 | tf_op jit(solution)/shard_map/ppermute | solution.py:452
  10.5 8.1 %collective-permute-start.5 = (bf16[112,384]{1,0:T(8,128)(2,1)S(1)}, bf16[112,384]{1,0:T(8,128)(2,1)S(1)}, u32[]{:S(2)}, u32[]{:S(2)}) collective-permute-start(bf16[112,384]{1,0:T(8,128)(2,1)S(1)} %get-tuple-element.22), channel_id=1, source_target_pairs={{0,1},{1,2},{2,3},{3,4},{4,5},{5,6},{6,7},{7,8},{8,9},{9,10},{10,1... | collective-permute-start | bytes 258056 | tf_op jit(solution)/shard_map/ppermute | solution.py:457
  15.2 8.8 %collective-permute-start.6 = (bf16[112,384]{1,0:T(8,128)(2,1)S(1)}, bf16[112,384]{1,0:T(8,128)(2,1)S(1)}, u32[]{:S(2)}, u32[]{:S(2)}) collective-permute-start(bf16[112,384]{1,0:T(8,128)(2,1)S(1)} %get-tuple-element.23), channel_id=1, source_target_pairs={{1,0},{2,1},{3,2},{4,3},{5,4},{6,5},{7,6},{8,7},{9,8},{10,9},{11,1... | collective-permute-start | bytes 258056 | tf_op jit(solution)/shard_map/ppermute | solution.py:457
  17.3 17.7 %collective-permute-start.3 = (bf16[48,384]{1,0:T(8,128)(2,1)S(1)}, bf16[48,384]{1,0:T(8,128)(2,1)S(1)}, u32[]{:S(2)}, u32[]{:S(2)}) collective-permute-start(bf16[48,384]{1,0:T(8,128)(2,1)S(1)} %get-tuple-element.20), channel_id=1, source_target_pairs={{128,129},{129,130},{130,131},{131,132},{132,133},{133,134},{134,1... | collective-permute-start | bytes 110600 | tf_op jit(solution)/shard_map/ppermute | solution.py:458
  18.0 18.4 %collective-permute-start.4 = (bf16[48,384]{1,0:T(8,128)(2,1)S(1)}, bf16[48,384]{1,0:T(8,128)(2,1)S(1)}, u32[]{:S(2)}, u32[]{:S(2)}) collective-permute-start(bf16[48,384]{1,0:T(8,128)(2,1)S(1)} %get-tuple-element.21), channel_id=1, source_target_pairs={{129,128},{130,129},{131,130},{132,131},{133,132},{134,133},{135,1... | collective-permute-start | bytes 110600 | tf_op jit(solution)/shard_map/ppermute | solution.py:458
  24.1 6.2 %copy-start.1 = (bf16[3,3,384,192]{2,3,1,0:T(8,128)(2,1)S(1)}, bf16[3,3,384,192]{2,3,1,0:T(8,128)(2,1)}, u32[]{:S(2)}) copy-start(bf16[3,3,384,192]{2,3,1,0:T(8,128)(2,1)} %param.16) | copy-start | bytes 3981316
  27.7 8.7 %collective-permute-start.8 = (bf16[2,4,24,384]{3,2,1,0:T(8,128)(2,1)S(1)}, bf16[2,4,24,384]{3,2,1,0:T(8,128)(2,1)S(1)}, u32[]{:S(2)}, u32[]{:S(2)}) collective-permute-start(bf16[2,4,24,384]{3,2,1,0:T(8,128)(2,1)S(1)} %get-tuple-element.24), channel_id=1, source_target_pairs={{112,128},{113,129},{114,130},{115,131},{116,132},{117,133},{118,1... | collective-permute-start | bytes 442376 | tf_op jit(solution)/shard_map/ppermute | solution.py:471
  29.0 7.4 %collective-permute-start.7 = (bf16[2,4,24,384]{3,2,1,0:T(8,128)(2,1)S(1)}, bf16[2,4,24,384]{3,2,1,0:T(8,128)(2,1)S(1)}, u32[]{:S(2)}, u32[]{:S(2)}) collective-permute-start(bf16[2,4,24,384]{3,2,1,0:T(8,128)(2,1)S(1)} %get-tuple-element.24), channel_id=1, source_target_pairs={{0,128},{1,129},{2,130},{3,131},{4,132},{5,133},{6,134},{7,135},{8... | collective-permute-start | bytes 442376 | tf_op jit(solution)/shard_map/ppermute | solution.py:471
  33.7 5.6 %collective-permute-start.10 = (bf16[2,4,24,384]{3,2,1,0:T(8,128)(2,1)S(1)}, bf16[2,4,24,384]{3,2,1,0:T(8,128)(2,1)S(1)}, u32[]{:S(2)}, u32[]{:S(2)}) collective-permute-start(bf16[2,4,24,384]{3,2,1,0:T(8,128)(2,1)S(1)} %get-tuple-element.27), channel_id=1, source_target_pairs={{112,128},{113,129},{114,130},{115,131},{116,132},{117,133},{118,1... | collective-permute-start | bytes 442376 | tf_op jit(solution)/shard_map/ppermute | solution.py:471
  35.1 6.4 %collective-permute-start.9 = (bf16[2,4,24,384]{3,2,1,0:T(8,128)(2,1)S(1)}, bf16[2,4,24,384]{3,2,1,0:T(8,128)(2,1)S(1)}, u32[]{:S(2)}, u32[]{:S(2)}) collective-permute-start(bf16[2,4,24,384]{3,2,1,0:T(8,128)(2,1)S(1)} %get-tuple-element.27), channel_id=1, source_target_pairs={{0,128},{1,129},{2,130},{3,131},{4,132},{5,133},{6,134},{7,135},{8... | collective-permute-start | bytes 442376 | tf_op jit(solution)/shard_map/ppermute | solution.py:471
  37.9 12.7 %collective-permute-start.11 = (bf16[400,384]{1,0:T(8,128)(2,1)S(1)}, bf16[400,384]{1,0:T(8,128)(2,1)S(1)}, u32[]{:S(2)}, u32[]{:S(2)}) collective-permute-start(bf16[400,384]{1,0:T(8,128)(2,1)S(1)} %get-tuple-element.25.lead), channel_id=1, source_target_pairs={{128,0},{129,1},{130,2},{131,3},{132,4},{133,5},{134,6},{135,7},{1... | collective-permute-start | bytes 921608 | tf_op jit(solution)/shard_map/ppermute | solution.py:496
  41.5 9.1 %copy-start.2 = (bf16[3,3,3,192,192]{4,3,2,1,0:T(8,128)(2,1)S(1)}, bf16[3,3,3,192,192]{4,3,2,1,0:T(8,128)(2,1)}, u32[]{:S(2)}) copy-start(bf16[3,3,3,192,192]{4,3,2,1,0:T(8,128)(2,1)} %param.20) | copy-start | bytes 5971972
  41.5 9.1 %copy-start.4 = (bf16[2,8,40,192]{3,2,1,0:T(8,128)(2,1)S(1)}, bf16[2,8,40,192]{3,2,1,0:T(8,128)(2,1)}, u32[]{:S(2)}) copy-start(bf16[2,8,40,192]{3,2,1,0:T(8,128)(2,1)} %cache.1) | copy-start | bytes 737284
  41.5 9.1 %copy-start.7 = (f32[192]{0:T(256)S(1)}, f32[192]{0:T(256)}, u32[]{:S(2)}) copy-start(f32[192]{0:T(256)} %param.17) | copy-start | bytes 2308
  41.5 9.1 %copy-start.8 = (f32[192]{0:T(256)S(1)}, f32[192]{0:T(256)}, u32[]{:S(2)}) copy-start(f32[192]{0:T(256)} %param.18) | copy-start | bytes 2308
  41.5 9.2 %copy-start.9 = (f32[192]{0:T(256)S(1)}, f32[192]{0:T(256)}, u32[]{:S(2)}) copy-start(f32[192]{0:T(256)} %param.21) | copy-start | bytes 2308

commit v5 on v4

--- a/solution.py
+++ b/solution.py
@@ -24,8 +24,7 @@
 
 def normed(values, gain_vec, channels):
     inv_rms = lax.rsqrt(jnp.sum(values * values, axis=-1, keepdims=True) * (1.0 / channels) + 1e-06)
-    scaled = values * inv_rms * gain_vec
-    half = 0.5 * scaled
+    half = values * inv_rms * (0.5 * gain_vec)
     return half + half * jnp.tanh(half)
 
 
@@ -248,10 +247,11 @@
         for lo, hi in ((0, 96), (96, 200)):
             part = raw[f, lo:hi]
             act[f, lo:hi] = part if lead else normed(part, g[...], CM)
-        for p in range(3):
-            for q in range(3):
-                at = p * PITCH + q
-                stores[f][:, (p * 3 + q) * CM : (p * 3 + q + 1) * CM] = act[f, at : at + 144].astype(BF16)
+        for q in range(3):
+            shifted = act[f, q : q + 192]
+            for p in range(3):
+                at = p * PITCH
+                stores[f][:, (p * 3 + q) * CM : (p * 3 + q + 1) * CM] = shifted[at : at + 144].astype(BF16)
     total = conv_frames(stores, w) + b[...]
     cell = lax.broadcasted_iota(jnp.int32, (PITCH, 1), 0)
     cols = cell + (info[2] * COLS - 1)

time: 57.6 us -> 57.2 us (level)
  no operation moved by 1% of the time
where the time goes in v5:
time: 57.2 us; the launch traced here: 56.8 us
  waiting for transfers between devices  19.2 us (34%)
  Pallas kernels  17.3 us (30%)
  starting transfers between devices  16.9 us (30%)
  local copies, waits for them, and re-layouts  2.92 us (5%)
    pallas_call x8, Pallas kernels, call(): pl.pallas_call(body, out_shape=[jax.ShapeDtypeStruct(shape, BF16) for sha...  17.3 us
    ppermute x1, waiting for transfers between devices, shards(): returned = lax.ppermute(second_a, 'segment', [(1, 0)])  8.14 us
    ppermute x2, starting transfers between devices, shards(): lax.ppermute(sides[k], AXES, pairs_between(0, 0, 0, 2 * k - 1))  6.79 us
    ppermute x2, waiting for transfers between devices, shards(): lax.ppermute(sides[k], AXES, pairs_between(0, 0, 0, 2 * k - 1))  5.4 us
    ppermute x4, starting transfers between devices, shards(): lax.ppermute(tile, AXES, pairs_between(0, 1, dh, 0, True))  5.19 us
    ppermute x1, waiting for transfers between devices, shards(): lax.ppermute(to_above, 'ha', [(i, (i - 1) % N_HA) for i in range(N_HA)])  3.37 us
    unnamed x22, local copies, waits for them, and re-layouts  2.92 us
    ppermute x4, waiting for transfers between devices, shards(): lax.ppermute(tile, AXES, pairs_between(0, 1, dh, 0, True))  2.26 us
  transfers between devices with their start and end apart: 12, of which 4 were waited for; matrix products, arithmetic and copies ran while one was open for 0% of the time, Pallas kernels for 17%

profile of v5, /device:TPU:125, one launch (start us, length us, event | category | flops | bytes accessed | tf_op | source)
XLA Modules:
  0.0 56.8 jit_solution(13447993760950909121)
XLA Ops:
  0.0 0.9 %copy.18 = bf16[1,2,4,20,384]{4,3,2,1,0:T(8,128)(2,1)S(1)} copy(bf16[1,2,4,20,384]{4,2,3,1,0:T(4,128)(2,1)} %param.15) | data formatting | bytes 245760 | tf_op args[4]
  0.9 1.0 %copy.13.latent = bf16[4,4,20,384]{3,2,1,0:T(8,128)(2,1)S(1)} copy(bf16[4,4,20,384]{3,1,2,0:T(4,128)(2,1)} %param.11) | data formatting | bytes 491520 | tf_op args[0]
  1.9 0.1 pad_add_fusion.info
  2.0 0.6 %shard_map.109._ = bf16[368,384]{1,0:T(8,128)(2,1)S(1)} custom-call(s32[3]{0:T(128)S(1)} %pad_add_fusion.info, bf16[4,4,20,384]{3,2,1,0:T(8,128)(2,1)S(1)} %copy.13.latent, bf16[2,4,20,384]{3,2,1,0:T(8,128)(2,1)S(1)} %bitcast.20), custom_call_target="tpu_custom_call" | custom-call | bytes 1048576 | tf_op jit(solution)/shard_map/pallas_call | solution.py:412
  2.6 0.7 %collective-permute-start = (bf16[368,384]{1,0:T(8,128)(2,1)S(1)}, bf16[368,384]{1,0:T(8,128)(2,1)S(1)}, u32[]{:S(2)}, u32[]{:S(2)}) collective-permute-start(bf16[368,384]{1,0:T(8,128)(2,1)S(1)} %shard_map.109._), channel_id=1, source_target_pairs={{0,112},{16,0},{32,16},{48,32},{64,48},{80,64},{96,80},{112,96},{1... | collective-permute-start | bytes 847880 | tf_op jit(solution)/shard_map/ppermute | solution.py:446
  3.3 1.0 %copy-done.3 = bf16[2,8,40,192]{3,2,1,0:T(8,128)(2,1)S(1)} copy-done((bf16[2,8,40,192]{3,2,1,0:T(8,128)(2,1)S(1)}, bf16[2,8,40,192]{3,2,1,0:T(8,128)(2,1)}, u32[]{:S(2)}) %copy-start.3) | copy-done | bytes 245784
  4.3 0.5 shard_map.110
  4.8 0.8 %collective-permute-start.1 = (bf16[128,384]{1,0:T(8,128)(2,1)S(1)}, bf16[128,384]{1,0:T(8,128)(2,1)S(1)}, u32[]{:S(2)}, u32[]{:S(2)}) collective-permute-start(bf16[128,384]{1,0:T(8,128)(2,1)S(1)} %get-tuple-element.18), channel_id=1, source_target_pairs={{128,144},{129,145},{130,146},{131,147},{132,148},{133,149},{134,1... | collective-permute-start | bytes 294920 | tf_op jit(solution)/shard_map/ppermute | solution.py:451
  5.6 0.0 copy-start.5
  5.7 0.0 copy-start.6
  5.7 0.8 %collective-permute-start.2 = (bf16[48,384]{1,0:T(8,128)(2,1)S(1)}, bf16[48,384]{1,0:T(8,128)(2,1)S(1)}, u32[]{:S(2)}, u32[]{:S(2)}) collective-permute-start(bf16[48,384]{1,0:T(8,128)(2,1)S(1)} %get-tuple-element.19), channel_id=1, source_target_pairs={{144,128},{145,129},{146,130},{147,131},{148,132},{149,133},{150,1... | collective-permute-start | bytes 110600 | tf_op jit(solution)/shard_map/ppermute | solution.py:452
  6.5 0.0 collective-permute-done.2.under
  6.5 0.0 collective-permute-done.1.above
  6.5 3.4 %collective-permute-done.below = bf16[368,384]{1,0:T(8,128)(2,1)S(1)} collective-permute-done((bf16[368,384]{1,0:T(8,128)(2,1)S(1)}, bf16[368,384]{1,0:T(8,128)(2,1)S(1)}, u32[]{:S(2)}, u32[]{:S(2)}) %collective-permute-start) | collective-permute-done | bytes 282656 | tf_op jit(solution)/shard_map/ppermute | solution.py:446
  9.9 0.7 %shard_map.111 = (bf16[112,384]{1,0:T(8,128)(2,1)S(1)}, bf16[112,384]{1,0:T(8,128)(2,1)S(1)}, bf16[48,384]{1,0:T(8,128)(2,1)S(1)}, bf16[48,384]{1,0:T(8,128)(2,1)S(1)}) custom-call(s32[3]{0:T(128)S(1)} %pad_add_fusion.info, bf16[4,4,20,384]{3,2,1,0:T(8,128)(2,1)S(1)} %copy.13.latent, bf16[2,4,20,384]{3,2,1,0:T(8,128)(2,1)S(1)} %bitcast.22, ...), custom_call_target="tpu_custom_call" | custom-call | flops 2000000000 | bytes 1048576 | tf_op jit(solution)/shard_map/pallas_call | solution.py:412
  10.5 4.7 %collective-permute-start.5 = (bf16[112,384]{1,0:T(8,128)(2,1)S(1)}, bf16[112,384]{1,0:T(8,128)(2,1)S(1)}, u32[]{:S(2)}, u32[]{:S(2)}) collective-permute-start(bf16[112,384]{1,0:T(8,128)(2,1)S(1)} %get-tuple-element.22), channel_id=1, source_target_pairs={{0,1},{1,2},{2,3},{3,4},{4,5},{5,6},{6,7},{7,8},{8,9},{9,10},{10,1... | collective-permute-start | bytes 258056 | tf_op jit(solution)/shard_map/ppermute | solution.py:457
  15.2 2.1 %collective-permute-start.6 = (bf16[112,384]{1,0:T(8,128)(2,1)S(1)}, bf16[112,384]{1,0:T(8,128)(2,1)S(1)}, u32[]{:S(2)}, u32[]{:S(2)}) collective-permute-start(bf16[112,384]{1,0:T(8,128)(2,1)S(1)} %get-tuple-element.23), channel_id=1, source_target_pairs={{1,0},{2,1},{3,2},{4,3},{5,4},{6,5},{7,6},{8,7},{9,8},{10,9},{11,1... | collective-permute-start | bytes 258056 | tf_op jit(solution)/shard_map/ppermute | solution.py:457
  17.3 0.7 %collective-permute-start.3 = (bf16[48,384]{1,0:T(8,128)(2,1)S(1)}, bf16[48,384]{1,0:T(8,128)(2,1)S(1)}, u32[]{:S(2)}, u32[]{:S(2)}) collective-permute-start(bf16[48,384]{1,0:T(8,128)(2,1)S(1)} %get-tuple-element.20), channel_id=1, source_target_pairs={{128,129},{129,130},{130,131},{131,132},{132,133},{133,134},{134,1... | collective-permute-start | bytes 110600 | tf_op jit(solution)/shard_map/ppermute | solution.py:458
  18.0 0.7 %collective-permute-start.4 = (bf16[48,384]{1,0:T(8,128)(2,1)S(1)}, bf16[48,384]{1,0:T(8,128)(2,1)S(1)}, u32[]{:S(2)}, u32[]{:S(2)}) collective-permute-start(bf16[48,384]{1,0:T(8,128)(2,1)S(1)} %get-tuple-element.21), channel_id=1, source_target_pairs={{129,128},{130,129},{131,130},{132,131},{133,132},{134,133},{135,1... | collective-permute-start | bytes 110600 | tf_op jit(solution)/shard_map/ppermute | solution.py:458
  18.7 0.0 collective-permute-done.5.left
  18.7 5.4 %collective-permute-done.6.right = bf16[112,384]{1,0:T(8,128)(2,1)S(1)} collective-permute-done((bf16[112,384]{1,0:T(8,128)(2,1)S(1)}, bf16[112,384]{1,0:T(8,128)(2,1)S(1)}, u32[]{:S(2)}, u32[]{:S(2)}) %collective-permute-start.6) | collective-permute-done | bytes 86048 | tf_op jit(solution)/shard_map/ppermute | solution.py:457
  24.1 0.0 copy-done
  24.1 0.0 copy-done.5
  24.1 0.0 copy-done.6
  24.1 0.0 copy-start.1
  24.1 3.5 %shard_map.112 = (bf16[2,4,24,384]{3,2,1,0:T(8,128)(2,1)S(1)}, bf16[2,112,3456]{2,1,0:T(8,128)(2,1)S(1)}) custom-call(s32[3]{0:T(128)S(1)} %pad_add_fusion.info, bf16[4,4,20,384]{3,2,1,0:T(8,128)(2,1)S(1)} %copy.13.latent, bf16[2,4,20,384]{3,2,1,0:T(8,128)(2,1)S(1)} %bitcast.23, bf16[368,384]{1,0:T(8,128)(2,1)S(1)} %collective-permute-done.below, ...), custom_call_target="tpu_custom_call" | custom-call | flops 1783627776 | bytes 1048576 | tf_op jit(solution)/shard_map/pallas_call | solution.py:412
  27.6 1.3 %collective-permute-start.8 = (bf16[2,4,24,384]{3,2,1,0:T(8,128)(2,1)S(1)}, bf16[2,4,24,384]{3,2,1,0:T(8,128)(2,1)S(1)}, u32[]{:S(2)}, u32[]{:S(2)}) collective-permute-start(bf16[2,4,24,384]{3,2,1,0:T(8,128)(2,1)S(1)} %get-tuple-element.24), channel_id=1, source_target_pairs={{112,128},{113,129},{114,130},{115,131},{116,132},{117,133},{118,1... | collective-permute-start | bytes 442376 | tf_op jit(solution)/shard_map/ppermute | solution.py:471
  28.9 1.3 %collective-permute-start.7 = (bf16[2,4,24,384]{3,2,1,0:T(8,128)(2,1)S(1)}, bf16[2,4,24,384]{3,2,1,0:T(8,128)(2,1)S(1)}, u32[]{:S(2)}, u32[]{:S(2)}) collective-permute-start(bf16[2,4,24,384]{3,2,1,0:T(8,128)(2,1)S(1)} %get-tuple-element.24), channel_id=1, source_target_pairs={{0,128},{1,129},{2,130},{3,131},{4,132},{5,133},{6,134},{7,135},{8... | collective-permute-start | bytes 442376 | tf_op jit(solution)/shard_map/ppermute | solution.py:471
  30.2 0.0 copy-done.1
  30.2 3.4 %shard_map.114 = (bf16[2,4,24,384]{3,2,1,0:T(8,128)(2,1)S(1)}, bf16[1536,1024]{1,0:T(8,128)(2,1)S(1)}) custom-call(s32[3]{0:T(128)S(1)} %pad_add_fusion.info, bf16[4,4,20,384]{3,2,1,0:T(8,128)(2,1)S(1)} %copy.13.latent, bf16[368,384]{1,0:T(8,128)(2,1)S(1)} %collective-permute-done.below, bf16[112,384]{1,0:T(8,128)(2,1)S(1)} %collective-permute-done.5.left, ...), custom_call_target="tpu_custom_call" | custom-call | flops 1783627776 | bytes 1048576 | tf_op jit(solution)/shard_map/pallas_call | solution.py:412
  33.7 1.3 %collective-permute-start.10 = (bf16[2,4,24,384]{3,2,1,0:T(8,128)(2,1)S(1)}, bf16[2,4,24,384]{3,2,1,0:T(8,128)(2,1)S(1)}, u32[]{:S(2)}, u32[]{:S(2)}) collective-permute-start(bf16[2,4,24,384]{3,2,1,0:T(8,128)(2,1)S(1)} %get-tuple-element.27), channel_id=1, source_target_pairs={{112,128},{113,129},{114,130},{115,131},{116,132},{117,133},{118,1... | collective-permute-start | bytes 442376 | tf_op jit(solution)/shard_map/ppermute | solution.py:471
  35.0 0.0 collective-permute-done.3.left
  35.0 1.3 %collective-permute-start.9 = (bf16[2,4,24,384]{3,2,1,0:T(8,128)(2,1)S(1)}, bf16[2,4,24,384]{3,2,1,0:T(8,128)(2,1)S(1)}, u32[]{:S(2)}, u32[]{:S(2)}) collective-permute-start(bf16[2,4,24,384]{3,2,1,0:T(8,128)(2,1)S(1)} %get-tuple-element.27), channel_id=1, source_target_pairs={{0,128},{1,129},{2,130},{3,131},{4,132},{5,133},{6,134},{7,135},{8... | collective-permute-start | bytes 442376 | tf_op jit(solution)/shard_map/ppermute | solution.py:471
  36.3 0.0 collective-permute-done.4.right
  36.3 0.0 collective-permute-done.8.top
  36.3 0.0 collective-permute-done.7.low
  36.3 1.5 %shard_map.113 = (bf16[400,384]{1,0:T(8,128)(2,1)S(1)}, bf16[2,144,3456]{2,1,0:T(8,128)(2,1)S(1)}, bf16[1536,1024]{1,0:T(8,128)(2,1)S(1)}) custom-call(s32[3]{0:T(128)S(1)} %pad_add_fusion.info, bf16[2,4,20,384]{3,2,1,0:T(8,128)(2,1)S(1)} %bitcast.24, bf16[368,384]{1,0:T(8,128)(2,1)S(1)} %collective-permute-done.below, ...), custom_call_target="tpu_custom_call" | custom-call | flops 2293235712 | bytes 1048576 | tf_op jit(solution)/shard_map/pallas_call | solution.py:412
  37.8 1.3 %collective-permute-start.11 = (bf16[400,384]{1,0:T(8,128)(2,1)S(1)}, bf16[400,384]{1,0:T(8,128)(2,1)S(1)}, u32[]{:S(2)}, u32[]{:S(2)}) collective-permute-start(bf16[400,384]{1,0:T(8,128)(2,1)S(1)} %get-tuple-element.25.lead), channel_id=1, source_target_pairs={{128,0},{129,1},{130,2},{131,3},{132,4},{133,5},{134,6},{135,7},{1... | collective-permute-start | bytes 921608 | tf_op jit(solution)/shard_map/ppermute | solution.py:496
  39.1 0.0 collective-permute-done.10.top
  39.1 2.3 %collective-permute-done.9.low = bf16[2,4,24,384]{3,2,1,0:T(8,128)(2,1)S(1)} collective-permute-done((bf16[2,4,24,384]{3,2,1,0:T(8,128)(2,1)S(1)}, bf16[2,4,24,384]{3,2,1,0:T(8,128)(2,1)S(1)}, u32[]{:S(2)}, u32[]{:S(2)}) %collective-permute-start.9) | collective-permute-done | bytes 147488 | tf_op jit(solution)/shard_map/ppermute | solution.py:471
  41.4 0.7 %shard_map.115.main = bf16[288,384]{1,0:T(8,128)(2,1)S(1)} custom-call(s32[3]{0:T(128)S(1)} %pad_add_fusion.info, bf16[2,4,24,384]{3,2,1,0:T(8,128)(2,1)S(1)} %collective-permute-done.9.low, bf16[2,4,24,384]{3,2,1,0:T(8,128)(2,1)S(1)} %collective-permute-done.10.top, bf16[2,144,3456]{2,1,0:T(8,128)(2,1)S(1)} %get-tuple-element.28.kept, ...), custom_call_target="tpu_custom_call" | custom-call | flops 2293235712 | bytes 1048576 | tf_op jit(solution)/shard_map/pallas_call | solution.py:412
  42.1 8.1 %collective-permute-done.11.returned = bf16[400,384]{1,0:T(8,128)(2,1)S(1)} collective-permute-done((bf16[400,384]{1,0:T(8,128)(2,1)S(1)}, bf16[400,384]{1,0:T(8,128)(2,1)S(1)}, u32[]{:S(2)}, u32[]{:S(2)}) %collective-permute-start.11) | collective-permute-done | bytes 307232 | tf_op jit(solution)/shard_map/ppermute | solution.py:496
  50.3 0.0 copy-done.2
  50.3 0.0 copy-done.4
  50.3 0.0 copy-done.7
  50.3 0.0 copy-done.8
  50.3 0.0 copy-done.9
  50.3 6.3 %shard_map.116 = bf16[2,8,40,192]{3,2,1,0:T(8,128)(2,1)} custom-call(s32[3]{0:T(128)S(1)} %pad_add_fusion.info, bf16[400,384]{1,0:T(8,128)(2,1)S(1)} %get-tuple-element.25.lead, bf16[288,384]{1,0:T(8,128)(2,1)S(1)} %shard_map.115.main, bf16[400,384]{1,0:T(8,128)(2,1)S(1)} %collective-permute-done.11.returned, bf16[2,8,40,192]{3,2,1,0:T(8,128)(2,1)S(1)} %copy-done.4, ...), custom_call_target="tpu_custom_call" | custom-call | flops 1528823808 | bytes 1048576 | tf_op jit(solution)/shard_map/pallas_call | solution.py:412
  (7 shorter events, 0.0 us)
Async XLA Ops:
  2.6 7.2 %collective-permute-start = (bf16[368,384]{1,0:T(8,128)(2,1)S(1)}, bf16[368,384]{1,0:T(8,128)(2,1)S(1)}, u32[]{:S(2)}, u32[]{:S(2)}) collective-permute-start(bf16[368,384]{1,0:T(8,128)(2,1)S(1)} %shard_map.109._), channel_id=1, source_target_pairs={{0,112},{16,0},{32,16},{48,32},{64,48},{80,64},{96,80},{112,96},{1... | collective-permute-start | bytes 847880 | tf_op jit(solution)/shard_map/ppermute | solution.py:446
  3.3 1.0 %copy-start.3 = (bf16[2,8,40,192]{3,2,1,0:T(8,128)(2,1)S(1)}, bf16[2,8,40,192]{3,2,1,0:T(8,128)(2,1)}, u32[]{:S(2)}) copy-start(bf16[2,8,40,192]{3,2,1,0:T(8,128)(2,1)} %cache.1) | copy-start | bytes 737284
  4.3 19.8 %copy-start = (bf16[1,3,3,3,384,384]{5,4,3,2,1,0:T(8,128)(2,1)S(1)}, bf16[1,3,3,3,384,384]{5,4,3,2,1,0:T(8,128)(2,1)}, u32[]{:S(2)}) copy-start(bf16[1,3,3,3,384,384]{5,4,3,2,1,0:T(8,128)(2,1)} %param.12) | copy-start | bytes 23887876
  4.8 1.6 %collective-permute-start.1 = (bf16[128,384]{1,0:T(8,128)(2,1)S(1)}, bf16[128,384]{1,0:T(8,128)(2,1)S(1)}, u32[]{:S(2)}, u32[]{:S(2)}) collective-permute-start(bf16[128,384]{1,0:T(8,128)(2,1)S(1)} %get-tuple-element.18), channel_id=1, source_target_pairs={{128,144},{129,145},{130,146},{131,147},{132,148},{133,149},{134,1... | collective-permute-start | bytes 294920 | tf_op jit(solution)/shard_map/ppermute | solution.py:451
  5.6 18.4 %copy-start.5 = (f32[1,384]{1,0:T(1,128)S(1)}, f32[1,384]{1,0:T(1,128)}, u32[]{:S(2)}) copy-start(f32[1,384]{1,0:T(1,128)} %b.7) | copy-start | bytes 4612
  5.7 18.4 %copy-start.6 = (f32[1,384]{1,0:T(1,128)S(1)}, f32[1,384]{1,0:T(1,128)}, u32[]{:S(2)}) copy-start(f32[1,384]{1,0:T(1,128)} %g.7) | copy-start | bytes 4612
  5.7 0.8 %collective-permute-start.2 = (bf16[48,384]{1,0:T(8,128)(2,1)S(1)}, bf16[48,384]{1,0:T(8,128)(2,1)S(1)}, u32[]{:S(2)}, u32[]{:S(2)}) collective-permute-start(bf16[48,384]{1,0:T(8,128)(2,1)S(1)} %get-tuple-element.19), channel_id=1, source_target_pairs={{144,128},{145,129},{146,130},{147,131},{148,132},{149,133},{150,1... | collective-permute-start | bytes 110600 | tf_op jit(solution)/shard_map/ppermute | solution.py:452
  10.5 8.1 %collective-permute-start.5 = (bf16[112,384]{1,0:T(8,128)(2,1)S(1)}, bf16[112,384]{1,0:T(8,128)(2,1)S(1)}, u32[]{:S(2)}, u32[]{:S(2)}) collective-permute-start(bf16[112,384]{1,0:T(8,128)(2,1)S(1)} %get-tuple-element.22), channel_id=1, source_target_pairs={{0,1},{1,2},{2,3},{3,4},{4,5},{5,6},{6,7},{7,8},{8,9},{9,10},{10,1... | collective-permute-start | bytes 258056 | tf_op jit(solution)/shard_map/ppermute | solution.py:457
  15.2 8.8 %collective-permute-start.6 = (bf16[112,384]{1,0:T(8,128)(2,1)S(1)}, bf16[112,384]{1,0:T(8,128)(2,1)S(1)}, u32[]{:S(2)}, u32[]{:S(2)}) collective-permute-start(bf16[112,384]{1,0:T(8,128)(2,1)S(1)} %get-tuple-element.23), channel_id=1, source_target_pairs={{1,0},{2,1},{3,2},{4,3},{5,4},{6,5},{7,6},{8,7},{9,8},{10,9},{11,1... | collective-permute-start | bytes 258056 | tf_op jit(solution)/shard_map/ppermute | solution.py:457
  17.3 17.6 %collective-permute-start.3 = (bf16[48,384]{1,0:T(8,128)(2,1)S(1)}, bf16[48,384]{1,0:T(8,128)(2,1)S(1)}, u32[]{:S(2)}, u32[]{:S(2)}) collective-permute-start(bf16[48,384]{1,0:T(8,128)(2,1)S(1)} %get-tuple-element.20), channel_id=1, source_target_pairs={{128,129},{129,130},{130,131},{131,132},{132,133},{133,134},{134,1... | collective-permute-start | bytes 110600 | tf_op jit(solution)/shard_map/ppermute | solution.py:458
  18.0 18.3 %collective-permute-start.4 = (bf16[48,384]{1,0:T(8,128)(2,1)S(1)}, bf16[48,384]{1,0:T(8,128)(2,1)S(1)}, u32[]{:S(2)}, u32[]{:S(2)}) collective-permute-start(bf16[48,384]{1,0:T(8,128)(2,1)S(1)} %get-tuple-element.21), channel_id=1, source_target_pairs={{129,128},{130,129},{131,130},{132,131},{133,132},{134,133},{135,1... | collective-permute-start | bytes 110600 | tf_op jit(solution)/shard_map/ppermute | solution.py:458
  24.1 6.1 %copy-start.1 = (bf16[3,3,384,192]{2,3,1,0:T(8,128)(2,1)S(1)}, bf16[3,3,384,192]{2,3,1,0:T(8,128)(2,1)}, u32[]{:S(2)}) copy-start(bf16[3,3,384,192]{2,3,1,0:T(8,128)(2,1)} %param.16) | copy-start | bytes 3981316
  27.6 8.7 %collective-permute-start.8 = (bf16[2,4,24,384]{3,2,1,0:T(8,128)(2,1)S(1)}, bf16[2,4,24,384]{3,2,1,0:T(8,128)(2,1)S(1)}, u32[]{:S(2)}, u32[]{:S(2)}) collective-permute-start(bf16[2,4,24,384]{3,2,1,0:T(8,128)(2,1)S(1)} %get-tuple-element.24), channel_id=1, source_target_pairs={{112,128},{113,129},{114,130},{115,131},{116,132},{117,133},{118,1... | collective-permute-start | bytes 442376 | tf_op jit(solution)/shard_map/ppermute | solution.py:471
  28.9 7.4 %collective-permute-start.7 = (bf16[2,4,24,384]{3,2,1,0:T(8,128)(2,1)S(1)}, bf16[2,4,24,384]{3,2,1,0:T(8,128)(2,1)S(1)}, u32[]{:S(2)}, u32[]{:S(2)}) collective-permute-start(bf16[2,4,24,384]{3,2,1,0:T(8,128)(2,1)S(1)} %get-tuple-element.24), channel_id=1, source_target_pairs={{0,128},{1,129},{2,130},{3,131},{4,132},{5,133},{6,134},{7,135},{8... | collective-permute-start | bytes 442376 | tf_op jit(solution)/shard_map/ppermute | solution.py:471
  33.7 5.5 %collective-permute-start.10 = (bf16[2,4,24,384]{3,2,1,0:T(8,128)(2,1)S(1)}, bf16[2,4,24,384]{3,2,1,0:T(8,128)(2,1)S(1)}, u32[]{:S(2)}, u32[]{:S(2)}) collective-permute-start(bf16[2,4,24,384]{3,2,1,0:T(8,128)(2,1)S(1)} %get-tuple-element.27), channel_id=1, source_target_pairs={{112,128},{113,129},{114,130},{115,131},{116,132},{117,133},{118,1... | collective-permute-start | bytes 442376 | tf_op jit(solution)/shard_map/ppermute | solution.py:471
  35.0 6.4 %collective-permute-start.9 = (bf16[2,4,24,384]{3,2,1,0:T(8,128)(2,1)S(1)}, bf16[2,4,24,384]{3,2,1,0:T(8,128)(2,1)S(1)}, u32[]{:S(2)}, u32[]{:S(2)}) collective-permute-start(bf16[2,4,24,384]{3,2,1,0:T(8,128)(2,1)S(1)} %get-tuple-element.27), channel_id=1, source_target_pairs={{0,128},{1,129},{2,130},{3,131},{4,132},{5,133},{6,134},{7,135},{8... | collective-permute-start | bytes 442376 | tf_op jit(solution)/shard_map/ppermute | solution.py:471
  37.8 12.5 %collective-permute-start.11 = (bf16[400,384]{1,0:T(8,128)(2,1)S(1)}, bf16[400,384]{1,0:T(8,128)(2,1)S(1)}, u32[]{:S(2)}, u32[]{:S(2)}) collective-permute-start(bf16[400,384]{1,0:T(8,128)(2,1)S(1)} %get-tuple-element.25.lead), channel_id=1, source_target_pairs={{128,0},{129,1},{130,2},{131,3},{132,4},{133,5},{134,6},{135,7},{1... | collective-permute-start | bytes 921608 | tf_op jit(solution)/shard_map/ppermute | solution.py:496
  41.4 8.9 %copy-start.2 = (bf16[3,3,3,192,192]{4,3,2,1,0:T(8,128)(2,1)S(1)}, bf16[3,3,3,192,192]{4,3,2,1,0:T(8,128)(2,1)}, u32[]{:S(2)}) copy-start(bf16[3,3,3,192,192]{4,3,2,1,0:T(8,128)(2,1)} %param.20) | copy-start | bytes 5971972
  41.4 8.9 %copy-start.4 = (bf16[2,8,40,192]{3,2,1,0:T(8,128)(2,1)S(1)}, bf16[2,8,40,192]{3,2,1,0:T(8,128)(2,1)}, u32[]{:S(2)}) copy-start(bf16[2,8,40,192]{3,2,1,0:T(8,128)(2,1)} %cache.1) | copy-start | bytes 737284
  41.4 8.9 %copy-start.7 = (f32[192]{0:T(256)S(1)}, f32[192]{0:T(256)}, u32[]{:S(2)}) copy-start(f32[192]{0:T(256)} %param.17) | copy-start | bytes 2308
  41.4 8.9 %copy-start.8 = (f32[192]{0:T(256)S(1)}, f32[192]{0:T(256)}, u32[]{:S(2)}) copy-start(f32[192]{0:T(256)} %param.18) | copy-start | bytes 2308
  41.4 8.9 %copy-start.9 = (f32[192]{0:T(256)S(1)}, f32[192]{0:T(256)}, u32[]{:S(2)}) copy-start(f32[192]{0:T(256)} %param.21) | copy-start | bytes 2308
